TPU v7x, 32 devices: a whole 2x2x4 slice. The times are simulated.
32 devices in a mesh: dp: 4 (over y, x), expert: 8 (over z, core).
Axes of the slice: x: 2, y: 2, z: 4, core: 2. Of those that a mesh axis runs over, the one named last changes fastest.
Arguments:
- tokens: bfloat16 [20480, 1536], P(('dp', 'expert')), may hold values from -6 to 6
- cotangent: bfloat16 [20480, 1536], P(('dp', 'expert')), may hold values from -6 to 6
- norm_attn: float32 [1536], replicated, may hold values from 0.5 to 1.5
- norm_moe: float32 [1536], replicated, may hold values from 0.5 to 1.5
- w_query: bfloat16 [1536, 1536], P('dp'), may hold values from -0.15625 to 0.15625
- key_weight: bfloat16 [1536, 256], P('dp'), may hold values from -0.15625 to 0.15625
- value_weight: bfloat16 [1536, 256], P('dp'), may hold values from -0.15625 to 0.15625
- w_out: bfloat16 [1536, 1536], P('dp'), may hold values from -0.4375 to 0.4375
- w_router: bfloat16 [1536, 8], replicated, may hold values from -0.078125 to 0.078125
- w_gate: bfloat16 [8, 1536, 768], P('expert'), may hold values from -0.15625 to 0.15625
- w_up: bfloat16 [8, 1536, 768], P('expert'), may hold values from -0.15625 to 0.15625
- w_down: bfloat16 [8, 768, 1536], P('expert'), may hold values from -1.25 to 1.25
- document_index: int32 [32, 640], P(('dp', 'expert')), may hold values from 0 to 7, never falling along the last dimension, each value on 1 to 320 neighbouring positions
- padding_token_mask: int32 [32, 640], P(('dp', 'expert')), may hold values 0 or 1
- routes: int32 [20480, 4], P(('dp', 'expert')), may hold values from 0 to 7, all different within a row
- pair_order: int32 [32, 2560], P(('dp', 'expert')), may hold values from 0 to 2559, each once within a row
Outputs:
- block_out: bfloat16 [20480, 1536], P(('dp', 'expert'))
- grad_tokens: float32 [20480, 1536], P(('dp', 'expert'))
- grad_norm_attn: float32 [1536], replicated
- grad_norm_moe: float32 [1536], replicated
- grad_query: float32 [1536, 1536], P('dp')
- grad_key: float32 [1536, 256], P('dp')
- grad_value: float32 [1536, 256], P('dp')
- grad_out: float32 [1536, 1536], P('dp')
- grad_router: float32 [1536, 8], replicated
- grad_gate: float32 [8, 1536, 768], P('expert')
- grad_up: float32 [8, 1536, 768], P('expert')
- grad_down: float32 [8, 768, 1536], P('expert')
Inputs may be any that keep to these rules, and one draw needn't show every extreme that they name: `routes`: each row names 4 different experts. `document_index`: within a sequence the ids never fall and start at 0; a document has at most 320 tokens. `pair_order`: each row holds every pair index of its sequence once.
All inputs are finite; a program needn't handle non-finite values. No bound on the sum of `padding_token_mask` on one device may be relied on, other than what follows from the above.
Results may differ from a plain program's by a relative error of at most 0.023.
Values may be sent and summed in bfloat16 or wider, within the bound.
No kernel may reach another device: no remote copies, remote signals or barrier semaphores. Data moves between devices by JAX's collectives and lax.ppermute only.
A program may use at most 320 MiB of HBM per device.

v0:
```python
import jax
import jax.numpy as jnp
from jax import lax
from jax.sharding import PartitionSpec as P

QUERY_HEADS = 12
KEY_VALUE_HEADS = 2
HEAD_SIZE = 128


epsilon = 1e-06
neg_fill = -1e30
highest = lax.Precision.HIGHEST


def slot_table(route_rows, order_row, experts, capacity):
    pair_count = order_row.shape[0]
    flat_routes = route_rows.reshape(-1)
    expert_at = jnp.take(flat_routes, order_row)
    columns = jnp.arange(experts, dtype=jnp.int32)
    onehot = (expert_at[:, None] == columns[None, :]).astype(jnp.int32)
    running = jnp.cumsum(onehot, axis=0, dtype=jnp.int32)
    ranking = jnp.take_along_axis(running, expert_at[:, None], axis=1)[:, 0] - 1
    is_kept = ranking < capacity
    target = jnp.where(is_kept, expert_at * capacity + ranking, experts * capacity)
    slot_pair = (
        jnp.full((experts * capacity,), pair_count, jnp.int32)
        .at[target]
        .set(order_row, mode="drop")
    )
    pair_slot = jnp.zeros((pair_count,), jnp.int32).at[order_row].set(target)
    return (slot_pair, pair_slot)


def visible(segment_row, pad_row):
    position = jnp.arange(segment_row.shape[0], dtype=jnp.int32)
    same_doc = segment_row[:, None] == segment_row[None, :]
    causal = position[None, :] <= position[:, None]
    present = (pad_row[None, :] == 1) | (position[None, :] == position[:, None])
    return same_doc & causal & present


def score_block(heads_of_query, heads_of_key, segment_row, pad_row):
    scores = jnp.einsum(
        "qkgd,skd->kgqs", heads_of_query, heads_of_key, preferred_element_type=jnp.float32
    ) * HEAD_SIZE ** (-0.5)
    return jnp.where(visible(segment_row, pad_row)[None, None], scores, neg_fill)


def expert_hidden(rows_in, w_gate, w_up):
    gate_pre = jnp.einsum("erd,edf->erf", rows_in, w_gate, preferred_element_type=jnp.float32)
    up_pre = jnp.einsum("erd,edf->erf", rows_in, w_up, preferred_element_type=jnp.float32)
    hidden = (gate_pre * jax.nn.sigmoid(gate_pre) * up_pre).astype(jnp.bfloat16)
    return (gate_pre, up_pre, hidden)


def norm_back(grad_normed, source, inverse, gain):
    scaled = grad_normed * gain
    grad_source = inverse * scaled - source * inverse**3 * jnp.mean(
        scaled * source, axis=1, keepdims=True
    )
    grad_gain = jnp.sum(grad_normed * source * inverse, axis=0)
    return (grad_source, grad_gain)


def body(
    tokens,
    cotangent,
    norm_attn,
    norm_moe,
    w_query,
    key_weight,
    value_weight,
    w_out,
    w_router,
    w_gate,
    w_up,
    w_down,
    document_index,
    padding_token_mask,
    routes,
    pair_order,
):
    token_rows, features = tokens.shape
    top_count = routes.shape[1]
    experts = w_gate.shape[0] * lax.axis_size("expert")
    capacity = 9 * token_rows * top_count // (8 * experts)
    group_of_heads = QUERY_HEADS // KEY_VALUE_HEADS
    score_scale = HEAD_SIZE ** (-0.5)
    segment_row = document_index[0]
    pad_row = padding_token_mask[0]
    source = tokens.astype(jnp.float32)
    inverse_one = lax.rsqrt(jnp.mean(source * source, axis=1, keepdims=True) + epsilon)
    normed_one = (source * inverse_one * norm_attn).astype(jnp.bfloat16)
    query_all, key_all, value_all, out_all = (
        lax.all_gather(w_query, "dp", axis=0, tiled=True),
        lax.all_gather(key_weight, "dp", axis=0, tiled=True),
        lax.all_gather(value_weight, "dp", axis=0, tiled=True),
        lax.all_gather(w_out, "dp", axis=0, tiled=True),
    )
    query_matrix = jnp.dot(normed_one, query_all, preferred_element_type=jnp.float32).astype(
        jnp.bfloat16
    )
    rows_of_key = jnp.dot(normed_one, key_all, preferred_element_type=jnp.float32).astype(
        jnp.bfloat16
    )
    rows_of_value = jnp.dot(normed_one, value_all, preferred_element_type=jnp.float32).astype(
        jnp.bfloat16
    )
    heads_of_query = query_matrix.reshape(token_rows, KEY_VALUE_HEADS, group_of_heads, HEAD_SIZE)
    heads_of_key = rows_of_key.reshape(token_rows, KEY_VALUE_HEADS, HEAD_SIZE)
    heads_of_value = rows_of_value.reshape(token_rows, KEY_VALUE_HEADS, HEAD_SIZE)
    scores = score_block(heads_of_query, heads_of_key, segment_row, pad_row)
    top_score = jnp.max(scores, axis=-1, keepdims=True)
    log_total = top_score + jnp.log(jnp.sum(jnp.exp(scores - top_score), axis=-1, keepdims=True))
    weights = jnp.exp(scores - log_total).astype(jnp.bfloat16)
    attention_mixture = jnp.einsum(
        "kgqs,skd->qkgd", weights, heads_of_value, preferred_element_type=jnp.float32
    )
    attention_mixture = attention_mixture.reshape(token_rows, QUERY_HEADS * HEAD_SIZE).astype(
        jnp.bfloat16
    )
    hidden_one = source + jnp.dot(attention_mixture, out_all, preferred_element_type=jnp.float32)
    inverse_two = lax.rsqrt(jnp.mean(hidden_one * hidden_one, axis=1, keepdims=True) + epsilon)
    normed_two = (hidden_one * inverse_two * norm_moe).astype(jnp.bfloat16)
    router = jax.nn.softmax(
        jnp.dot(normed_two, w_router, preferred_element_type=jnp.float32), axis=-1
    )
    columns = jnp.arange(experts, dtype=jnp.int32)
    onehot = (routes[:, :, None] == columns[None, None, :]).astype(jnp.float32)
    chosen = jnp.sum(router[:, None, :] * onehot, axis=2)
    slot_pair, pair_slot = slot_table(routes, pair_order[0], experts, capacity)
    slot_token = slot_pair // top_count
    zero_row = jnp.zeros((1, features), jnp.bfloat16)
    dispatched = jnp.concatenate([normed_two, zero_row])[slot_token].reshape(
        experts, capacity, features
    )
    received = lax.all_to_all(dispatched, "expert", split_axis=0, concat_axis=1, tiled=True)
    gate_pre, up_pre, hidden = expert_hidden(received, w_gate, w_up)
    produced = jnp.einsum(
        "erf,efd->erd", hidden, w_down, preferred_element_type=jnp.float32
    ).astype(jnp.bfloat16)
    returned = lax.all_to_all(produced, "expert", split_axis=1, concat_axis=0, tiled=True)
    returned_rows = jnp.concatenate([returned.reshape(experts * capacity, features), zero_row])
    per_pair = returned_rows[pair_slot].reshape(token_rows, top_count, features).astype(jnp.float32)
    routed = jnp.sum(chosen[:, :, None] * per_pair, axis=1)
    block_out = (hidden_one + routed).astype(jnp.bfloat16)
    cot_full = cotangent.astype(jnp.float32)
    grad_chosen = jnp.sum(per_pair * cot_full[:, None, :], axis=2)
    chosen_rows = jnp.concatenate([chosen.reshape(-1), jnp.zeros((1,), jnp.float32)])
    cot_rows = jnp.concatenate([cot_full, jnp.zeros((1, features), jnp.float32)])
    grad_produced = (
        (chosen_rows[slot_pair][:, None] * cot_rows[slot_token])
        .reshape(experts, capacity, features)
        .astype(jnp.bfloat16)
    )
    grad_arrived, rows_in = (
        lax.all_to_all(grad_produced, "expert", split_axis=0, concat_axis=1, tiled=True),
        lax.all_to_all(dispatched, "expert", split_axis=0, concat_axis=1, tiled=True),
    )
    gate_kept, up_kept, hidden_kept = expert_hidden(rows_in, w_gate, w_up)
    grad_hidden = jnp.einsum(
        "erd,efd->erf", grad_arrived, w_down, preferred_element_type=jnp.float32
    )
    sigmoid_gate = jax.nn.sigmoid(gate_kept)
    slope = sigmoid_gate * (1.0 + gate_kept * (1.0 - sigmoid_gate))
    grad_gate_pre = (grad_hidden * up_kept * slope).astype(jnp.bfloat16)
    grad_up_pre = (grad_hidden * gate_kept * sigmoid_gate).astype(jnp.bfloat16)
    grad_rows = jnp.einsum(
        "erf,edf->erd", grad_gate_pre, w_gate, preferred_element_type=jnp.float32
    )
    grad_rows = (
        grad_rows
        + jnp.einsum("erf,edf->erd", grad_up_pre, w_up, preferred_element_type=jnp.float32)
    ).astype(jnp.bfloat16)
    sent_back = lax.all_to_all(grad_rows, "expert", split_axis=1, concat_axis=0, tiled=True)
    local_gate = jnp.einsum(
        "erd,erf->edf", rows_in, grad_gate_pre, preferred_element_type=jnp.float32
    )
    local_up = jnp.einsum("erd,erf->edf", rows_in, grad_up_pre, preferred_element_type=jnp.float32)
    local_down = jnp.einsum(
        "erf,erd->efd", hidden_kept, grad_arrived, preferred_element_type=jnp.float32
    )
    grad_gate, grad_up, grad_down = (
        lax.psum(local_gate.astype(jnp.bfloat16), "dp").astype(jnp.float32),
        lax.psum(local_up.astype(jnp.bfloat16), "dp").astype(jnp.float32),
        lax.psum(local_down.astype(jnp.bfloat16), "dp").astype(jnp.float32),
    )
    grad_select = jnp.sum(onehot * grad_chosen[:, :, None], axis=1)
    grad_logits = router * (grad_select - jnp.sum(router * grad_select, axis=1, keepdims=True))
    back_rows = jnp.concatenate([sent_back.reshape(experts * capacity, features), zero_row])
    from_experts = jnp.sum(
        back_rows[pair_slot].reshape(token_rows, top_count, features).astype(jnp.float32), axis=1
    )
    grad_normed_two = (
        jnp.dot(grad_logits, w_router.astype(jnp.float32).T, precision=highest) + from_experts
    )
    local_router = jnp.dot(normed_two.astype(jnp.float32).T, grad_logits, precision=highest)
    through_two, local_norm_moe = norm_back(grad_normed_two, hidden_one, inverse_two, norm_moe)
    grad_hidden_one = cot_full + through_two
    grad_branch = grad_hidden_one.astype(jnp.bfloat16)
    local_out = jnp.dot(attention_mixture.T, grad_branch, preferred_element_type=jnp.float32)
    mixture_gradient = jnp.dot(grad_branch, out_all.T, preferred_element_type=jnp.float32).astype(
        jnp.bfloat16
    )
    heads_gradient = mixture_gradient.reshape(
        token_rows, KEY_VALUE_HEADS, group_of_heads, HEAD_SIZE
    )
    scores = score_block(heads_of_query, heads_of_key, segment_row, pad_row)
    probs = jnp.exp(scores - log_total)
    grad_weights = jnp.einsum(
        "qkgd,skd->kgqs", heads_gradient, heads_of_value, preferred_element_type=jnp.float32
    )
    grad_scores = (
        probs * (grad_weights - jnp.sum(probs * grad_weights, axis=-1, keepdims=True))
    ).astype(jnp.bfloat16)
    grad_queries = (
        jnp.einsum("kgqs,skd->qkgd", grad_scores, heads_of_key, preferred_element_type=jnp.float32)
        * score_scale
    )
    grad_queries = grad_queries.reshape(token_rows, QUERY_HEADS * HEAD_SIZE).astype(jnp.bfloat16)
    key_rows_gradient = (
        jnp.einsum(
            "kgqs,qkgd->skd", grad_scores, heads_of_query, preferred_element_type=jnp.float32
        )
        * score_scale
    )
    key_rows_gradient = key_rows_gradient.reshape(token_rows, KEY_VALUE_HEADS * HEAD_SIZE).astype(
        jnp.bfloat16
    )
    value_rows_gradient = jnp.einsum(
        "kgqs,qkgd->skd", weights, heads_gradient, preferred_element_type=jnp.float32
    )
    value_rows_gradient = value_rows_gradient.reshape(
        token_rows, KEY_VALUE_HEADS * HEAD_SIZE
    ).astype(jnp.bfloat16)
    local_query = jnp.dot(normed_one.T, grad_queries, preferred_element_type=jnp.float32)
    local_key = jnp.dot(normed_one.T, key_rows_gradient, preferred_element_type=jnp.float32)
    local_value = jnp.dot(normed_one.T, value_rows_gradient, preferred_element_type=jnp.float32)
    grad_normed_one = jnp.dot(grad_queries, query_all.T, preferred_element_type=jnp.float32)
    grad_normed_one = grad_normed_one + jnp.dot(
        key_rows_gradient, key_all.T, preferred_element_type=jnp.float32
    )
    grad_normed_one = grad_normed_one + jnp.dot(
        value_rows_gradient, value_all.T, preferred_element_type=jnp.float32
    )
    through_one, local_norm_attn = norm_back(grad_normed_one, source, inverse_one, norm_attn)
    grad_tokens = grad_hidden_one + through_one
    summed = (
        lax.psum(local_query.astype(jnp.bfloat16), "expert").astype(jnp.float32),
        lax.psum(local_key.astype(jnp.bfloat16), "expert").astype(jnp.float32),
        lax.psum(local_value.astype(jnp.bfloat16), "expert").astype(jnp.float32),
        lax.psum(local_out.astype(jnp.bfloat16), "expert").astype(jnp.float32),
    )
    grad_query, grad_key, grad_value, grad_out = (
        lax.psum_scatter(
            summed[0].astype(jnp.bfloat16), "dp", scatter_dimension=0, tiled=True
        ).astype(jnp.float32),
        lax.psum_scatter(
            summed[1].astype(jnp.bfloat16), "dp", scatter_dimension=0, tiled=True
        ).astype(jnp.float32),
        lax.psum_scatter(
            summed[2].astype(jnp.bfloat16), "dp", scatter_dimension=0, tiled=True
        ).astype(jnp.float32),
        lax.psum_scatter(
            summed[3].astype(jnp.bfloat16), "dp", scatter_dimension=0, tiled=True
        ).astype(jnp.float32),
    )
    grad_router, grad_norm_attn, grad_norm_moe = lax.psum(
        (local_router, local_norm_attn, local_norm_moe), ("dp", "expert")
    )
    return (
        block_out,
        grad_tokens,
        grad_norm_attn,
        grad_norm_moe,
        grad_query,
        grad_key,
        grad_value,
        grad_out,
        grad_router,
        grad_gate,
        grad_up,
        grad_down,
    )


def solution(mesh):
    placed = (
        P(("dp", "expert"), None),
        P(("dp", "expert"), None),
        P(),
        P(),
        P("dp", None),
        P("dp", None),
        P("dp", None),
        P("dp", None),
        P(),
        P("expert", None, None),
        P("expert", None, None),
        P("expert", None, None),
        P(("dp", "expert"), None),
        P(("dp", "expert"), None),
        P(("dp", "expert"), None),
        P(("dp", "expert"), None),
    )
    return jax.shard_map(
        body,
        mesh=mesh,
        in_specs=placed,
        out_specs=(
            P(("dp", "expert"), None),
            P(("dp", "expert"), None),
            P(),
            P(),
            P("dp", None),
            P("dp", None),
            P("dp", None),
            P("dp", None),
            P(),
            P("expert", None, None),
            P("expert", None, None),
            P("expert", None, None),
        ),
        check_vma=False,
    )
```

profile of v0, /device:TPU:0, one launch (start us, length us, event | category | flops | bytes accessed | tf_op | source)
XLA Modules:
  0.0 1732.4 jit_solution(9522593730457458381)
XLA Ops:
  28.8 15.3 gather_fusion.6
  54.2 21.2 %all_gather.13 = bf16[1536,256]{1,0:T(8,128)(2,1)S(1)} all-gather(bf16[384,256]{1,0:T(8,128)(2,1)S(1)} %copy-done.40), channel_id=1, replica_groups=mesh['dp'=4,'expert'=8] {'dp'}, dimensions={0}, use_global_device_ids=true | all-gather | bytes 983040 | tf_op jit(solution)/shard_map/all_gather | solution.py:97
  151.5 21.0 %gather_fusion.1 = bf16[2880,1536]{1,0:T(8,128)(2,1)} fusion(bf16[641,1536]{1,0:T(8,128)(2,1)} %concatenate.15, s32[3072]{0:T(1024)S(1)} %get-tuple-element.50), kind=kCustom, calls=%fused_computation.1 | custom fusion | bytes 17706240 | tf_op jit(solution)/shard_map/gather | solution.py:135
  181.5 20.8 %gather_fusion.4 = f32[2880,1536]{1,0:T(8,128)} fusion(f32[641,1536]{1,0:T(8,128)} %concatenate.18, s32[3072]{0:T(1024)S(1)} %get-tuple-element.50), kind=kCustom, calls=%fused_computation.4 | custom fusion | bytes 35400960 | tf_op jit(solution)/shard_map/gather | solution.py:153
  206.8 15.3 gather_fusion.3
  231.7 139.5 %all-to-all-done = bf16[8,360,1536]{2,1,0:T(8,128)(2,1)} async-done(((bf16[8,360,1536]{2,1,0:T(8,128)(2,1)}), bf16[8,360,1536]{2,1,0:T(8,128)(2,1)}, u32[]{:S(2)}, u32[]{:S(2)}) %all-to-all-start) | async-done | bytes 8847392 | tf_op jit(solution)/shard_map/all_to_all | solution.py:138
  400.5 169.6 %all-to-all-done.2 = bf16[8,360,1536]{2,1,0:T(8,128)(2,1)} async-done(((bf16[8,360,1536]{2,1,0:T(8,128)(2,1)}), bf16[8,360,1536]{2,1,0:T(8,128)(2,1)}, u32[]{:S(2)}, u32[]{:S(2)}) %all-to-all-start.2) | async-done | bytes 8847392 | tf_op jit(solution)/shard_map/all_to_all | solution.py:158
  570.1 18.8 %multiply_convert_fusion.1 = (bf16[2880,768]{1,0:T(8,128)(2,1)}, bf16[2880,768]{1,0:T(8,128)(2,1)}, bf16[2880,768]{1,0:T(8,128)(2,1)}) fusion(f32[2880,768]{1,0:T(8,128)} %fusion.27, f32[2880,768]{1,0:T(8,128)} %fusion.23, bf16[2880,1536]{1,0:T(8,128)(2,1)} %bitcast.21, bf16[1,768,1536]{2,1,0:T(8,128)(2,1)S(1)} %copy-done), kind=kOutput, calls=%fused_computation.28 | convolution fusion | flops 6830161920 | bytes 42172416 | tf_op jit(solution)/shard_map/erd,efd->erf/dot_general | solution.py:162
  598.5 54.6 %copy.142 = bf16[1,2880,1536]{2,0,1:T(2,128)(2,1)} copy(bf16[1,2880,1536]{2,1,0:T(8,128)(2,1)S(1)} %fusion.6) | data formatting | bytes 17694720 | tf_op jit(solution)/shard_map/convert_element_type | solution.py:142
  653.6 187.3 %reduce.18 = bf16[2880,1536]{1,0:T(8,128)(2,1)} reduce(bf16[2880,1,1536]{2,1,0:T(2,128)(2,1)} %bitcast.183, bf16[]{:T(256)} %broadcast.571), dimensions={1}, to_apply=%bitcast.177.reduce_sub_computation | reduce | bytes 17694722
  881.7 54.3 %copy.141 = bf16[1,2880,1536]{2,0,1:T(2,128)(2,1)} copy(bf16[1,2880,1536]{2,1,0:T(8,128)(2,1)S(1)} %fusion.5) | data formatting | bytes 17694720 | tf_op jit(solution)/shard_map/convert_element_type | solution.py:175
  936.1 187.8 %reduce.17 = bf16[2880,1536]{1,0:T(8,128)(2,1)} reduce(bf16[2880,1,1536]{2,1,0:T(2,128)(2,1)} %bitcast.184, bf16[]{:T(256)} %broadcast.571), dimensions={1}, to_apply=%bitcast.176.reduce_sub_computation | reduce | bytes 17694722
  1187.4 14.2 reshape.634
  1222.7 21.0 %gather_fusion.2 = bf16[2560,1536]{1,0:T(8,128)(2,1)} fusion(bf16[2881,1536]{1,0:T(8,128)(2,1)} %concatenate.16, s32[3072]{0:T(1024)S(1)} %pad_clamp_fusion.1), kind=kCustom, calls=%fused_computation.2 | custom fusion | bytes 15738880 | tf_op jit(solution)/shard_map/gather | solution.py:145
  1243.8 15.2 reshape.532
  1259.0 17.7 %multiply_reduce_fusion = (f32[640,4]{1,0:T(8,128)S(1)}, f32[640,1536]{1,0:T(8,128)}) fusion(f32[640,4,1536]{2,1,0:T(4,128)} %reshape.532, f32[640,1536]{1,0:T(8,128)} %convert_element_type.200, f32[640,4]{1,0:T(8,128)S(1)} %copy-done.20), kind=kLoop, calls=%fused_computation.19 | loop fusion | flops 14743040 | bytes 23613440 | tf_op jit(solution)/shard_map/reduce_sum | solution.py:149
  1276.9 56.4 %all-to-all-done.3 = bf16[8,2,276480]{2,1,0:T(2,128)(2,1)} async-done(((bf16[8,2,276480]{2,1,0:T(2,128)(2,1)}), bf16[8,2,276480]{2,1,0:T(2,128)(2,1)}, u32[]{:S(2)}, u32[]{:S(2)}) %all-to-all-start.3) | async-done | bytes 8847392 | tf_op jit(solution)/shard_map/all_to_all | solution.py:176
  1367.5 21.0 %gather_fusion.5 = bf16[2560,1536]{1,0:T(8,128)(2,1)} fusion(bf16[2881,1536]{1,0:T(8,128)(2,1)} %concatenate.19, s32[3072]{0:T(1024)S(1)} %pad_clamp_fusion.1), kind=kCustom, calls=%fused_computation.5 | custom fusion | bytes 15738880 | tf_op jit(solution)/shard_map/gather | solution.py:193
  1388.6 15.1 reshape.533
  1403.7 14.3 reduce_sum.144
  1525.9 57.6 %reduce-scatter.5.cloned.1.call-done = bf16[384,1536]{1,0:T(8,128)(2,1)} async-done(((bf16[1536,1536]{1,0:T(8,128)(2,1)}), bf16[384,1536]{1,0:T(8,128)(2,1)}) %reduce-scatter.5.cloned.1.call-update) | async-done | bytes 1179664 | tf_op jit(solution)/shard_map/reduce_scatter | solution.py:256
  1583.5 60.1 %reduce-scatter.11.cloned.1.call-done = bf16[384,1536]{1,0:T(8,128)(2,1)} async-done(((bf16[1536,1536]{1,0:T(8,128)(2,1)}), bf16[384,1536]{1,0:T(8,128)(2,1)}) %reduce-scatter.11.cloned.1.call-update) | async-done | bytes 1179664 | tf_op jit(solution)/shard_map/reduce_scatter | solution.py:265
  1646.1 41.7 %all-reduce.4 = (f32[1536]{0:T(1024)}, f32[1536]{0:T(1024)}, f32[1536,8]{0,1:T(8,128)}) all-reduce(f32[1536]{0:T(1024)S(1)} %get-tuple-element.16, f32[1536]{0:T(1024)S(1)} %get-tuple-element.14, f32[1536,8]{0,1:T(8,128)S(1)} %fusion.53), channel_id=1, replica_groups=mesh['dp'=4,'expert'=8] {'dp','expert'}, use_global_device_ids=true, to_apply=%region_20.21 | all-reduce | flops 15360 | bytes 122880 | tf_op jit(solution)/shard_map/psum | solution.py:269
  1694.3 24.5 %all-reduce.10.cloned.1.call-done = (bf16[384,1536]{1,0:T(8,128)(2,1)}, bf16[384,256]{1,0:T(8,128)(2,1)}, bf16[384,256]{1,0:T(8,128)(2,1)}, bf16[384,1536]{1,0:T(8,128)(2,1)}) async-done(((bf16[384,1536]{1,0:T(8,128)(2,1)}, bf16[384,256]{1,0:T(8,128)(2,1)}, bf16[384,256]{1,0:T(8,128)(2,1)}, bf16[384,1536]{1,0:T(8,128)(2,1)}), (bf16[384,1536]{1,0:T(8,128)(2,1)}, bf16[384,256]{1,0:T(8,128)(2,1)}, ...) | async-done | bytes 2752528 | tf_op jit(solution)/shard_map/psum | solution.py:250
  (284 shorter events, 452.3 us)
Async XLA Ops:
  7.2 562.9 %copy-start = (bf16[1,768,1536]{2,1,0:T(8,128)(2,1)S(1)}, bf16[1,768,1536]{2,1,0:T(8,128)(2,1)}, u32[]{:S(2)}) copy-start(bf16[1,768,1536]{2,1,0:T(8,128)(2,1)} %param.27) | copy-start | bytes 7077892
  7.2 85.7 %all-gather.3.cloned.1.call-start = ((), (), s32[]{:S(2)}) async-start(), calls=%async_computation.8 | async-start | bytes 5898240 | tf_op jit(solution)/shard_map/all_gather | solution.py:96
  7.9 132.6 %all-gather.5.cloned.1.call-start = ((), (), s32[]{:S(2)}) async-start(), calls=%async_computation.9 | async-start | bytes 5898240 | tf_op jit(solution)/shard_map/all_gather | solution.py:99
  10.2 34.0 %copy-start.45 = (s32[2560]{0:T(1024)}, s32[2560]{0:T(1024)S(1)}, u32[]{:S(2)}) copy-start(s32[2560]{0:T(1024)S(1)} %reduce.7) | copy-start | bytes 30724
  28.7 25.4 %copy-start.66 = (s32[1,640]{1,0:T(1,128)S(1)}, s32[1,640]{1,0:T(1,128)}, u32[]{:S(2)}) copy-start(s32[1,640]{1,0:T(1,128)} %param.29) | copy-start | bytes 7684
  28.7 25.4 %copy-start.40 = (bf16[384,256]{1,0:T(8,128)(2,1)S(1)}, bf16[384,256]{1,0:T(8,128)(2,1)}, u32[]{:S(2)}) copy-start(bf16[384,256]{1,0:T(8,128)(2,1)} %param.21) | copy-start | bytes 589828
  28.7 46.6 %copy-start.41 = (bf16[384,256]{1,0:T(8,128)(2,1)S(1)}, bf16[384,256]{1,0:T(8,128)(2,1)}, u32[]{:S(2)}) copy-start(bf16[384,256]{1,0:T(8,128)(2,1)} %param.22) | copy-start | bytes 589828
  44.0 45.8 %copy-start.43 = (s32[2560]{0:T(1024)}, s32[2560]{0:T(1024)S(1)}, u32[]{:S(2)}) copy-start(s32[2560]{0:T(1024)S(1)} %gather_fusion.6) | copy-start | bytes 30724
  44.0 46.7 %copy-start.62 = (f32[1536]{0:T(1024)S(1)}, f32[1536]{0:T(1024)}, u32[]{:S(2)}) copy-start(f32[1536]{0:T(1024)} %param.18) | copy-start | bytes 18436
  54.1 36.7 %copy-start.5 = (bf16[640,1536]{1,0:T(8,128)(2,1)S(1)}, bf16[640,1536]{1,0:T(8,128)(2,1)}, u32[]{:S(2)}) copy-start(bf16[640,1536]{1,0:T(8,128)(2,1)} %param.16) | copy-start | bytes 5898244
  90.8 36.0 %copy-start.8 = (pred[640,640]{0,1:T(8,128)(4,1)}, pred[640,640]{0,1:T(8,128)(4,1)S(1)}, u32[]{:S(2)}) copy-start(pred[640,640]{0,1:T(8,128)(4,1)S(1)} %fusion.30) | copy-start | bytes 1228804
  92.9 33.9 %copy-start.30 = (bf16[640,256]{0,1:T(8,128)(2,1)}, bf16[640,256]{0,1:T(8,128)(2,1)S(1)}, u32[]{:S(2)}) copy-start(bf16[640,256]{0,1:T(8,128)(2,1)S(1)} %convolution_convert_fusion.12) | copy-start | bytes 983044
  172.5 198.7 %all-to-all-start = ((bf16[8,360,1536]{2,1,0:T(8,128)(2,1)}), bf16[8,360,1536]{2,1,0:T(8,128)(2,1)}, u32[]{:S(2)}, u32[]{:S(2)}) async-start(bf16[8,360,1536]{2,1,0:T(8,128)(2,1)} %bitcast.187), calls=%async_computation | async-start | bytes 17694720 | tf_op jit(solution)/shard_map/all_to_all | solution.py:138
  371.2 198.9 %all-to-all-start.2 = ((bf16[8,360,1536]{2,1,0:T(8,128)(2,1)}), bf16[8,360,1536]{2,1,0:T(8,128)(2,1)}, u32[]{:S(2)}, u32[]{:S(2)}) async-start(bf16[8,360,1536]{2,1,0:T(8,128)(2,1)} %multiply_convert_fusion), calls=%async_computation.2 | async-start | bytes 17694720 | tf_op jit(solution)/shard_map/all_to_all | solution.py:158
  851.4 282.9 %all-to-all-start.1 = ((bf16[8,2,276480]{2,1,0:T(2,128)(2,1)}), bf16[8,2,276480]{2,1,0:T(2,128)(2,1)}, u32[]{:S(2)}, u32[]{:S(2)}) async-start(bf16[8,2,276480]{2,1,0:T(2,128)(2,1)} %reshape.633), calls=%async_computation.1 | async-start | bytes 17694720 | tf_op jit(solution)/shard_map/all_to_all | solution.py:143
  1134.3 199.0 %all-to-all-start.3 = ((bf16[8,2,276480]{2,1,0:T(2,128)(2,1)}), bf16[8,2,276480]{2,1,0:T(2,128)(2,1)}, u32[]{:S(2)}, u32[]{:S(2)}) async-start(bf16[8,2,276480]{2,1,0:T(2,128)(2,1)} %reshape.635), calls=%async_computation.3 | async-start | bytes 17694720 | tf_op jit(solution)/shard_map/all_to_all | solution.py:176
  1139.5 367.4 %all-reduce.12.cloned.1.call-start = ((), (), s32[]{:S(2)}) async-start(), calls=%async_computation.15 | async-start | bytes 14155776 | tf_op jit(solution)/shard_map/psum | solution.py:185
  1139.6 25.4 %slice-start.6 = ((s8[4423680]{0:T(1024)(128)(4,1)}), s8[229376]{0:T(1024)(128)(4,1)S(1)}, s32[]{:S(2)}) async-start(s8[4423680]{0:T(1024)(128)(4,1)} %bitcast.211), calls=%async_computation.22 | async-start | bytes 458752
  1187.4 338.5 %reduce-scatter.7.cloned.1.call-start = ((), (), s32[]{:S(2)}) async-start(), calls=%async_computation.11 | async-start | bytes 983040 | tf_op jit(solution)/shard_map/reduce_scatter | solution.py:259
  1470.2 55.7 %reduce-scatter.9.cloned.1.call-start = ((), (), s32[]{:S(2)}) async-start(), calls=%async_computation.12 | async-start | bytes 983040 | tf_op jit(solution)/shard_map/reduce_scatter | solution.py:262
  1484.7 98.8 %reduce-scatter.5.cloned.1.call-start = ((), (), s32[]{:S(2)}) async-start(), calls=%async_computation.10 | async-start | bytes 5898240 | tf_op jit(solution)/shard_map/reduce_scatter | solution.py:256
  1497.8 145.9 %reduce-scatter.11.cloned.1.call-start = ((), (), s32[]{:S(2)}) async-start(), calls=%async_computation.13 | async-start | bytes 5898240 | tf_op jit(solution)/shard_map/reduce_scatter | solution.py:265
  1506.9 211.9 %all-reduce.10.cloned.1.call-start = ((), (), s32[]{:S(2)}) async-start(), calls=%async_computation.14 | async-start | bytes 5505024 | tf_op jit(solution)/shard_map/psum | solution.py:250
  1525.9 161.9 %copy-start.64 = (f32[640]{0:T(1024)S(1)}, f32[640]{0:T(1024)}, u32[]{:S(2)}) copy-start(f32[640]{0:T(1024)} %get-tuple-element.35) | copy-start | bytes 7684
  (65 other events, 522.4 us)
Sparse Core Ops, SparseCore 0:
  9.9 66.0 all-gather.2
  77.8 57.0 all-gather.4
  1187.5 152.9 all-reduce.11
  1470.3 24.3 reduce-scatter.6
  1497.5 26.0 reduce-scatter.8
  1526.4 57.0 reduce-scatter.4
  1586.5 57.0 reduce-scatter.10
  1646.3 72.4 all-reduce.9
where the time goes:
time: 1740 us; the launch traced here: 1730 us
  waiting for transfers between devices  509 us (29%)
  other arithmetic  479 us (28%)
  local copies, waits for them, and re-layouts  402 us (23%)
  matrix products  231 us (13%)
  blocking collectives  75 us (4%)
  starting transfers between devices  21.5 us (1%)
    unnamed x9, other arithmetic  377 us
    all_to_all x1, waiting for transfers between devices, body(): lax.all_to_all(grad_produced, 'expert', split_axis=0, concat_axis=1, tile...  170 us
    all_to_all x1, waiting for transfers between devices, body(): lax.all_to_all(dispatched, 'expert', split_axis=0, concat_axis=1, tiled=T...  139 us
    unnamed x164, local copies, waits for them, and re-layouts  85.3 us
    reduce_scatter x1, waiting for transfers between devices, body(): lax.psum_scatter(summed[3].astype(jnp.bfloat16), 'dp', scatter_dimension=...  60.1 us
    reduce_scatter x1, waiting for transfers between devices, body(): lax.psum_scatter(summed[0].astype(jnp.bfloat16), 'dp', scatter_dimension=...  57.6 us
    all_to_all x1, waiting for transfers between devices, body(): lax.all_to_all(grad_rows, 'expert', split_axis=1, concat_axis=0, tiled=True)  56.4 us
    convert_element_type x1, local copies, waits for them, and re-layouts, body(): produced = jnp.einsum('erf,efd->erd', hidden, w_down, preferred_element_t...  54.6 us
  transfers between devices with their start and end apart: 12, of which 6 were waited for; matrix products, arithmetic and copies ran while one was open for 45% of the time, Pallas kernels for 0%

commit v1 on v0

v1 whole, which is shorter than its diff:
```python
import functools
import jax
import jax.numpy as jnp
from jax import lax
from jax.experimental import pallas as pl
from jax.experimental.pallas import tpu as pltpu

bf16 = jnp.bfloat16
f32 = jnp.float32
NT_DIMS = (((1,), (1,)), ((), ()))
TN_DIMS = (((0,), (0,)), ((), ()))


def mm(a, b):
    return jnp.dot(a, b, preferred_element_type=f32)


def mm_nt(a, b):
    return lax.dot_general(a, b, NT_DIMS, preferred_element_type=f32)


def mm_tn(a, b):
    return lax.dot_general(a, b, TN_DIMS, preferred_element_type=f32)


def split_three(v):
    high = v.astype(bf16)
    rest = v - high.astype(f32)
    middle = rest.astype(bf16)
    low = (rest - middle.astype(f32)).astype(bf16)
    return high, middle, low


def expert_kernel(
    experts, chunks, tokens, features, ff, rows,
    hosted, slot_row, slot_col,
    n_same, n_other, c_same, c_other, gate0, up0, down0, gate1, up1, down1,
    po_same, po_other, pg_same, pg_other, x_out, gp_out, h_out, gg_out, gu_out,
    wg, wu, wd, nbuf, cbuf, po, pg, x, gp, gc, h, gg, gu, dmat, dtmat, gcol, vcol,
    w_sem, in_sem, act_sem, p_sem,
):
    wide = 256
    tiles = features // wide
    ff_tiles = ff // wide
    weight_copies = []
    for slot, (g_ref, u_ref, d_ref) in enumerate(((gate0, up0, down0), (gate1, up1, down1))):
        weight_copies.append((
            pltpu.make_async_copy(g_ref, wg.at[slot], w_sem.at[slot, 0]),
            pltpu.make_async_copy(u_ref, wu.at[slot], w_sem.at[slot, 1]),
            pltpu.make_async_copy(d_ref, wd.at[slot], w_sem.at[slot, 2]),
        ))

    def input_copies(chunk):
        return (
            pltpu.make_async_copy(n_same.at[chunk], nbuf.at[0], in_sem.at[0]),
            pltpu.make_async_copy(n_other.at[chunk], nbuf.at[1], in_sem.at[1]),
            pltpu.make_async_copy(c_same.at[chunk], cbuf.at[0], in_sem.at[2]),
            pltpu.make_async_copy(c_other.at[chunk], cbuf.at[1], in_sem.at[3]),
        )

    def act_copies(chunk, slot):
        at = pl.ds(pl.multiple_of(chunk * 2 * rows, 16), 2 * rows)
        return (
            pltpu.make_async_copy(x, x_out.at[slot, at], act_sem.at[0]),
            pltpu.make_async_copy(gp, gp_out.at[slot, at], act_sem.at[1]),
            pltpu.make_async_copy(h, h_out.at[slot, at], act_sem.at[2]),
            pltpu.make_async_copy(gg, gg_out.at[slot, at], act_sem.at[3]),
            pltpu.make_async_copy(gu, gu_out.at[slot, at], act_sem.at[4]),
        )

    def partial_copies(chunk):
        return (
            pltpu.make_async_copy(pg.at[0], pg_same.at[chunk], p_sem.at[0]),
            pltpu.make_async_copy(pg.at[1], pg_other.at[chunk], p_sem.at[1]),
            pltpu.make_async_copy(po.at[0], po_same.at[chunk], p_sem.at[2]),
            pltpu.make_async_copy(po.at[1], po_other.at[chunk], p_sem.at[3]),
        )

    def one_expert(chunk, slot):
        expert = hosted[slot]
        lane = lax.broadcasted_iota(jnp.int32, (rows, 128), 1)
        mine = lax.rem(lane, experts) == expert
        for q in range(2):
            at = slice(q * rows, (q + 1) * rows)
            row_slots = slot_row[chunk * 2 + slot, q:q + 1, :]
            onehot = lax.broadcasted_iota(jnp.int32, (rows, tokens), 0) == row_slots
            dmat[q] = jnp.where(onehot, 1.0, 0.0).astype(bf16)
            col_slots = slot_col[chunk * 2 + slot, :, q:q + 1]
            onehot_t = lax.broadcasted_iota(jnp.int32, (tokens, rows), 1) == col_slots
            dtmat[q] = jnp.where(onehot_t, 1.0, 0.0).astype(bf16)
            parts = mm(dmat[q], nbuf[q, :, features:features + 128])
            g = jnp.sum(jnp.where(mine & (lane < 3 * experts), parts, 0.0), axis=1, keepdims=True)
            gcol[at, :] = jnp.broadcast_to(g, (rows, 128))

            @pl.loop(0, tiles)
            def _(tile):
                cols = pl.ds(pl.multiple_of(tile * wide, wide), wide)
                x[at, cols] = mm(dmat[q], nbuf[q, :, cols]).astype(bf16)
                cot = mm(dmat[q], cbuf[q, :, cols])
                gc[at, cols] = cot.astype(bf16)
                gp[at, cols] = (cot * gcol[at, 0:1]).astype(bf16)

        @pl.loop(0, ff_tiles)
        def _(tile):
            cols = pl.ds(pl.multiple_of(tile * wide, wide), wide)
            gate = mm(x[...], wg[slot, :, cols])
            up = mm(x[...], wu[slot, :, cols])
            dh = mm_nt(gp[...], wd[slot, cols, :])
            sig = 1.0 / (1.0 + jnp.exp(-gate))
            act = gate * sig
            h[:, cols] = (act * up).astype(bf16)
            gg[:, cols] = (dh * up * (sig * (1.0 + gate * (1.0 - sig)))).astype(bf16)
            gu[:, cols] = (dh * act).astype(bf16)

        vcol[...] = jnp.zeros_like(vcol)

        @pl.loop(0, tiles)
        def _(tile):
            cols = pl.ds(pl.multiple_of(tile * wide, wide), wide)
            produced = mm(h[...], wd[slot, :, cols]).astype(bf16).astype(f32)
            along = produced * gc[:, cols].astype(f32)
            vcol[...] += along[:, :128] + along[:, 128:]
            scaled = (produced * gcol[:, 0:1]).astype(bf16)
            back = mm_nt(gg[...], wg[slot, cols, :]) + mm_nt(gu[...], wu[slot, cols, :])
            back = back.astype(bf16)
            for q in range(2):
                at = slice(q * rows, (q + 1) * rows)
                out_part = mm(dtmat[q], scaled[at])
                back_part = mm(dtmat[q], back[at])
                out_old = jnp.where(slot == 0, 0.0, po[q, :, cols].astype(f32))
                back_old = jnp.where(slot == 0, 0.0, pg[q, :, cols].astype(f32))
                po[q, :, cols] = (out_part + out_old).astype(bf16)
                pg[q, :, cols] = (back_part + back_old).astype(bf16)

        for q in range(2):
            at = slice(q * rows, (q + 1) * rows)
            high, middle, low = split_three(jnp.sum(vcol[at, :], axis=1, keepdims=True))
            payload = jnp.where(lane == expert, high.astype(f32), 0.0)
            payload = jnp.where(lane == expert + experts, middle.astype(f32), payload)
            payload = jnp.where(lane == expert + 2 * experts, low.astype(f32), payload)
            tail_part = mm(dtmat[q], payload.astype(bf16))
            tail = slice(features, features + 128)
            tail_old = jnp.where(slot == 0, 0.0, pg[q, :, tail].astype(f32))
            pg[q, :, tail] = (tail_part + tail_old).astype(bf16)

    for copies in weight_copies:
        for copy in copies:
            copy.start()
    for copy in input_copies(0):
        copy.start()

    @pl.loop(0, chunks)
    def _(chunk):
        for copy in input_copies(chunk):
            copy.wait()

        @pl.loop(0, 2)
        def _(slot):
            @pl.when((chunk == 0) & (slot == 0))
            def _():
                for copy in weight_copies[0]:
                    copy.wait()

            @pl.when((chunk == 0) & (slot == 1))
            def _():
                for copy in weight_copies[1]:
                    copy.wait()

            @pl.when(slot == 1)
            def _():
                for copy in act_copies(chunk, 0):
                    copy.wait()

            one_expert(chunk, slot)
            for copy in act_copies(chunk, slot):
                copy.start()

        for copy in partial_copies(chunk):
            copy.start()
        for copy in act_copies(chunk, 1):
            copy.wait()
        for copy in partial_copies(chunk):
            copy.wait()

        @pl.when(chunk + 1 < chunks)
        def _():
            for copy in input_copies(chunk + 1):
                copy.start()


def expert_call(hosted, slot_row, slot_col, n_same, n_other, c_same, c_other, own, partner, experts, rows):
    chunks, tokens, features = c_same.shape
    ff = own[0].shape[1]
    wide_n = n_same.shape[2]
    shape = jax.ShapeDtypeStruct
    anywhere = pl.BlockSpec(memory_space=pl.ANY)
    slots_total = chunks * 2 * rows
    act_f = shape((2, slots_total, features), bf16)
    act_h = shape((2, slots_total, ff), bf16)
    out_shape = (
        [shape((chunks, tokens, features), bf16)] * 2
        + [shape((chunks, tokens, wide_n), bf16)] * 2
        + [act_f, act_f, act_h, act_h, act_h]
    )
    many = 2 * rows
    flops = chunks * 2 * (14 * many * features * ff + 8 * many * tokens * features)
    return pl.pallas_call(
        functools.partial(expert_kernel, experts, chunks, tokens, features, ff, rows),
        out_shape=out_shape,
        in_specs=[
            pl.BlockSpec(memory_space=pltpu.SMEM),
            pl.BlockSpec(memory_space=pltpu.VMEM),
            pl.BlockSpec(memory_space=pltpu.VMEM),
        ] + [anywhere] * 10,
        out_specs=[anywhere] * 9,
        scratch_shapes=[
            pltpu.VMEM((2, features, ff), bf16),
            pltpu.VMEM((2, features, ff), bf16),
            pltpu.VMEM((2, ff, features), bf16),
            pltpu.VMEM((2, tokens, wide_n), bf16),
            pltpu.VMEM((2, tokens, features), bf16),
            pltpu.VMEM((2, tokens, features), bf16),
            pltpu.VMEM((2, tokens, wide_n), bf16),
            pltpu.VMEM((many, features), bf16),
            pltpu.VMEM((many, features), bf16),
            pltpu.VMEM((many, features), bf16),
            pltpu.VMEM((many, ff), bf16),
            pltpu.VMEM((many, ff), bf16),
            pltpu.VMEM((many, ff), bf16),
            pltpu.VMEM((2, rows, tokens), bf16),
            pltpu.VMEM((2, tokens, rows), bf16),
            pltpu.VMEM((many, 128), f32),
            pltpu.VMEM((many, 128), f32),
            pltpu.SemaphoreType.DMA((2, 3)),
            pltpu.SemaphoreType.DMA((4,)),
            pltpu.SemaphoreType.DMA((5,)),
            pltpu.SemaphoreType.DMA((4,)),
        ],
        compiler_params=pltpu.CompilerParams(vmem_limit_bytes=60 * 1024 * 1024),
        cost_estimate=pl.CostEstimate(flops=flops, bytes_accessed=40 << 20, transcendentals=chunks * 2 * many * ff),
        name="expert_rows",
    )(hosted, slot_row, slot_col, n_same, n_other, c_same, c_other, *own, *partner)


def weight_gradient_kernel(parts, *refs):
    ins, (gate_ref, up_ref, down_ref) = refs[:5 * parts], refs[5 * parts:]
    gate = up = down = None
    for p in range(parts):
        x, gg, gu, h, gp = ins[5 * p:5 * p + 5]
        g, u, d = mm_tn(x[0], gg[0]), mm_tn(x[0], gu[0]), mm_tn(h[0], gp[0])
        gate, up, down = (g, u, d) if gate is None else (gate + g, up + u, down + d)
    gate_ref[...] = gate.astype(bf16)
    up_ref[...] = up.astype(bf16)
    down_ref[...] = down.astype(bf16)


def weight_gradient_call(slot, saved):
    features, ff = saved[0][0].shape[2], saved[0][2].shape[2]
    steps = 6
    tall_f, tall_h = features // steps, ff // steps
    in_specs, args = [], []
    flops = 0
    for x, gp, h, gg, gu in saved:
        slots = x.shape[1]
        flops += 6 * slots * features * ff
        in_specs += [
            pl.BlockSpec((1, slots, tall_f), lambda i: (slot, 0, i)),
            pl.BlockSpec((1, slots, ff), lambda i: (slot, 0, 0)),
            pl.BlockSpec((1, slots, ff), lambda i: (slot, 0, 0)),
            pl.BlockSpec((1, slots, tall_h), lambda i: (slot, 0, i)),
            pl.BlockSpec((1, slots, features), lambda i: (slot, 0, 0)),
        ]
        args += [x, gg, gu, h, gp]
    return pl.pallas_call(
        functools.partial(weight_gradient_kernel, len(saved)),
        grid=(steps,),
        in_specs=in_specs,
        out_specs=[
            pl.BlockSpec((tall_f, ff), lambda i: (i, 0)),
            pl.BlockSpec((tall_f, ff), lambda i: (i, 0)),
            pl.BlockSpec((tall_h, features), lambda i: (i, 0)),
        ],
        out_shape=[
            jax.ShapeDtypeStruct((features, ff), bf16),
            jax.ShapeDtypeStruct((features, ff), bf16),
            jax.ShapeDtypeStruct((ff, features), bf16),
        ],
        compiler_params=pltpu.CompilerParams(vmem_limit_bytes=60 * 1024 * 1024),
        cost_estimate=pl.CostEstimate(flops=flops, bytes_accessed=24 << 20, transcendentals=0),
        name="expert_weight_gradients",
    )(*args)


from jax.sharding import PartitionSpec as P

QUERY_HEADS = 12
KEY_VALUE_HEADS = 2
HEAD_SIZE = 128


epsilon = 1e-06
neg_fill = -1e30
highest = lax.Precision.HIGHEST


def visible(segment_row, pad_row):
    position = jnp.arange(segment_row.shape[0], dtype=jnp.int32)
    same_doc = segment_row[:, None] == segment_row[None, :]
    causal = position[None, :] <= position[:, None]
    present = (pad_row[None, :] == 1) | (position[None, :] == position[:, None])
    return same_doc & causal & present


def score_block(heads_of_query, heads_of_key, segment_row, pad_row):
    scores = jnp.einsum(
        "qkgd,skd->kgqs", heads_of_query, heads_of_key, preferred_element_type=jnp.float32
    ) * HEAD_SIZE ** (-0.5)
    return jnp.where(visible(segment_row, pad_row)[None, None], scores, neg_fill)


def norm_back(grad_normed, source, inverse, gain):
    scaled = grad_normed * gain
    grad_source = inverse * scaled - source * inverse**3 * jnp.mean(
        scaled * source, axis=1, keepdims=True
    )
    grad_gain = jnp.sum(grad_normed * source * inverse, axis=0)
    return (grad_source, grad_gain)


def pair_slots(routes, order_row, experts, capacity):
    pair_count = order_row.shape[0]
    place = (
        jnp.zeros((pair_count,), jnp.int32)
        .at[order_row]
        .set(jnp.arange(pair_count, dtype=jnp.int32), unique_indices=True, mode="promise_in_bounds")
        .reshape(routes.shape)
    )
    columns = jnp.arange(experts, dtype=jnp.int32)
    hit = routes[None, :, :] == columns[:, None, None]
    key = jnp.min(jnp.where(hit, place[None], pair_count), axis=2)
    rank = jnp.sum((key[:, None, :] < key[:, :, None]).astype(jnp.int32), axis=2)
    return jnp.where((key < pair_count) & (rank < capacity), rank, -1)


def body(
    tokens,
    cotangent,
    norm_attn,
    norm_moe,
    w_query,
    key_weight,
    value_weight,
    w_out,
    w_router,
    w_gate,
    w_up,
    w_down,
    document_index,
    padding_token_mask,
    routes,
    pair_order,
):
    token_rows, features = tokens.shape
    top_count = routes.shape[1]
    experts = lax.axis_size("expert")
    data = lax.axis_size("dp")
    chips = experts // 2
    half = chips // 2
    ff = w_gate.shape[2]
    capacity = 9 * token_rows * top_count // (8 * experts)
    slot_rows = (capacity + 15) // 16 * 16
    group_of_heads = QUERY_HEADS // KEY_VALUE_HEADS
    score_scale = HEAD_SIZE ** (-0.5)
    me = lax.axis_index("expert")
    my_dp = lax.axis_index("dp")
    core = lax.rem(me, 2)
    core_swap = [(j, j ^ 1) for j in range(experts)]
    partner_swap = [(j, (j + experts // 2) % experts) for j in range(experts)]

    def shifted(j, k):
        chip = j // 2
        return ((chip // half) * half + (chip % half + k) % half) * 2 + j % 2

    def swap(v):
        return lax.ppermute(v, "expert", core_swap)

    def shift(v, k):
        return lax.ppermute(v, "expert", [(j, shifted(j, k)) for j in range(experts)])

    def across(v):
        return lax.ppermute(v, "expert", partner_swap)

    def gathered(shard):
        width = shard.shape[1] // 2
        mine = lax.dynamic_slice_in_dim(shard, core * width, width, axis=1)
        mine = lax.all_gather(mine, "dp", axis=0, tiled=True)
        other = swap(mine)
        first = jnp.where(core == 0, mine, other)
        second = jnp.where(core == 0, other, mine)
        return jnp.concatenate([first, second], axis=1)

    qkv_all = gathered(jnp.concatenate([w_query, key_weight, value_weight], axis=1))
    out_all = gathered(w_out)

    def dp_part(w):
        rows = w.shape[0] // data
        return lax.dynamic_slice_in_dim(w, my_dp * rows, rows, axis=0)

    own = (w_gate[0], w_up[0], w_down[0])
    partner = tuple(
        lax.all_gather(across(dp_part(w)), "dp", axis=0, tiled=True) for w in own
    )

    slots = pair_slots(routes, pair_order[0], experts, capacity)
    all_slots = lax.all_gather(slots, "expert", axis=0, tiled=False)
    hosted = jnp.stack([me, lax.rem(me + experts // 2, experts)]).astype(jnp.int32)

    def tables(sources):
        picked = jnp.stack([
            jnp.stack([
                jnp.stack([all_slots[source, hosted[0]], all_slots[source ^ 1, hosted[0]]]),
                jnp.stack([all_slots[source, hosted[1]], all_slots[source ^ 1, hosted[1]]]),
            ])
            for source in sources
        ])
        picked = picked.reshape(len(sources) * 2, 2, token_rows)
        return picked, jnp.swapaxes(picked, 1, 2)

    def source_of(k):
        chip = me // 2
        return ((chip // half) * half + lax.rem(chip % half + half - k, half)) * 2 + core

    cot_same = cotangent
    cot_other = swap(cotangent)
    cot_far_same = [shift(cotangent, k) for k in range(1, half)]
    cot_far_other = [swap(v) for v in cot_far_same]

    source = tokens.astype(jnp.float32)
    inverse_one = lax.rsqrt(jnp.mean(source * source, axis=1, keepdims=True) + epsilon)
    normed_one = (source * inverse_one * norm_attn).astype(jnp.bfloat16)
    qkv = jnp.dot(normed_one, qkv_all, preferred_element_type=jnp.float32).astype(jnp.bfloat16)
    query_width = QUERY_HEADS * HEAD_SIZE
    kv_width = KEY_VALUE_HEADS * HEAD_SIZE
    heads_of_query = qkv[:, :query_width].reshape(
        token_rows, KEY_VALUE_HEADS, group_of_heads, HEAD_SIZE
    )
    heads_of_key = qkv[:, query_width:query_width + kv_width].reshape(
        token_rows, KEY_VALUE_HEADS, HEAD_SIZE
    )
    heads_of_value = qkv[:, query_width + kv_width:].reshape(token_rows, KEY_VALUE_HEADS, HEAD_SIZE)
    segment_row = document_index[0]
    pad_row = padding_token_mask[0]
    scores = score_block(heads_of_query, heads_of_key, segment_row, pad_row)
    top_score = jnp.max(scores, axis=-1, keepdims=True)
    log_total = top_score + jnp.log(jnp.sum(jnp.exp(scores - top_score), axis=-1, keepdims=True))
    weights = jnp.exp(scores - log_total).astype(jnp.bfloat16)
    attention_mixture = jnp.einsum(
        "kgqs,skd->qkgd", weights, heads_of_value, preferred_element_type=jnp.float32
    )
    attention_mixture = attention_mixture.reshape(token_rows, query_width).astype(jnp.bfloat16)
    hidden_one = source + jnp.dot(attention_mixture, out_all, preferred_element_type=jnp.float32)
    inverse_two = lax.rsqrt(jnp.mean(hidden_one * hidden_one, axis=1, keepdims=True) + epsilon)
    normed_two = (hidden_one * inverse_two * norm_moe).astype(jnp.bfloat16)
    router = jax.nn.softmax(
        jnp.dot(normed_two, w_router, preferred_element_type=jnp.float32), axis=-1
    )
    payload = jnp.concatenate(
        [normed_two, *split_three(router), jnp.zeros((token_rows, 128 - 3 * experts), jnp.bfloat16)],
        axis=1,
    )

    payload_far_same = [shift(payload, k) for k in range(1, half)]
    payload_other = swap(payload)
    near_row, near_col = tables([me])
    near = expert_call(
        hosted, near_row, near_col, payload[None], payload_other[None], cot_same[None],
        cot_other[None], own, partner, experts, slot_rows,
    )
    payload_far_other = [swap(v) for v in payload_far_same]
    far_row, far_col = tables([source_of(k) for k in range(1, half)])
    far = expert_call(
        hosted, far_row, far_col, jnp.stack(payload_far_same), jnp.stack(payload_far_other),
        jnp.stack(cot_far_same), jnp.stack(cot_far_other), own, partner, experts, slot_rows,
    )

    def returned(near_same, near_other, far_same, far_other):
        total = near_same[0].astype(jnp.float32) + swap(near_other[0]).astype(jnp.float32)
        for k in range(1, half):
            both = far_same[k - 1].astype(jnp.float32) + swap(far_other[k - 1]).astype(jnp.float32)
            total = total + shift(both.astype(jnp.bfloat16), half - k).astype(jnp.float32)
        return total

    back = returned(near[2], near[3], far[2], far[3])
    routed = returned(near[0], near[1], far[0], far[1])
    block_out = (hidden_one + routed).astype(jnp.bfloat16)
    from_experts = back[:, :features]
    grad_select = (
        back[:, features:features + experts]
        + back[:, features + experts:features + 2 * experts]
        + back[:, features + 2 * experts:features + 3 * experts]
    )

    saved = [tuple(near[4:]), tuple(far[4:])]
    local_partner = weight_gradient_call(1, saved)
    local_own = weight_gradient_call(0, saved)

    def scattered(v):
        return lax.psum_scatter(v, "dp", scatter_dimension=0, tiled=True)

    expert_gradients = []
    for from_partner, from_own in zip(local_partner, local_own):
        arrived = across(scattered(from_partner))
        total = scattered(from_own).astype(jnp.float32) + arrived.astype(jnp.float32)
        whole = lax.all_gather(total.astype(jnp.bfloat16), "dp", axis=0, tiled=True)
        expert_gradients.append(whole.astype(jnp.float32)[None])
    grad_gate, grad_up, grad_down = expert_gradients

    cot_full = cotangent.astype(jnp.float32)
    grad_logits = router * (grad_select - jnp.sum(router * grad_select, axis=1, keepdims=True))
    grad_normed_two = (
        jnp.dot(grad_logits, w_router.astype(jnp.float32).T, precision=highest) + from_experts
    )
    local_router = jnp.dot(normed_two.astype(jnp.float32).T, grad_logits, precision=highest)
    through_two, local_norm_moe = norm_back(grad_normed_two, hidden_one, inverse_two, norm_moe)
    grad_hidden_one = cot_full + through_two
    grad_branch = grad_hidden_one.astype(jnp.bfloat16)

    def reduced(v):
        width = v.shape[1] // 2
        keep = lax.dynamic_slice_in_dim(v, core * width, width, axis=1)
        give = lax.dynamic_slice_in_dim(v, (1 - core) * width, width, axis=1)
        part = keep.astype(jnp.float32) + swap(give.astype(jnp.bfloat16)).astype(jnp.float32)
        part = scattered(part.astype(jnp.bfloat16))
        step = 1
        while step < chips:
            pairs = [(j, ((j // 2) ^ step) * 2 + j % 2) for j in range(experts)]
            arrived = lax.ppermute(part, "expert", pairs)
            part = (part.astype(jnp.float32) + arrived.astype(jnp.float32)).astype(jnp.bfloat16)
            step *= 2
        other = swap(part)
        first = jnp.where(core == 0, part, other)
        second = jnp.where(core == 0, other, part)
        return jnp.concatenate([first, second], axis=1).astype(jnp.float32)

    local_out = jnp.dot(attention_mixture.T, grad_branch, preferred_element_type=jnp.float32)
    grad_out = reduced(local_out)
    mixture_gradient = jnp.dot(grad_branch, out_all.T, preferred_element_type=jnp.float32).astype(
        jnp.bfloat16
    )
    heads_gradient = mixture_gradient.reshape(
        token_rows, KEY_VALUE_HEADS, group_of_heads, HEAD_SIZE
    )
    scores = score_block(heads_of_query, heads_of_key, segment_row, pad_row)
    probs = jnp.exp(scores - log_total)
    grad_weights = jnp.einsum(
        "qkgd,skd->kgqs", heads_gradient, heads_of_value, preferred_element_type=jnp.float32
    )
    grad_scores = (
        probs * (grad_weights - jnp.sum(probs * grad_weights, axis=-1, keepdims=True))
    ).astype(jnp.bfloat16)
    grad_queries = (
        jnp.einsum("kgqs,skd->qkgd", grad_scores, heads_of_key, preferred_element_type=jnp.float32)
        * score_scale
    )
    grad_queries = grad_queries.reshape(token_rows, query_width).astype(jnp.bfloat16)
    key_rows_gradient = (
        jnp.einsum(
            "kgqs,qkgd->skd", grad_scores, heads_of_query, preferred_element_type=jnp.float32
        )
        * score_scale
    )
    key_rows_gradient = key_rows_gradient.reshape(token_rows, kv_width).astype(jnp.bfloat16)
    value_rows_gradient = jnp.einsum(
        "kgqs,qkgd->skd", weights, heads_gradient, preferred_element_type=jnp.float32
    )
    value_rows_gradient = value_rows_gradient.reshape(token_rows, kv_width).astype(jnp.bfloat16)
    grad_qkv = jnp.concatenate([grad_queries, key_rows_gradient, value_rows_gradient], axis=1)
    local_qkv = jnp.dot(normed_one.T, grad_qkv, preferred_element_type=jnp.float32)
    summed_qkv = reduced(local_qkv)
    grad_query = summed_qkv[:, :query_width]
    grad_key = summed_qkv[:, query_width:query_width + kv_width]
    grad_value = summed_qkv[:, query_width + kv_width:]
    grad_normed_one = jnp.dot(grad_qkv, qkv_all.T, preferred_element_type=jnp.float32)
    through_one, local_norm_attn = norm_back(grad_normed_one, source, inverse_one, norm_attn)
    grad_tokens = grad_hidden_one + through_one
    grad_router, grad_norm_attn, grad_norm_moe = lax.psum(
        (local_router, local_norm_attn, local_norm_moe), ("dp", "expert")
    )
    return (
        block_out,
        grad_tokens,
        grad_norm_attn,
        grad_norm_moe,
        grad_query,
        grad_key,
        grad_value,
        grad_out,
        grad_router,
        grad_gate,
        grad_up,
        grad_down,
    )


def solution(mesh):
    placed = (
        P(("dp", "expert"), None),
        P(("dp", "expert"), None),
        P(),
        P(),
        P("dp", None),
        P("dp", None),
        P("dp", None),
        P("dp", None),
        P(),
        P("expert", None, None),
        P("expert", None, None),
        P("expert", None, None),
        P(("dp", "expert"), None),
        P(("dp", "expert"), None),
        P(("dp", "expert"), None),
        P(("dp", "expert"), None),
    )
    return jax.shard_map(
        body,
        mesh=mesh,
        in_specs=placed,
        out_specs=(
            P(("dp", "expert"), None),
            P(("dp", "expert"), None),
            P(),
            P(),
            P("dp", None),
            P("dp", None),
            P("dp", None),
            P("dp", None),
            P(),
            P("expert", None, None),
            P("expert", None, None),
            P("expert", None, None),
        ),
        check_vma=False,
    )
```

time: 1740 us -> 918 us (0.53)
  other arithmetic: 479 us -> 104 us
  local copies, waits for them, and re-layouts: 402 us -> 36.6 us
  Pallas kernels: 0 us -> 168 us
  waiting for transfers between devices: 509 us -> 353 us
  matrix products: 231 us -> 92.9 us
  blocking collectives: 75 us -> 127 us
    unnamed x9 -> x1, other arithmetic: 377 us -> 0.02 us
    all_to_all x4 -> x0, waiting for transfers between devices: 366 us -> none  [the longest x1 170 us: body(): lax.all_to_all(grad_produced, 'expert', split_axis=0, concat_axis=1, tile...]
    ppermute x0 -> x28, waiting for transfers between devices: none -> 249 us  [the longest x6 136 us: across(): return lax.ppermute(v, 'expert', partner_swap)]
    pallas_call x0 -> x4, Pallas kernels: none -> 168 us  [the longest x2 133 us: expert_call(): pl.pallas_call(functools.partial(expert_kernel, experts, chunks, tokens,...]
    convert_element_type x5 -> x2, local copies, waits for them, and re-layouts: 143 us -> 3.13 us  [reduced(): give.astype(jnp.bfloat16)]
    gather x7 -> x0, local copies, waits for them, and re-layouts: 128 us -> none  [the longest x1 21 us: body(): returned_rows[pair_slot].reshape(token_rows, top_count, features)]
    reduce_scatter x4 -> x8, waiting for transfers between devices: 118 us -> 0.08 us  [scattered(): return lax.psum_scatter(v, 'dp', scatter_dimension=0, tiled=True)]
    dot_general x18 -> x3, matrix products: 140 us -> 22.6 us  [the longest x1 11.1 us: body(): jnp.dot(grad_qkv, qkv_all.T, preferred_element_type=jnp.float32)]
  transfers between devices with their start and end apart: 12 -> 44, of which waited for: 6 -> 16; matrix products, arithmetic and copies ran while one was open for 45% -> 25% of each run, Pallas kernels for 0% -> 9%
where the time goes in v1:
time: 918 us; the launch traced here: 916 us
  waiting for transfers between devices  353 us (38%)
  Pallas kernels  168 us (18%)
  blocking collectives  127 us (14%)
  other arithmetic  104 us (11%)
  matrix products  92.9 us (10%)
  local copies, waits for them, and re-layouts  36.6 us (4%)
  starting transfers between devices  19.1 us (2%)
  between operations  15.3 us (2%)
    ppermute x6, waiting for transfers between devices, across(): return lax.ppermute(v, 'expert', partner_swap)  136 us
    pallas_call x2, Pallas kernels, expert_call(): pl.pallas_call(functools.partial(expert_kernel, experts, chunks, tokens,...  133 us
    all_gather x1, blocking collectives, body(): all_slots = lax.all_gather(slots, 'expert', axis=0, tiled=False)  85.7 us
    ppermute x4, waiting for transfers between devices, shift(): lax.ppermute(v, 'expert', [(j, shifted(j, k)) for j in range(experts)])  80.7 us
    all_gather x3, waiting for transfers between devices, body(): whole = lax.all_gather(total.astype(jnp.bfloat16), 'dp', axis=0, tiled=True)  78 us
    psum x1, blocking collectives, body(): lax.psum((local_router, local_norm_attn, local_norm_moe), ('dp', 'expert'))  41.2 us
    pallas_call x2, Pallas kernels, weight_gradient_call(): pl.pallas_call(functools.partial(weight_gradient_kernel, len(saved)), gri...  34.8 us
    all_gather x2, waiting for transfers between devices, gathered(): mine = lax.all_gather(mine, 'dp', axis=0, tiled=True)  23.9 us
  transfers between devices with their start and end apart: 44, of which 16 were waited for; matrix products, arithmetic and copies ran while one was open for 25% of the time, Pallas kernels for 9%

profile of v1, /device:TPU:0, one launch (start us, length us, event | category | flops | bytes accessed | tf_op | source)
XLA Modules:
  0.0 915.6 jit_solution(10655660759188569480)
XLA Ops:
  16.1 26.0 %collective-permute-done.5 = bf16[384,768]{1,0:T(8,128)(2,1)S(1)} collective-permute-done((bf16[384,768]{1,0:T(8,128)(2,1)S(1)}, bf16[384,768]{1,0:T(8,128)(2,1)S(1)}, u32[]{:S(2)}, u32[]{:S(2)}) %collective-permute-start.5) | collective-permute-done | bytes 589856 | tf_op jit(solution)/shard_map/ppermute | solution.py:391
  44.2 28.0 %collective-permute-done.4 = bf16[384,768]{1,0:T(8,128)(2,1)S(1)} collective-permute-done((bf16[384,768]{1,0:T(8,128)(2,1)S(1)}, bf16[384,768]{1,0:T(8,128)(2,1)S(1)}, u32[]{:S(2)}, u32[]{:S(2)}) %collective-permute-start.4) | collective-permute-done | bytes 589856 | tf_op jit(solution)/shard_map/ppermute | solution.py:391
  73.2 23.9 %all-gather.11.cloned.1.call-done = bf16[1536,768]{1,0:T(8,128)(2,1)} async-done(((bf16[384,768]{1,0:T(8,128)(2,1)}), bf16[1536,768]{1,0:T(8,128)(2,1)}) %all-gather.11.cloned.1.call-update) | async-done | bytes 2359312 | tf_op jit(solution)/shard_map/all_gather | solution.py:396
  102.9 25.7 %collective-permute-done.6 = bf16[192,1536]{1,0:T(8,128)(2,1)} collective-permute-done((bf16[192,1536]{1,0:T(8,128)(2,1)}, bf16[192,1536]{1,0:T(8,128)(2,1)}, u32[]{:S(2)}, u32[]{:S(2)}) %collective-permute-start.6) | collective-permute-done | bytes 589856 | tf_op jit(solution)/shard_map/ppermute | solution.py:391
  154.9 10.6 %exponential_reduce_fusion = f32[2,6,640]{2,1,0:T(8,128)S(1)} fusion(f32[2,640,640,6]{2,1,3,0:T(8,128)} %get-tuple-element.100, f32[2,6,640]{2,1,0:T(8,128)S(1)} %get-tuple-element.99, pred[640,640]{0,1:T(8,128)(4,1)S(1)} %fusion.24), kind=kLoop, calls=%fused_computation.8 | loop fusion | flops 19653120 | bytes 20131840 | tf_op jit(solution)/shard_map/reduce_sum | solution.py:455
  165.5 11.9 %convolution_convert_fusion.1 = bf16[2,128,6,640]{3,1,2,0:T(8,128)(2,1)S(1)} fusion(bf16[640,2,128,1]{2,1,0,3:T(2,128)(2,1)S(1)} %bitcast.157, f32[2,640,640,6]{2,1,3,0:T(8,128)} %get-tuple-element.100, f32[2,6,640]{2,1,0:T(8,128)S(1)} %log_add_fusion, pred[640,640]{0,1:T(8,128)(4,1)S(1)} %fusion.24), kind=kOutput, calls=%fused_computation.62 | convolution fusion | flops 1278935040 | bytes 22394880 | tf_op jit(solution)/shard_map/kgqs,skd->qkgd/dot_general | solution.py:457
  181.2 11.5 %multiply_convert_fusion.1 = bf16[640,1536]{1,0:T(8,128)(2,1)S(1)} fusion(f32[640,1536]{1,0:T(8,128)S(1)} %get-tuple-element.102, f32[1536]{0:T(1024)S(1)} %copy-done.33, f32[640]{0:T(1024)S(1)} %get-tuple-element.98), kind=kLoop, calls=%fused_computation.50 | loop fusion | flops 2949120 | bytes 5906944 | tf_op jit(solution)/shard_map/convert_element_type | solution.py:463
  211.6 85.7 %all_gather.30 = s32[8,8,640]{2,1,0:T(8,128)S(1)} all-gather(s32[1,8,640]{2,1,0:T(8,128)S(1)} %bitcast_select_fusion.1), channel_id=1, replica_groups=mesh['dp'=4,'expert'=8] {'expert'}, dimensions={0}, use_global_device_ids=true | all-gather | bytes 184320 | tf_op jit(solution)/shard_map/all_gather | solution.py:415
  302.1 66.3 %expert_rows.2 = (bf16[1,640,1536]{2,1,0:T(8,128)(2,1)}, bf16[1,640,1536]{2,1,0:T(8,128)(2,1)}, bf16[1,640,1664]{2,1,0:T(8,128)(2,1)}, bf16[1,640,1664]{2,1,0:T(...) custom-call(s32[2]{0:T(128)} %pad_add_fusion.2.hosted, ...), custom_call_target="tpu_custom_call" | custom-call | flops 35886465024 | bytes 41943040 | tf_op jit(solution)/shard_map/expert_rows/pallas_call | solution.py:207
  368.5 66.4 %expert_rows.3 = (bf16[1,640,1536]{2,1,0:T(8,128)(2,1)}, bf16[1,640,1536]{2,1,0:T(8,128)(2,1)}, bf16[1,640,1664]{2,1,0:T(8,128)(2,1)}, bf16[1,640,1664]{2,1,0:T(...) custom-call(s32[2]{0:T(128)} %pad_add_fusion.2.hosted, ...), custom_call_target="tpu_custom_call" | custom-call | flops 35886465024 | bytes 41943040 | tf_op jit(solution)/shard_map/expert_rows/pallas_call | solution.py:207
  434.9 17.3 %expert_weight_gradients.3 = (bf16[1536,768]{1,0:T(8,128)(2,1)}, bf16[1536,768]{1,0:T(8,128)(2,1)}, bf16[768,1536]{1,0:T(8,128)(2,1)}) custom-call(bf16[2,736,1536]{2,1,0:T(8,128)(2,1)} %get-tuple-element.44.refs_0_, bf16[2,736,768]{2,1,0:T(8,128)(2,1)} %get-tuple-element.45.refs_1_, bf16[2,736,768]{2,1,0:T(8,128)(2,1)} %get-tuple-element.46.refs_2_, ...), custom_call_target="tpu_custom_call" | custom-call | flops 10418651136 | bytes 25165824 | tf_op jit(solution)/shard_map/expert_weight_gradients/pallas_call | solution.py:274
  452.3 17.5 %expert_weight_gradients.2 = (bf16[1536,768]{1,0:T(8,128)(2,1)}, bf16[1536,768]{1,0:T(8,128)(2,1)}, bf16[768,1536]{1,0:T(8,128)(2,1)}) custom-call(bf16[2,736,1536]{2,1,0:T(8,128)(2,1)} %get-tuple-element.44.refs_0_, bf16[2,736,768]{2,1,0:T(8,128)(2,1)} %get-tuple-element.45.refs_1_, bf16[2,736,768]{2,1,0:T(8,128)(2,1)} %get-tuple-element.46.refs_2_, ...), custom_call_target="tpu_custom_call" | custom-call | flops 10418651136 | bytes 25165824 | tf_op jit(solution)/shard_map/expert_weight_gradients/pallas_call | solution.py:274
  483.5 45.4 %collective-permute-done.16 = bf16[640,1664]{1,0:T(8,128)(2,1)} collective-permute-done((bf16[640,1664]{1,0:T(8,128)(2,1)}, bf16[640,1664]{1,0:T(8,128)(2,1)}, u32[]{:S(2)}, u32[]{:S(2)}) %collective-permute-start.16) | collective-permute-done | bytes 2129952 | tf_op jit(solution)/shard_map/ppermute | solution.py:388
  535.2 35.2 %collective-permute-done.13 = bf16[640,1536]{1,0:T(8,128)(2,1)} collective-permute-done((bf16[640,1536]{1,0:T(8,128)(2,1)}, bf16[640,1536]{1,0:T(8,128)(2,1)}, u32[]{:S(2)}, u32[]{:S(2)}) %collective-permute-start.13) | collective-permute-done | bytes 1966112 | tf_op jit(solution)/shard_map/ppermute | solution.py:388
  592.1 14.1 %fusion = (f32[2,6,640]{2,1,0:T(8,128)S(1)}, f32[2,640,640,6]{2,1,3,0:T(8,128)}) fusion(f32[2,640,640,6]{2,1,3,0:T(8,128)} %get-tuple-element.100, f32[2,6,640]{2,1,0:T(8,128)S(1)} %log_add_fusion, pred[640,640]{0,1:T(8,128)(4,1)S(1)} %fusion.24, bf16[640,2,6,128]{0,3,2,1:T(8,128)(2,1)S(1)} %bitcast.151, bf16[640,2,128,1]{2,1,0,3:T(2,128)(2,1)S(1)} %bitcast.158), kind=kOutput, calls=%fused_computation.3 | convolution fusion | flops 1282859520 | bytes 42086400 | tf_op jit(solution)/shard_map/qkgd,skd->kgqs/dot_general | solution.py:555
  606.2 14.2 %fusion.2 = bf16[2,6,640,640]{2,3,1,0:T(8,128)(2,1)S(1)} fusion(f32[2,640,640,6]{2,1,3,0:T(8,128)} %get-tuple-element.107, f32[2,640,640,6]{2,1,3,0:T(8,128)} %get-tuple-element.100, f32[2,6,640]{2,1,0:T(8,128)S(1)} %get-tuple-element.106, f32[2,6,640]{2,1,0:T(8,128)S(1)} %log_add_fusion, pred[640,640]{0,1:T(8,128)(4,1)S(1)} %fusion.24), kind=kLoop, calls=%fused_computation.5 | loop fusion | flops 29491200 | bytes 49623040 | tf_op jit(solution)/shard_map/convert_element_type | solution.py:560
  659.1 28.1 %collective-permute-done.25 = bf16[384,768]{1,0:T(8,128)(2,1)S(1)} collective-permute-done((bf16[384,768]{1,0:T(8,128)(2,1)}, bf16[384,768]{1,0:T(8,128)(2,1)S(1)}, u32[]{:S(2)}, u32[]{:S(2)}) %collective-permute-start.25) | collective-permute-done | bytes 589856 | tf_op jit(solution)/shard_map/ppermute | solution.py:391
  689.5 28.3 %collective-permute-done.26 = bf16[384,768]{1,0:T(8,128)(2,1)S(1)} collective-permute-done((bf16[384,768]{1,0:T(8,128)(2,1)}, bf16[384,768]{1,0:T(8,128)(2,1)S(1)}, u32[]{:S(2)}, u32[]{:S(2)}) %collective-permute-start.26) | collective-permute-done | bytes 589856 | tf_op jit(solution)/shard_map/ppermute | solution.py:391
  720.3 11.1 %fusion.17 = (f32[1536]{0:T(1024)S(1)}, f32[640]{0:T(1024)S(1)}, f32[640,1536]{1,0:T(8,128)}) fusion(bf16[640,1536]{1,0:T(8,128)(2,1)} %param.16, f32[640]{0:T(1024)S(1)} %copy-done.38, f32[1536]{0:T(1024)S(1)} %copy-done.42, bf16[1536,1024]{1,0:T(8,128)(2,1)} %copy-done.13, bf16[1536,1024]{1,0:T(8,128)(2,1)} %copy-done.12, ...), kind=kOutput, calls=%fused_computation.38 | convolution fusion | flops 4053858304 | bytes 14828544 | tf_op jit(solution)/shard_map/dot_general | solution.py:583
  732.5 41.2 %all-reduce = (f32[1536]{0:T(1024)}, f32[1536]{0:T(1024)}, f32[1536,8]{0,1:T(8,128)}) all-reduce(f32[1536]{0:T(1024)S(1)} %get-tuple-element.62, f32[1536]{0:T(1024)S(1)} %get-tuple-element.60, f32[1536,8]{0,1:T(8,128)S(1)} %fusion.43), channel_id=1, replica_groups=mesh['dp'=4,'expert'=8] {'dp','expert'}, use_global_device_ids=true, to_apply=%region_14.15 | all-reduce | flops 15360 | bytes 122880 | tf_op jit(solution)/shard_map/psum | solution.py:586
  784.8 34.7 %all-gather.19.cloned.1.call-done = bf16[1536,768]{1,0:T(8,128)(2,1)} async-done(((bf16[384,768]{1,0:T(8,128)(2,1)}), bf16[1536,768]{1,0:T(8,128)(2,1)}) %all-gather.19.cloned.1.call-update) | async-done | bytes 2359312 | tf_op jit(solution)/shard_map/all_gather | solution.py:514
  827.2 31.5 %all-gather.21.cloned.1.call-done = bf16[1536,768]{1,0:T(8,128)(2,1)} async-done(((bf16[384,768]{1,0:T(8,128)(2,1)}), bf16[1536,768]{1,0:T(8,128)(2,1)}) %all-gather.21.cloned.1.call-update) | async-done | bytes 2359312 | tf_op jit(solution)/shard_map/all_gather | solution.py:514
  871.8 14.4 %collective-permute-done.19 = bf16[384,1024]{1,0:T(8,128)(2,1)S(1)} collective-permute-done((bf16[384,1024]{1,0:T(8,128)(2,1)S(1)}, bf16[384,1024]{1,0:T(8,128)(2,1)S(1)}, u32[]{:S(2)}, u32[]{:S(2)}) %collective-permute-start.19) | collective-permute-done | bytes 786464 | tf_op jit(solution)/shard_map/ppermute | solution.py:537
  886.6 11.9 %all-gather.23.cloned.1.call-done = bf16[768,1536]{1,0:T(8,128)(2,1)} async-done(((bf16[192,1536]{1,0:T(8,128)(2,1)}), bf16[768,1536]{1,0:T(8,128)(2,1)}) %all-gather.23.cloned.1.call-update) | async-done | bytes 2359312 | tf_op jit(solution)/shard_map/all_gather | solution.py:514
  (273 shorter events, 199.3 us)
Async XLA Ops:
  7.2 65.9 %all-gather.9.cloned.1.call-start = ((), (), s32[]{:S(2)}) async-start(), calls=%async_computation.8 | async-start | bytes 3932160 | tf_op jit(solution)/shard_map/all_gather | solution.py:396
  9.9 87.2 %all-gather.11.cloned.1.call-start = ((), (), s32[]{:S(2)}) async-start(), calls=%async_computation.9 | async-start | bytes 2949120 | tf_op jit(solution)/shard_map/all_gather | solution.py:396
  10.9 289.9 %all-gather.15.cloned.1.call-start = ((), (), s32[]{:S(2)}) async-start(), calls=%async_computation.11 | async-start | bytes 2949120 | tf_op jit(solution)/shard_map/all_gather | solution.py:411
  42.9 257.8 %all-gather.13.cloned.1.call-start = ((), (), s32[]{:S(2)}) async-start(), calls=%async_computation.10 | async-start | bytes 2949120 | tf_op jit(solution)/shard_map/all_gather | solution.py:411
  73.1 227.7 %all-gather.17.cloned.1.call-start = ((), (), s32[]{:S(2)}) async-start(), calls=%async_computation.12 | async-start | bytes 2949120 | tf_op jit(solution)/shard_map/all_gather | solution.py:411
  73.1 60.6 %collective-permute-start = (bf16[1536,1024]{1,0:T(8,128)(2,1)}, bf16[1536,1024]{1,0:T(8,128)(2,1)}, u32[]{:S(2)}, u32[]{:S(2)}) collective-permute-start(bf16[1536,1024]{1,0:T(8,128)(2,1)} %all-gather.9.cloned.1.call-done), channel_id=1, source_target_pairs={{0,1},{1,0},{2,3},{3,2},{4,5},{5,4},{6,7},{7,6},{8,9},{9,8},{10,11... | collective-permute-start | bytes 9437192 | tf_op jit(solution)/shard_map/ppermute | solution.py:385
  128.6 529.2 %reduce-scatter.15.cloned.1.call-start = ((), (), s32[]{:S(2)}) async-start(), calls=%async_computation.16 | async-start | bytes 2949120 | tf_op jit(solution)/shard_map/reduce_scatter | solution.py:508
  196.9 103.7 %collective-permute-start.8 = (bf16[640,1664]{1,0:T(8,128)(2,1)}, bf16[640,1664]{1,0:T(8,128)(2,1)}, u32[]{:S(2)}, u32[]{:S(2)}) collective-permute-start(bf16[640,1664]{1,0:T(8,128)(2,1)} %concatenate.24), channel_id=1, source_target_pairs={{0,2},{1,3},{2,0},{3,1},{4,6},{5,7},{6,4},{7,5},{8,10},{9,11},{10,... | collective-permute-start | bytes 6389768 | tf_op jit(solution)/shard_map/ppermute | solution.py:388
  197.4 103.4 %collective-permute-start.2 = (bf16[640,1664]{1,0:T(8,128)(2,1)}, bf16[640,1664]{1,0:T(8,128)(2,1)S(1)}, u32[]{:S(2)}, u32[]{:S(2)}) collective-permute-start(bf16[640,1664]{1,0:T(8,128)(2,1)} %concatenate.24), channel_id=1, source_target_pairs={{0,1},{1,0},{2,3},{3,2},{4,5},{5,4},{6,7},{7,6},{8,9},{9,8},{10,11... | collective-permute-start | bytes 6389768 | tf_op jit(solution)/shard_map/ppermute | solution.py:385
  197.4 102.9 %collective-permute-start.10 = (bf16[640,1536]{1,0:T(8,128)(2,1)}, bf16[640,1536]{1,0:T(8,128)(2,1)}, u32[]{:S(2)}, u32[]{:S(2)}) collective-permute-start(bf16[640,1536]{1,0:T(8,128)(2,1)} %param.17), channel_id=1, source_target_pairs={{0,2},{1,3},{2,0},{3,1},{4,6},{5,7},{6,4},{7,5},{8,10},{9,11},{10,... | collective-permute-start | bytes 5898248 | tf_op jit(solution)/shard_map/ppermute | solution.py:388
  198.9 101.9 %collective-permute-start.3 = (bf16[640,1536]{1,0:T(8,128)(2,1)}, bf16[640,1536]{1,0:T(8,128)(2,1)}, u32[]{:S(2)}, u32[]{:S(2)}) collective-permute-start(bf16[640,1536]{1,0:T(8,128)(2,1)} %param.17), channel_id=1, source_target_pairs={{0,1},{1,0},{2,3},{3,2},{4,5},{5,4},{6,7},{7,6},{8,9},{9,8},{10,11... | collective-permute-start | bytes 5898248 | tf_op jit(solution)/shard_map/ppermute | solution.py:385
  300.2 68.2 %collective-permute-start.11 = (bf16[640,1536]{1,0:T(8,128)(2,1)}, bf16[640,1536]{1,0:T(8,128)(2,1)}, u32[]{:S(2)}, u32[]{:S(2)}) collective-permute-start(bf16[640,1536]{1,0:T(8,128)(2,1)} %collective-permute-done.10), channel_id=1, source_target_pairs={{0,1},{1,0},{2,3},{3,2},{4,5},{5,4},{6,7},{7,6},{8,9},{9,8},{10,11... | collective-permute-start | bytes 5898248 | tf_op jit(solution)/shard_map/ppermute | solution.py:385
  300.6 67.9 %collective-permute-start.9 = (bf16[640,1664]{1,0:T(8,128)(2,1)}, bf16[640,1664]{1,0:T(8,128)(2,1)}, u32[]{:S(2)}, u32[]{:S(2)}) collective-permute-start(bf16[640,1664]{1,0:T(8,128)(2,1)} %collective-permute-done.8), channel_id=1, source_target_pairs={{0,1},{1,0},{2,3},{3,2},{4,5},{5,4},{6,7},{7,6},{8,9},{9,8},{10,11... | collective-permute-start | bytes 6389768 | tf_op jit(solution)/shard_map/ppermute | solution.py:385
  452.3 206.8 %reduce-scatter.13.cloned.1.call-start = ((), (), s32[]{:S(2)}) async-start(), calls=%async_computation.15 | async-start | bytes 2949120 | tf_op jit(solution)/shard_map/reduce_scatter | solution.py:508
  469.8 219.5 %reduce-scatter.19.cloned.1.call-start = ((), (), s32[]{:S(2)}) async-start(), calls=%async_computation.19 | async-start | bytes 2949120 | tf_op jit(solution)/shard_map/reduce_scatter | solution.py:508
  470.6 218.9 %reduce-scatter.17.cloned.1.call-start = ((), (), s32[]{:S(2)}) async-start(), calls=%async_computation.18 | async-start | bytes 2949120 | tf_op jit(solution)/shard_map/reduce_scatter | solution.py:508
  471.3 248.9 %reduce-scatter.23.cloned.1.call-start = ((), (), s32[]{:S(2)}) async-start(), calls=%async_computation.22 | async-start | bytes 2949120 | tf_op jit(solution)/shard_map/reduce_scatter | solution.py:508
  471.9 301.7 %reduce-scatter.21.cloned.1.call-start = ((), (), s32[]{:S(2)}) async-start(), calls=%async_computation.21 | async-start | bytes 2949120 | tf_op jit(solution)/shard_map/reduce_scatter | solution.py:508
  483.3 87.2 %collective-permute-start.13 = (bf16[640,1536]{1,0:T(8,128)(2,1)}, bf16[640,1536]{1,0:T(8,128)(2,1)}, u32[]{:S(2)}, u32[]{:S(2)}) collective-permute-start(bf16[640,1536]{1,0:T(8,128)(2,1)} %fusion.18), channel_id=1, source_target_pairs={{0,2},{1,3},{2,0},{3,1},{4,6},{5,7},{6,4},{7,5},{8,10},{9,11},{10,... | collective-permute-start | bytes 5898248 | tf_op jit(solution)/shard_map/ppermute | solution.py:388
  483.4 299.3 %reduce-scatter.11.cloned.1.call-start = ((), (), s32[]{:S(2)}) async-start(), calls=%async_computation.14 | async-start | bytes 2949120 | tf_op jit(solution)/shard_map/reduce_scatter | solution.py:508
  641.5 141.2 %reduce-scatter.9.cloned.1.call-start = ((), (), s32[]{:S(2)}) async-start(), calls=%async_computation.13 | async-start | bytes 3932160 | tf_op jit(solution)/shard_map/reduce_scatter | solution.py:508
  657.8 161.7 %all-gather.19.cloned.1.call-start = ((), (), s32[]{:S(2)}) async-start(), calls=%async_computation.17 | async-start | bytes 2949120 | tf_op jit(solution)/shard_map/all_gather | solution.py:514
  689.3 169.4 %all-gather.21.cloned.1.call-start = ((), (), s32[]{:S(2)}) async-start(), calls=%async_computation.20 | async-start | bytes 2949120 | tf_op jit(solution)/shard_map/all_gather | solution.py:514
  719.9 178.6 %all-gather.23.cloned.1.call-start = ((), (), s32[]{:S(2)}) async-start(), calls=%async_computation.23 | async-start | bytes 2949120 | tf_op jit(solution)/shard_map/all_gather | solution.py:514
  (69 other events, 1535.2 us)
Sparse Core Ops, SparseCore 0:
  10.4 46.6 all-gather.8
  59.6 37.4 all-gather.10
  99.5 37.4 all-gather.14
  139.3 37.4 all-gather.12
  178.5 37.4 all-gather.16
  452.4 36.0 reduce-scatter.14
  491.5 37.3 reduce-scatter.12
  532.0 37.3 reduce-scatter.18
  572.4 37.3 reduce-scatter.16
  612.8 37.3 reduce-scatter.22
  653.3 37.3 reduce-scatter.20
  694.2 37.3 reduce-scatter.10
  735.2 44.7 reduce-scatter.8
  782.2 37.2 all-gather.18
  821.2 37.4 all-gather.20
  861.0 37.4 all-gather.22

commit v2 on v0

v2 whole, which is shorter than its diff:
```python
import functools

import jax
import jax.numpy as jnp
from jax import lax
from jax.experimental import pallas as pl
from jax.experimental.pallas import tpu as pltpu
from jax.sharding import PartitionSpec as P

bf16 = jnp.bfloat16
f32 = jnp.float32
MIB = 1024 * 1024
LONG = pl.CostEstimate(flops=16 << 30, bytes_accessed=30 * MIB, transcendentals=0)
COST = pl.CostEstimate(flops=1000, bytes_accessed=1000, transcendentals=0)
NT_DIMS = (((1,), (1,)), ((), ()))
TN_DIMS = (((0,), (0,)), ((), ()))


def mm(a, b):
    return jnp.dot(a, b, preferred_element_type=f32)


def mm_nt(a, b):
    return lax.dot_general(a, b, NT_DIMS, preferred_element_type=f32)


def mm_tn(a, b):
    return lax.dot_general(a, b, TN_DIMS, preferred_element_type=f32)


def split_three(v):
    high = v.astype(bf16)
    rest = v - high.astype(f32)
    middle = rest.astype(bf16)
    low = (rest - middle.astype(f32)).astype(bf16)
    return high, middle, low


def lanes(start, size):
    return pl.ds(pl.multiple_of(start, 128), size)


def specs(kinds):
    table = {"s": pltpu.SMEM, "v": pltpu.VMEM, "a": pl.ANY}
    return [pl.BlockSpec(memory_space=table[kind]) for kind in kinds]


def params():
    return pltpu.CompilerParams(vmem_limit_bytes=60 * MIB)


def expert_kernel(experts, slots, base, data, pieces, chunks, n_weights, n_prev, n_saved, rows, *refs):
    count = len(slots)
    hosted, sources, refs = refs[0], refs[1:1 + 4 * chunks], refs[1 + 4 * chunks:]
    sources = [sources[4 * i:4 * i + 4] for i in range(chunks)]
    weight_refs, refs = refs[:n_weights], refs[n_weights:]
    prev, refs = refs[:n_prev], refs[n_prev + n_saved:]
    po_same, po_other, pg_same, pg_other, x_out, gp_out, h_out, gg_out, gu_out = refs[:9]
    (wg, wu, wd, nbuf, cbuf, x, gp, gc, sc, h, gg, gu, dmat, dtmat, gcol, vcol, tail_t,
     w_sem, in_sem, act_sem, p_sem) = refs[9:]
    tokens, features = sources[0][2].shape
    extra = sources[0][0].shape[1] - features
    ff = wg.shape[2]
    wide = features // 2
    tail = slice(features, features + extra)

    weight_copies = []
    taken = 0
    for place, slot in enumerate(slots):
        if slot == 0:
            pairs = list(zip(weight_refs[taken:taken + 3], (wg.at[place], wu.at[place], wd.at[place])))
            taken += 3
        else:
            tall_f, tall_h = features // data, ff // data
            pairs = []
            for index, begin, size, whose, first in pieces:
                ref = weight_refs[taken + index]
                source = jnp.bitwise_xor(hosted[2], whose[1]) if whose[0] else whose[1]
                wide_rows = max(0, min(size, tall_f - first))
                if wide_rows:
                    at = pl.ds(pl.multiple_of(source * tall_f + first, 16), wide_rows)
                    pairs += [
                        (ref.at[pl.ds(begin, wide_rows), pl.ds(0, ff)], wg.at[place, at]),
                        (ref.at[pl.ds(begin, wide_rows), pl.ds(ff, ff)], wu.at[place, at]),
                    ]
                if wide_rows < size:
                    at = pl.ds(pl.multiple_of(source * tall_h + first + wide_rows - tall_f, 16), size - wide_rows)
                    pairs.append((ref.at[pl.ds(begin + wide_rows, size - wide_rows)], wd.at[place, at]))
            taken += 1 + max(piece[0] for piece in pieces)
        weight_copies.append([
            pltpu.make_async_copy(source, target, w_sem.at[place, i])
            for i, (source, target) in enumerate(pairs)
        ])

    def input_copies(index):
        targets = (nbuf.at[0], nbuf.at[1], cbuf.at[0], cbuf.at[1])
        return [
            pltpu.make_async_copy(source, target, in_sem.at[i])
            for i, (source, target) in enumerate(zip(sources[index], targets))
        ]

    def act_copies(chunk, place):
        at = pl.ds(pl.multiple_of(base + chunk * 2 * rows, 16), 2 * rows)
        return [
            pltpu.make_async_copy(source.at[place], target.at[place, at], act_sem.at[place, i])
            for i, (source, target) in enumerate(
                ((x, x_out), (gp, gp_out), (h, h_out), (gg, gg_out), (gu, gu_out)))
        ]

    def partial_copies(chunk):
        return (
            pltpu.make_async_copy(nbuf.at[0], pg_same.at[chunk], p_sem.at[0]),
            pltpu.make_async_copy(nbuf.at[1], pg_other.at[chunk], p_sem.at[1]),
            pltpu.make_async_copy(cbuf.at[0], po_same.at[chunk], p_sem.at[2]),
            pltpu.make_async_copy(cbuf.at[1], po_other.at[chunk], p_sem.at[3]),
        )

    def dispatch(q):
        columns = nbuf[q, :, tail].astype(f32)
        tail_t[...] = columns.T
        token_lane = lax.broadcasted_iota(jnp.int32, (tokens, extra), 1)
        wanted = lax.broadcasted_iota(jnp.int32, (tokens, count * rows), 1)
        slot_cols = []
        for place in range(count):
            expert = hosted[slots[place]]
            row = (tail_t[pl.ds(3 * experts + expert, 1), :] * 128.0
                   + tail_t[pl.ds(4 * experts + expert, 1), :] - 1.0).astype(jnp.int32)
            hit = lax.broadcasted_iota(jnp.int32, (rows, tokens), 0) == row
            dmat[q, place * rows:(place + 1) * rows, :] = jnp.where(hit, 1.0, 0.0).astype(bf16)
            factor = jnp.where(token_lane == 3 * experts + expert, 128.0, 0.0)
            factor = jnp.where(token_lane == 4 * experts + expert, 1.0, factor)
            slot_cols.append(jnp.sum(columns * factor, axis=1, keepdims=True).astype(jnp.int32) - 1)
        target = slot_cols[0]
        if count == 2:
            second = wanted >= rows
            target = jnp.where(second, slot_cols[1], slot_cols[0])
            wanted = jnp.where(second, wanted - rows, wanted)
        dtmat[q] = jnp.where(wanted == target, 1.0, 0.0).astype(bf16)
        parts = mm(dmat[q], nbuf[q, :, tail])
        lane = lax.broadcasted_iota(jnp.int32, (rows, extra), 1)
        for place in range(count):
            expert = hosted[slots[place]]
            mine = (lane == expert) | (lane == expert + experts) | (lane == expert + 2 * experts)
            g = jnp.sum(jnp.where(mine, parts[place * rows:(place + 1) * rows], 0.0), axis=1, keepdims=True)
            gcol[place, q * rows:(q + 1) * rows, :] = jnp.broadcast_to(g, (rows, 128))

        @pl.loop(0, 2)
        def _(tile):
            cols = lanes(tile * wide, wide)
            found = mm(dmat[q], nbuf[q, :, cols]).astype(bf16)
            cot = mm(dmat[q], cbuf[q, :, cols])
            gc[q, :, cols] = cot.astype(bf16)
            for place in range(count):
                at = slice(q * rows, (q + 1) * rows)
                own = slice(place * rows, (place + 1) * rows)
                x[place, at, cols] = found[own]
                gp[place, at, cols] = (cot[own] * gcol[place, at, 0:1]).astype(bf16)

    def forward_backward(place):
        for q in range(2):
            at = slice(q * rows, (q + 1) * rows)
            gate = mm(x[place, at, :], wg[place])
            up = mm(x[place, at, :], wu[place])
            dh = mm_nt(gp[place, at, :], wd[place])
            sig = 1.0 / (1.0 + jnp.exp(-gate))
            act = gate * sig
            h[place, at, :] = (act * up).astype(bf16)
            gg[place, at, :] = (dh * up * (sig * (1.0 + gate * (1.0 - sig)))).astype(bf16)
            gu[place, at, :] = (dh * act).astype(bf16)

    def produce(place):
        vcol[place] = jnp.zeros(vcol.shape[1:], f32)

        @pl.loop(0, 2)
        def _(tile):
            cols = lanes(tile * wide, wide)
            for q in range(2):
                at = slice(q * rows, (q + 1) * rows)
                own = pl.ds(pl.multiple_of(place * rows, 16), rows)
                produced = mm(h[place, at, :], wd[place, :, cols]).astype(bf16).astype(f32)
                along = produced * gc[q, own, cols].astype(f32)
                folded = along[:, :128]
                for part in range(1, wide // 128):
                    folded = folded + along[:, part * 128:(part + 1) * 128]
                vcol[place, at, :] += folded
                sc[q, own, cols] = (produced * gcol[place, at, 0:1]).astype(bf16)
                back = mm_nt(gg[place, at, :], wg[place, cols, :]) + mm_nt(gu[place, at, :], wu[place, cols, :])
                gc[q, own, cols] = back.astype(bf16)

    def combine(q):
        at = slice(q * rows, (q + 1) * rows)
        lane = lax.broadcasted_iota(jnp.int32, (rows, extra), 1)
        payload = []
        for place in range(count):
            expert = hosted[slots[place]]
            high, middle, low = split_three(jnp.sum(vcol[place, at, :], axis=1, keepdims=True))
            part = jnp.where(lane == expert, high.astype(f32), 0.0)
            part = jnp.where(lane == expert + experts, middle.astype(f32), part)
            part = jnp.where(lane == expert + 2 * experts, low.astype(f32), part)
            payload.append(part.astype(bf16))
        payload = jnp.concatenate(payload, axis=0) if count > 1 else payload[0]
        tail_sum = mm(dtmat[q], payload)
        if n_prev:
            tail_sum = tail_sum + nbuf[q, :, tail].astype(f32)
        nbuf[q, :, tail] = tail_sum.astype(bf16)

        @pl.loop(0, 2)
        def _(tile):
            cols = lanes(tile * wide, wide)
            back = mm(dtmat[q], gc[q, :, cols])
            out = mm(dtmat[q], sc[q, :, cols])
            if n_prev:
                back = back + nbuf[q, :, cols].astype(f32)
                out = out + cbuf[q, :, cols].astype(f32)
            nbuf[q, :, cols] = back.astype(bf16)
            cbuf[q, :, cols] = out.astype(bf16)

    def prev_copies(chunk):
        po0, po1, pg0, pg1 = prev
        return (
            pltpu.make_async_copy(pg0.at[chunk], nbuf.at[0], in_sem.at[0]),
            pltpu.make_async_copy(pg1.at[chunk], nbuf.at[1], in_sem.at[1]),
            pltpu.make_async_copy(po0.at[chunk], cbuf.at[0], in_sem.at[2]),
            pltpu.make_async_copy(po1.at[chunk], cbuf.at[1], in_sem.at[3]),
        )

    for copy in input_copies(0):
        copy.start()
    for copies in weight_copies:
        for copy in copies:
            copy.start()

    @pl.loop(0, chunks)
    def _(chunk):
        for copy in input_copies(0):
            copy.wait()
        for q in range(2):
            dispatch(q)
        if n_prev:
            for copy in prev_copies(chunk):
                copy.start()
        for place in range(count):
            @pl.when(chunk == 0)
            def _():
                for copy in weight_copies[place]:
                    copy.wait()

            forward_backward(place)
            for copy in act_copies(chunk, place):
                copy.start()
            produce(place)
        if n_prev:
            for copy in prev_copies(chunk):
                copy.wait()
        for q in range(2):
            combine(q)
        for copy in partial_copies(chunk):
            copy.start()
        for place in range(count):
            for copy in act_copies(chunk, place):
                copy.wait()
        for copy in partial_copies(chunk):
            copy.wait()

        for index in range(1, chunks):
            @pl.when(chunk + 1 == index)
            def _():
                for copy in input_copies(index):
                    copy.start()


def expert_call(hosted, slots, sources, weights, prev, saved, base, total, experts, rows, data, pieces, cost):
    chunks = len(sources)
    tokens, features = sources[0][2].shape
    ff = weights[0].shape[1] if slots[0] == 0 else weights[0].shape[1] // 2
    wide_n = sources[0][0].shape[1]
    extra = wide_n - features
    count = len(slots)
    shape = jax.ShapeDtypeStruct
    act_f = shape((count, total, features), bf16)
    act_h = shape((count, total, ff), bf16)
    out_shape = (
        [shape((chunks, tokens, features), bf16)] * 2
        + [shape((chunks, tokens, wide_n), bf16)] * 2
        + [act_f, act_f, act_h, act_h, act_h]
    )
    many = 2 * rows
    first_prev = 1 + 4 * chunks + len(weights)
    first_saved = first_prev + len(prev)
    return pl.pallas_call(
        functools.partial(
            expert_kernel, experts, slots, base, data, pieces, chunks, len(weights), len(prev), len(saved), rows),
        out_shape=out_shape,
        in_specs=specs("s" + "a" * (4 * chunks + len(weights) + len(prev) + len(saved))),
        out_specs=specs("a" * 9),
        input_output_aliases={
            **{first_prev + i: i for i in range(len(prev))},
            **{first_saved + i: 4 + i for i in range(len(saved))},
        },
        scratch_shapes=[
            pltpu.VMEM((count, features, ff), bf16),
            pltpu.VMEM((count, features, ff), bf16),
            pltpu.VMEM((count, ff, features), bf16),
            pltpu.VMEM((2, tokens, wide_n), bf16),
            pltpu.VMEM((2, tokens, features), bf16),
            pltpu.VMEM((count, many, features), bf16),
            pltpu.VMEM((count, many, features), bf16),
            pltpu.VMEM((2, count * rows, features), bf16),
            pltpu.VMEM((2, count * rows, features), bf16),
            pltpu.VMEM((count, many, ff), bf16),
            pltpu.VMEM((count, many, ff), bf16),
            pltpu.VMEM((count, many, ff), bf16),
            pltpu.VMEM((2, count * rows, tokens), bf16),
            pltpu.VMEM((2, tokens, count * rows), bf16),
            pltpu.VMEM((count, many, 128), f32),
            pltpu.VMEM((count, many, 128), f32),
            pltpu.VMEM((extra, tokens), f32),
            pltpu.SemaphoreType.DMA((count, 3 * max(1, len(pieces)))),
            pltpu.SemaphoreType.DMA((4,)),
            pltpu.SemaphoreType.DMA((count, 5)),
            pltpu.SemaphoreType.DMA((4,)),
        ],
        compiler_params=params(),
        cost_estimate=cost,
        name="expert_rows",
    )(hosted, *[v for group in sources for v in group], *weights, *prev, *saved)


def weight_gradient_kernel(data, x_in, gg_in, gu_in, h_in, gp_in, out, x, gg, gu, h, gp, wide, down, sem, out_sem):
    features, ff = x.shape[1], h.shape[1]
    loads = [
        pltpu.make_async_copy(source.at[0], target, sem.at[i])
        for i, (source, target) in enumerate(((gg_in, gg), (x_in, x), (gu_in, gu), (h_in, h), (gp_in, gp)))
    ]
    for copy in loads:
        copy.start()
    tall_f, tall_h = features // data, ff // data
    step = tall_f + tall_h
    stores = [
        pltpu.make_async_copy(wide.at[pl.ds(d * tall_f, tall_f)], out.at[pl.ds(d * step, tall_f)], out_sem.at[2 * d])
        for d in range(data)
    ] + [
        pltpu.make_async_copy(down.at[pl.ds(d * tall_h, tall_h)], out.at[pl.ds(d * step + tall_f, tall_h)],
                              out_sem.at[2 * d + 1])
        for d in range(data)
    ]
    for copy in loads[:3]:
        copy.wait()
    tall = 256

    @pl.loop(0, features // tall)
    def _(tile):
        cols = lanes(tile * tall, tall)
        at = pl.ds(pl.multiple_of(tile * tall, tall), tall)
        wide[at, :ff] = mm_tn(x[:, cols], gg[...]).astype(bf16)
        wide[at, ff:] = mm_tn(x[:, cols], gu[...]).astype(bf16)

    for copy in stores[:data]:
        copy.start()
    for copy in loads[3:]:
        copy.wait()

    @pl.loop(0, ff // tall)
    def _(tile):
        cols = lanes(tile * tall, tall)
        at = pl.ds(pl.multiple_of(tile * tall, tall), tall)
        down[at, :] = mm_tn(h[:, cols], gp[...]).astype(bf16)

    for copy in stores[data:]:
        copy.start()
    for copy in stores:
        copy.wait()


def weight_gradient_call(saved, data):
    x, gp, h, gg, gu = saved
    slots, features, ff = x.shape[1], x.shape[2], h.shape[2]
    return pl.pallas_call(
        functools.partial(weight_gradient_kernel, data),
        out_shape=jax.ShapeDtypeStruct((features + ff, 2 * ff), bf16),
        in_specs=specs("aaaaa"),
        out_specs=pl.BlockSpec(memory_space=pl.ANY),
        scratch_shapes=[
            pltpu.VMEM((slots, features), bf16),
            pltpu.VMEM((slots, ff), bf16),
            pltpu.VMEM((slots, ff), bf16),
            pltpu.VMEM((slots, ff), bf16),
            pltpu.VMEM((slots, features), bf16),
            pltpu.VMEM((features, 2 * ff), bf16),
            pltpu.VMEM((ff, features), bf16),
            pltpu.SemaphoreType.DMA((5,)),
            pltpu.SemaphoreType.DMA((2 * data,)),
        ],
        compiler_params=params(),
        cost_estimate=COST,
        name="expert_weight_gradients",
    )(x, gg, gu, h, gp)


epsilon = 1e-06
neg_fill = -1e30
QUERY_HEADS = 12
KEY_VALUE_HEADS = 2
HEAD_SIZE = 128
GROUP = QUERY_HEADS // KEY_VALUE_HEADS
SCORE_SCALE = HEAD_SIZE ** (-0.5)


def piece_copies(place, own, pieces, begin, weight, sem):
    rows, half = own[0].shape[0], weight.shape[1] // 2
    mine, core = place[0], place[1]
    copies = []
    column = 0
    for part in own:
        at = weight.at[pl.ds(pl.multiple_of(mine * rows, 16), rows), pl.ds(column, part.shape[1])]
        copies.append(pltpu.make_async_copy(part, at, sem.at[len(copies)]))
        column += part.shape[1]
    for (k, skip), pair in zip(((1, 0), (2, 0), (3, 0), (3, rows // 2)), pieces):
        first = pl.multiple_of(jnp.bitwise_xor(mine, k) * rows + skip, 16)
        for part, which in zip(pair, (core, 1 - core)):
            at = weight.at[pl.ds(first, part.shape[0]), lanes(which * half, half)]
            copies.append(pltpu.make_async_copy(part.at[:, pl.ds(begin, half)], at, sem.at[len(copies)]))
    return copies


def attention_mask(segment_row, segment_col, pad_row, first, size, span):
    row = first + lax.broadcasted_iota(jnp.int32, (size, span), 0)
    col = lax.broadcasted_iota(jnp.int32, (size, span), 1)
    same = segment_col[first:first + size, :] == segment_row[:, :span]
    return same & (((pad_row[:, :span] == 1) & (col < row)) | (col == row))


def stacked(ref, rows, c):
    return jnp.concatenate(
        [ref[rows, lanes((c * GROUP + g) * HEAD_SIZE, HEAD_SIZE)] for g in range(GROUP)], axis=0
    )


def attend_kernel(
    n_own, n_pairs, tokens_total, block,
    place, tokens, gain, segment_row, segment_col, pad_row, *refs,
):
    own = refs[:n_own]
    flat = refs[n_own:n_own + 2 * n_pairs]
    pieces = [(flat[2 * k], flat[2 * k + 1]) for k in range(n_pairs)]
    normed, qkv, mixture, totals, weight, sem = refs[n_own + 2 * n_pairs:]
    copies = piece_copies(place, own, pieces, 0, weight, sem)
    for copy in copies:
        copy.start()
    width = QUERY_HEADS * HEAD_SIZE
    kv_width = KEY_VALUE_HEADS * HEAD_SIZE
    source = tokens[...].astype(f32)
    inverse = lax.rsqrt(jnp.mean(source * source, axis=1, keepdims=True) + epsilon)
    normed[...] = (source * inverse * gain[...]).astype(bf16)
    for copy in copies:
        copy.wait()
    wide = 512

    @pl.loop(0, qkv.shape[1] // wide)
    def _(tile):
        cols = lanes(tile * wide, wide)
        qkv[:, cols] = mm(normed[...], weight[:, cols]).astype(bf16)

    totals[...] = jnp.zeros_like(totals)
    segment_of_row, segment_of_col, pad = segment_row[...], segment_col[...], pad_row[...]

    @pl.loop(0, KEY_VALUE_HEADS)
    def _(c):
        for first in range(0, tokens_total, block):
            span = first + block
            rows = slice(first, span)
            mask = attention_mask(segment_of_row, segment_of_col, pad, first, block, span)
            keys = qkv[:span, lanes(width + c * HEAD_SIZE, HEAD_SIZE)]
            values = qkv[:span, lanes(width + kv_width + c * HEAD_SIZE, HEAD_SIZE)]
            scores = mm_nt(stacked(qkv, rows, c), keys) * SCORE_SCALE
            lane = lax.broadcasted_iota(jnp.int32, (block, 128), 1)
            stats = totals[rows, :]
            weights = []
            for g in range(GROUP):
                part = jnp.where(mask, scores[g * block:(g + 1) * block], neg_fill)
                top = jnp.max(part, axis=1, keepdims=True)
                raised = jnp.exp(part - top)
                total = jnp.sum(raised, axis=1, keepdims=True)
                stats = jnp.where(lane == c * GROUP + g, top + jnp.log(total), stats)
                weights.append((raised * (1.0 / total)).astype(bf16))
            totals[rows, :] = stats
            mixed = mm(jnp.concatenate(weights, axis=0), values).astype(bf16)
            for g in range(GROUP):
                mixture[rows, lanes((c * GROUP + g) * HEAD_SIZE, HEAD_SIZE)] = mixed[g * block:(g + 1) * block]


def attend_call(place, tokens, gain, segments, pads, own, pieces):
    rows, features = tokens.shape
    width = (QUERY_HEADS + 2 * KEY_VALUE_HEADS) * HEAD_SIZE
    mixed = QUERY_HEADS * HEAD_SIZE
    flat = [part for pair in pieces for part in pair]
    shape = jax.ShapeDtypeStruct
    return pl.pallas_call(
        functools.partial(attend_kernel, len(own), len(pieces), rows, 128),
        out_shape=[
            shape((rows, features), bf16), shape((rows, width), bf16), shape((rows, mixed), bf16),
            shape((rows, 128), f32),
        ],
        in_specs=specs("s" + "v" * 5 + "a" * (len(own) + len(flat))),
        out_specs=specs("vvvv"),
        scratch_shapes=[
            pltpu.VMEM((features, width), bf16),
            pltpu.SemaphoreType.DMA((len(own) + len(flat),)),
        ],
        compiler_params=params(),
        cost_estimate=COST,
        name="attend",
    )(place, tokens, gain, segments, segments.reshape(rows, 1), pads, *own, *flat)


def attend_back_kernel(tokens_total, block, segment_row, segment_col, pad_row, qkv, totals, given, normed,
                       grad, local, grad_keys, grad_values):
    width = QUERY_HEADS * HEAD_SIZE
    kv_width = KEY_VALUE_HEADS * HEAD_SIZE
    segment_of_row, segment_of_col, pad = segment_row[...], segment_col[...], pad_row[...]

    @pl.loop(0, KEY_VALUE_HEADS)
    def _(c):
        grad_keys[...] = jnp.zeros_like(grad_keys)
        grad_values[...] = jnp.zeros_like(grad_values)
        for first in range(0, tokens_total, block):
            span = first + block
            rows = slice(first, span)
            mask = attention_mask(segment_of_row, segment_of_col, pad, first, block, span)
            keys = qkv[:span, lanes(width + c * HEAD_SIZE, HEAD_SIZE)]
            values = qkv[:span, lanes(width + kv_width + c * HEAD_SIZE, HEAD_SIZE)]
            queries = stacked(qkv, rows, c)
            arrived = stacked(given, rows, c)
            scores = mm_nt(queries, keys) * SCORE_SCALE
            grad_weights = mm_nt(arrived, values)
            lane = lax.broadcasted_iota(jnp.int32, (block, 128), 1)
            stats = totals[rows, :]
            weights, grad_scores = [], []
            for g in range(GROUP):
                at = slice(g * block, (g + 1) * block)
                total = jnp.sum(jnp.where(lane == c * GROUP + g, stats, 0.0), axis=1, keepdims=True)
                probs = jnp.exp(jnp.where(mask, scores[at], neg_fill) - total)
                weights.append(probs.astype(bf16))
                dw = grad_weights[at]
                mean = jnp.sum(probs * dw, axis=1, keepdims=True)
                grad_scores.append((probs * (dw - mean)).astype(bf16))
            weights = jnp.concatenate(weights, axis=0)
            grad_scores = jnp.concatenate(grad_scores, axis=0)
            grad_queries = (mm(grad_scores, keys) * SCORE_SCALE).astype(bf16)
            for g in range(GROUP):
                grad[rows, lanes((c * GROUP + g) * HEAD_SIZE, HEAD_SIZE)] = grad_queries[g * block:(g + 1) * block]
            grad_keys[:span, :] += mm_tn(grad_scores, queries)
            grad_values[:span, :] += mm_tn(weights, arrived)
        grad[:, lanes(width + c * HEAD_SIZE, HEAD_SIZE)] = (grad_keys[...] * SCORE_SCALE).astype(bf16)
        grad[:, lanes(width + kv_width + c * HEAD_SIZE, HEAD_SIZE)] = grad_values[...].astype(bf16)

    tall = 256

    @pl.loop(0, normed.shape[1] // tall)
    def _(tile):
        cols = lanes(tile * tall, tall)
        local[pl.ds(pl.multiple_of(tile * tall, tall), tall), :] = mm_tn(normed[:, cols], grad[...]).astype(bf16)


def attend_back_call(segments, pads, qkv, totals, given, normed):
    rows, width = qkv.shape
    features = normed.shape[1]
    shape = jax.ShapeDtypeStruct
    return pl.pallas_call(
        functools.partial(attend_back_kernel, rows, 128),
        out_shape=[shape((rows, width), bf16), shape((features, width), bf16)],
        in_specs=specs("v" * 7),
        out_specs=specs("vv"),
        scratch_shapes=[pltpu.VMEM((rows, HEAD_SIZE), f32), pltpu.VMEM((rows, HEAD_SIZE), f32)],
        compiler_params=params(),
        cost_estimate=COST,
        name="attend_back",
    )(segments, segments.reshape(rows, 1), pads, qkv, totals, given, normed)


def route_kernel(experts, n_own, n_pairs, place, mixture, tokens, gain, router_weight, slots, *refs):
    own = refs[:n_own]
    flat = refs[n_own:n_own + 2 * n_pairs]
    pieces = [(flat[2 * k], flat[2 * k + 1]) for k in range(n_pairs)]
    hidden, payload, weight, sem = refs[n_own + 2 * n_pairs:]
    copies = piece_copies(place, own, pieces, (QUERY_HEADS + 2 * KEY_VALUE_HEADS) * HEAD_SIZE // 2, weight, sem)
    for copy in copies:
        copy.start()
    for copy in copies:
        copy.wait()
    features = tokens.shape[1]
    wide = features // 2

    @pl.loop(0, 2)
    def _(tile):
        cols = lanes(tile * wide, wide)
        hidden[:, cols] = tokens[:, cols].astype(f32) + mm(mixture[...], weight[:, cols])

    value = hidden[...]
    inverse = lax.rsqrt(jnp.mean(value * value, axis=1, keepdims=True) + epsilon)
    payload[:, :features] = (value * inverse * gain[...]).astype(bf16)
    extra = payload.shape[1] - features
    logits = mm(payload[:, :features], router_weight[...])
    lane = lax.broadcasted_iota(jnp.int32, logits.shape, 1)
    logits = jnp.where(lane < experts, logits, neg_fill)
    raised = jnp.exp(logits - jnp.max(logits, axis=1, keepdims=True))
    router = raised / jnp.sum(raised, axis=1, keepdims=True)
    high, middle, low = split_three(router)
    tail = high.astype(f32)
    tail = tail + pltpu.roll(middle.astype(f32), experts, 1)
    tail = tail + pltpu.roll(low.astype(f32), 2 * experts, 1)
    payload[:, features:] = (tail + slots[...]).astype(bf16)


def tail_width(experts):
    return (5 * experts + 127) // 128 * 128


def route_call(place, mixture, tokens, gain, router_weight, slots, own, pieces, experts):
    rows, features = tokens.shape
    extra = tail_width(experts)
    flat = [part for pair in pieces for part in pair]
    shape = jax.ShapeDtypeStruct
    return pl.pallas_call(
        functools.partial(route_kernel, experts, len(own), len(pieces)),
        out_shape=[shape((rows, features), f32), shape((rows, features + extra), bf16)],
        in_specs=specs("s" + "v" * 5 + "a" * (len(own) + len(flat))),
        out_specs=specs("vv"),
        scratch_shapes=[
            pltpu.VMEM((mixture.shape[1], features), bf16),
            pltpu.SemaphoreType.DMA((len(own) + len(flat),)),
        ],
        compiler_params=params(),
        cost_estimate=COST,
        name="route",
    )(place, mixture, tokens, gain, router_weight, slots, *own, *flat)


def branch_kernel(experts, n_back, n_own, n_pairs, place, cotangent, hidden, payload, gain, router_weight,
                  mixture, *refs):
    backs, refs = refs[:n_back], refs[n_back:]
    own = refs[:n_own]
    flat = refs[n_own:n_own + 2 * n_pairs]
    pieces = [(flat[2 * k], flat[2 * k + 1]) for k in range(n_pairs)]
    grad_hidden, given, local_out, local_gain, local_router, weight, branch, sem = refs[n_own + 2 * n_pairs:]
    copies = piece_copies(place, own, pieces, (QUERY_HEADS + 2 * KEY_VALUE_HEADS) * HEAD_SIZE // 2, weight, sem)
    for copy in copies:
        copy.start()
    rows, features = cotangent.shape
    extra = payload.shape[1] - features

    def arrived(cols):
        total = backs[0][:, cols].astype(f32)
        for ref in backs[1:]:
            total = total + ref[:, cols].astype(f32)
        return total

    def three(value):
        width = value.shape[1]
        return (value + pltpu.roll(value, width - experts, 1)
                + pltpu.roll(value, width - 2 * experts, 1))

    lane = lax.broadcasted_iota(jnp.int32, (rows, extra), 1)
    router = jnp.where(lane < experts, three(payload[:, features:].astype(f32)), 0.0)
    select = jnp.where(lane < experts, three(arrived(slice(features, features + extra))), 0.0)
    logits = router * (select - jnp.sum(router * select, axis=1, keepdims=True))
    high, middle, low = split_three(logits)
    packed = high.astype(f32) + pltpu.roll(middle.astype(f32), experts, 1)
    packed = (packed + pltpu.roll(low.astype(f32), 2 * experts, 1)).astype(bf16)
    grad_normed = arrived(slice(0, features)) + mm_nt(packed, router_weight[...])
    local_router[...] = mm_tn(packed, payload[:, :features])
    value = hidden[...]
    inverse = lax.rsqrt(jnp.mean(value * value, axis=1, keepdims=True) + epsilon)
    along = grad_normed * value
    local_gain[...] = jnp.sum(along * inverse, axis=0, keepdims=True)
    mean = jnp.mean(along * gain[...], axis=1, keepdims=True)
    total = cotangent[...].astype(f32) + inverse * (grad_normed * gain[...]) - value * (inverse * inverse * inverse * mean)
    grad_hidden[...] = total
    branch[...] = total.astype(bf16)
    tall = 256

    @pl.loop(0, mixture.shape[1] // tall)
    def _(tile):
        cols = lanes(tile * tall, tall)
        local_out[pl.ds(pl.multiple_of(tile * tall, tall), tall), :] = mm_tn(mixture[:, cols], branch[...]).astype(bf16)

    for copy in copies:
        copy.wait()
    wide = mixture.shape[1] // 2

    @pl.loop(0, 2)
    def _(tile):
        at = pl.ds(pl.multiple_of(tile * wide, 128), wide)
        given[:, lanes(tile * wide, wide)] = mm_nt(branch[...], weight[at, :]).astype(bf16)


def branch_call(place, cotangent, hidden, payload, gain, router_weight, mixture, backs, own, pieces, experts):
    rows, features = cotangent.shape
    extra = payload.shape[1] - features
    mixed = mixture.shape[1]
    flat = [part for pair in pieces for part in pair]
    shape = jax.ShapeDtypeStruct
    return pl.pallas_call(
        functools.partial(branch_kernel, experts, len(backs), len(own), len(pieces)),
        out_shape=[
            shape((rows, features), f32), shape((rows, mixed), bf16), shape((mixed, features), bf16),
            shape((1, features), f32), shape((extra, features), f32),
        ],
        in_specs=specs("s" + "v" * (6 + len(backs)) + "a" * (len(own) + len(flat))),
        out_specs=specs("vvvvv"),
        scratch_shapes=[
            pltpu.VMEM((mixed, features), bf16),
            pltpu.VMEM((rows, features), bf16),
            pltpu.SemaphoreType.DMA((len(own) + len(flat),)),
        ],
        compiler_params=params(),
        cost_estimate=COST,
        name="branch",
    )(place, cotangent, hidden, payload, gain, router_weight, mixture, *backs, *own, *flat)


def input_grad_kernel(n_own, n_pairs, place, tokens, gain, grad, grad_hidden, *refs):
    own = refs[:n_own]
    flat = refs[n_own:n_own + 2 * n_pairs]
    pieces = [(flat[2 * k], flat[2 * k + 1]) for k in range(n_pairs)]
    out, local_gain, weight, normed_grad, sem = refs[n_own + 2 * n_pairs:]
    copies = piece_copies(place, own, pieces, 0, weight, sem)
    for copy in copies:
        copy.start()
    for copy in copies:
        copy.wait()
    features = tokens.shape[1]
    wide = features // 2

    @pl.loop(0, 2)
    def _(tile):
        at = pl.ds(pl.multiple_of(tile * wide, 128), wide)
        normed_grad[:, lanes(tile * wide, wide)] = mm_nt(grad[...], weight[at, :])

    value = tokens[...].astype(f32)
    inverse = lax.rsqrt(jnp.mean(value * value, axis=1, keepdims=True) + epsilon)
    grad_normed = normed_grad[...]
    along = grad_normed * value
    local_gain[...] = jnp.sum(along * inverse, axis=0, keepdims=True)
    mean = jnp.mean(along * gain[...], axis=1, keepdims=True)
    out[...] = grad_hidden[...] + inverse * (grad_normed * gain[...]) - value * (inverse * inverse * inverse * mean)


def input_grad_call(place, tokens, gain, grad, grad_hidden, own, pieces):
    rows, features = tokens.shape
    flat = [part for pair in pieces for part in pair]
    shape = jax.ShapeDtypeStruct
    return pl.pallas_call(
        functools.partial(input_grad_kernel, len(own), len(pieces)),
        out_shape=[shape((rows, features), f32), shape((1, features), f32)],
        in_specs=specs("s" + "v" * 4 + "a" * (len(own) + len(flat))),
        out_specs=specs("vv"),
        scratch_shapes=[
            pltpu.VMEM((features, grad.shape[1]), bf16),
            pltpu.VMEM((rows, features), f32),
            pltpu.SemaphoreType.DMA((len(own) + len(flat),)),
        ],
        compiler_params=params(),
        cost_estimate=COST,
        name="input_grad",
    )(place, tokens, gain, grad, grad_hidden, *own, *flat)


def pair_slots(routes, order_row, experts, capacity):
    pair_count = order_row.shape[0]
    place = (
        jnp.zeros((pair_count,), jnp.int32)
        .at[order_row]
        .set(jnp.arange(pair_count, dtype=jnp.int32), unique_indices=True, mode="promise_in_bounds")
        .reshape(routes.shape)
    )
    columns = jnp.arange(experts, dtype=jnp.int32)
    hit = routes[None, :, :] == columns[:, None, None]
    key = jnp.min(jnp.where(hit, place[None], pair_count), axis=2)
    rank = jnp.sum((key[:, None, :] < key[:, :, None]).astype(jnp.int32), axis=2)
    return jnp.where((key < pair_count) & (rank < capacity), rank + 1, 0).T


def body(
    tokens,
    cotangent,
    norm_attn,
    norm_moe,
    w_query,
    key_weight,
    value_weight,
    w_out,
    w_router,
    w_gate,
    w_up,
    w_down,
    document_index,
    padding_token_mask,
    routes,
    pair_order,
):
    token_rows, features = tokens.shape
    top_count = routes.shape[1]
    experts = lax.axis_size("expert")
    data = lax.axis_size("dp")
    chips = experts // 2
    half = chips // 2
    ff = w_gate.shape[2]
    capacity = 9 * token_rows * top_count // (8 * experts)
    slot_rows = (capacity + 15) // 16 * 16
    extra = tail_width(experts)
    query_width = QUERY_HEADS * HEAD_SIZE
    kv_width = KEY_VALUE_HEADS * HEAD_SIZE
    me = lax.axis_index("expert")
    my_dp = lax.axis_index("dp")
    core = lax.rem(me, 2)
    place = jnp.stack([my_dp, core]).astype(jnp.int32)
    hosted = jnp.stack([me, lax.rem(me + experts // 2, experts), my_dp]).astype(jnp.int32)

    def swap(v):
        return lax.ppermute(v, "expert", [(j, j ^ 1) for j in range(experts)])

    def shift(v, k):
        def to(j):
            chip = j // 2
            return ((chip // half) * half + (chip % half + k) % half) * 2 + j % 2

        return lax.ppermute(v, "expert", [(j, to(j)) for j in range(experts)])

    def across(v):
        return lax.ppermute(v, "expert", [(j, (j + experts // 2) % experts) for j in range(experts)])

    def chip_xor(v, step):
        return lax.ppermute(v, "expert", [(j, ((j // 2) ^ step) * 2 + j % 2) for j in range(experts)])

    def dp_xor(v, k):
        return lax.ppermute(v, "dp", [(j, j ^ k) for j in range(data)])

    def core_half(v):
        width = v.shape[1] // 2
        return jnp.where(core == 0, v[:, :width], v[:, width:])

    def after(v, *others):
        return lax.optimization_barrier((v, others))[0]

    def from_dp(v):
        return [dp_xor(v, k) for k in range(1, data)]

    def dp_part(w):
        rows = w.shape[0] // data
        return lax.dynamic_slice_in_dim(w, my_dp * rows, rows, axis=0)

    own = [w_gate[0], w_up[0], w_down[0]]
    quarter = jnp.concatenate(
        [jnp.concatenate([dp_part(own[0]), dp_part(own[1])], axis=1), dp_part(own[2])], axis=0
    )
    part_rows = quarter.shape[0] // 2
    crossed_one = across(quarter[:part_rows])

    cot_far_same = [shift(cotangent, k) for k in range(1, half)]

    qkv_own = [w_query, key_weight, value_weight]
    qkv_half = (query_width + 2 * kv_width) // 2
    mine = jnp.concatenate([core_half(jnp.concatenate(qkv_own, axis=1)), core_half(w_out)], axis=1)
    near_one, near_two = dp_xor(mine, 1), dp_xor(mine, 2)
    tall = mine.shape[0] // 2
    got = [near_one, near_two, dp_xor(near_two[:tall], 1), dp_xor(near_one[tall:], 2)]
    slots = pair_slots(routes, pair_order[0], experts, capacity)
    slot_columns = jnp.pad(
        jnp.concatenate([slots // 128, slots % 128], axis=1).astype(f32),
        ((0, 0), (3 * experts, extra - 5 * experts)),
    )
    router_weight = jnp.pad(w_router, ((0, 0), (0, extra - experts)))
    router_weight_three = jnp.pad(jnp.concatenate([w_router] * 3, axis=1), ((0, 0), (0, extra - 3 * experts)))
    ready = after(got, crossed_one, cot_far_same, slot_columns, router_weight, router_weight_three)
    pieces = [(v, swap(v)) for v in ready]
    crossed_two = across(after(quarter[part_rows:], crossed_one))
    cot_other = swap(after(cotangent, pieces))
    cot_far_other = [swap(after(v, pieces)) for v in cot_far_same]
    partner_one = lax.all_gather(after(crossed_one, pieces), "dp", axis=0, tiled=True)

    gain_one = norm_attn.reshape(1, features)
    gain_two = norm_moe.reshape(1, features)

    normed_one, qkv, mixture, totals = attend_call(
        place, tokens, gain_one, document_index, padding_token_mask, qkv_own, pieces
    )
    hidden_one, payload = route_call(
        place, after(mixture, crossed_two, cot_other, cot_far_other), tokens, gain_two, router_weight,
        slot_columns, [w_out], pieces, experts,
    )

    payload_far_same = [shift(payload, k) for k in range(1, half)]
    payload_other = swap(payload)
    total_rows = chips // 2 * 2 * slot_rows

    two = after(crossed_two, payload_other)
    partner = [partner_one, two] + from_dp(two)
    spread = tuple((0, d * part_rows, part_rows, (False, d), 0) for d in range(data))
    spread += tuple((1 + k, 0, part_rows, (True, k), part_rows) for k in range(data))

    def rows_of(slot, sources, weights, prev, saved, base, cost=COST):
        return expert_call(
            hosted, (slot,), sources, weights, prev, saved, base, total_rows, experts, slot_rows, data, spread, cost
        )

    one = [(payload, payload_other, cotangent, cot_other)]
    near = rows_of(0, one, own, [], [], 0)
    near_saved = near[4:]
    near = rows_of(1, one, partner, near[:4], [], 0, LONG)
    payload_far_other = [swap(after(v, near[0])) for v in payload_far_same]
    many = list(zip(payload_far_same, payload_far_other, cot_far_same, cot_far_other))
    far = rows_of(1, many, partner, [], near[4:], 2 * slot_rows)
    partner_local = weight_gradient_call(far[4:], data)
    far = rows_of(0, many, own, far[:4], near_saved, 2 * slot_rows)
    saved = far[4:]

    def returned(near_same, near_other, far_same, far_other):
        sums = [
            (far_same[k].astype(f32) + swap(far_other[k]).astype(f32)).astype(bf16)
            for k in range(half - 1)
        ]
        return [near_same[0], swap(near_other[0])], sums

    def scattered(v):
        return lax.psum_scatter(v, "dp", scatter_dimension=0, tiled=True)

    partner_sum = scattered(partner_local)
    backs, back_sums = returned(near[2], near[3], far[2], far[3])
    backs += [shift(v, half - 1 - k) for k, v in enumerate(back_sums)]
    own_local = weight_gradient_call([after(saved[0], back_sums), *saved[1:]], data)
    own_sum = scattered(after(own_local, partner_sum, backs))
    grad_hidden, given, local_out, local_norm_moe, local_router = branch_call(
        place, cotangent, hidden_one, payload, gain_two, router_weight_three, mixture, backs,
        [w_out], pieces, experts,
    )

    def halved(v):
        width = v.shape[1] // 2
        keep = core_half(v)
        give = jnp.where(core == 0, v[:, width:], v[:, :width])
        return (keep.astype(f32) + swap(give).astype(f32)).astype(bf16)

    def fold(sides, stage, *others):
        done = []
        for side, order in zip(sides, ((0, 1), (1, 0))):
            axis = order[stage]
            bit, step = ((my_dp // 2, 2), (lax.rem(my_dp, 2), 1))[axis]
            keep = lax.dynamic_index_in_dim(side, bit, axis, keepdims=True)
            give = lax.dynamic_index_in_dim(side, 1 - bit, axis, keepdims=True)
            done.append((keep.astype(f32) + after(dp_xor(give, step), *others).astype(f32)).astype(bf16))
        return done

    def sides_of(part):
        rows, quart = part.shape[0] // data, part.shape[1] // 2
        return [v.reshape(2, 2, rows, quart) for v in (part[:, :quart], part[:, quart:])]

    def chip_sum(part):
        sizes = []
        step = 1
        chip = me // 2
        while step < chips:
            size = part.shape[0] // 2
            bit = lax.rem(chip // step, 2)
            keep = lax.dynamic_slice_in_dim(part, bit * size, size, axis=0)
            give = lax.dynamic_slice_in_dim(part, (1 - bit) * size, size, axis=0)
            part = (keep.astype(f32) + chip_xor(give, step).astype(f32)).astype(bf16)
            sizes.append((step, bit))
            step *= 2
        for step, bit in reversed(sizes):
            other = chip_xor(part, step)
            part = jnp.concatenate(
                [jnp.where(bit == 0, part, other), jnp.where(bit == 0, other, part)], axis=0
            )
        return part

    def joined(part):
        other = swap(part)
        first = jnp.where(core == 0, part, other)
        second = jnp.where(core == 0, other, part)
        return first, second

    thirds = jnp.split(partner_sum, 3, axis=0)
    arrived_one = across(after(thirds[0], backs))
    arrived_two = across(after(thirds[1], arrived_one))
    given, local_out = after((given, local_out), arrived_one)
    out_half = halved(local_out)
    outs, out_sums = returned(near[0], near[1], far[0], far[1])
    half_rows = token_rows // 2
    outs_one = [shift(after(v[:half_rows], arrived_one), half - 1 - k) for k, v in enumerate(out_sums)]
    grad_qkv, local_qkv = attend_back_call(
        document_index, padding_token_mask, qkv, totals, given, normed_one
    )
    local_qkv = after(local_qkv, arrived_two, outs_one)
    arrived_three = across(after(thirds[2], arrived_two))
    outs_two = [shift(after(v[half_rows:], outs_one), half - 1 - k) for k, v in enumerate(out_sums)]
    sides = sides_of(jnp.concatenate([out_half, halved(local_qkv)], axis=1))
    grad_tokens, local_norm_attn = input_grad_call(
        place, tokens, gain_one, grad_qkv, grad_hidden, qkv_own, pieces
    )
    sides = fold(sides, 0, grad_tokens)
    arrived_three = after(arrived_three, sides)
    arrived = jnp.concatenate([arrived_one, arrived_two, arrived_three], axis=0)
    expert_sum = (own_sum.astype(f32) + arrived.astype(f32)).astype(bf16)
    whole = lax.all_gather(expert_sum, "dp", axis=0, tiled=True).reshape(data, -1, 2 * ff)
    tall = features // data
    grad_gate = whole[:, :tall, :ff].reshape(1, features, ff).astype(f32)
    grad_up = whole[:, :tall, ff:].reshape(1, features, ff).astype(f32)
    grad_down = whole[:, tall:, :].reshape(1, ff, features).astype(f32)
    outs_two = after(outs_two, grad_tokens)
    sides = fold(sides, 1, outs_two)
    outs += [jnp.concatenate([one, two], axis=0) for one, two in zip(outs_one, outs_two)]
    rows = features // data
    part = jnp.concatenate([v.reshape(rows, -1) for v in sides], axis=1)
    local_norm_attn = after(local_norm_attn, part)
    first, second = joined(chip_sum(part))
    out_half = features // 2
    grad_out = jnp.concatenate([first[:, :out_half], second[:, :out_half]], axis=1).astype(f32)
    first, second = first[:, out_half:].astype(f32), second[:, out_half:].astype(f32)
    kept = query_width - qkv_half
    grad_query = jnp.concatenate([first, second[:, :kept]], axis=1)
    grad_key = second[:, kept:kept + kv_width]
    grad_value = second[:, kept + kv_width:]

    routed = outs[0].astype(f32)
    for part in outs[1:]:
        routed = routed + part.astype(f32)
    block_out = (hidden_one + routed).astype(bf16)

    local_router = local_router[:3 * experts].reshape(3, experts, features).sum(0)
    small = jnp.concatenate([local_router, local_norm_attn, local_norm_moe], axis=0)
    small = small + swap(small)
    for step in range(data.bit_length() - 1):
        small = small + dp_xor(small, 1 << step)
    step = 1
    while step < chips:
        small = small + chip_xor(small, step)
        step *= 2
    grad_router = small[:experts].T
    grad_norm_attn = small[experts]
    grad_norm_moe = small[experts + 1]
    return (
        block_out,
        grad_tokens,
        grad_norm_attn,
        grad_norm_moe,
        grad_query,
        grad_key,
        grad_value,
        grad_out,
        grad_router,
        grad_gate,
        grad_up,
        grad_down,
    )


def solution(mesh):
    rows = P(("dp", "expert"), None)
    over_dp = P("dp", None)
    over_expert = P("expert", None, None)
    return jax.shard_map(
        body,
        mesh=mesh,
        in_specs=(
            rows, rows, P(), P(), over_dp, over_dp, over_dp, over_dp, P(),
            over_expert, over_expert, over_expert, rows, rows, rows, rows,
        ),
        out_specs=(
            rows, rows, P(), P(), over_dp, over_dp, over_dp, over_dp, P(),
            over_expert, over_expert, over_expert,
        ),
        check_vma=False,
    )
```

time: 1740 us -> 645 us (0.37)
  other arithmetic: 479 us -> 57.3 us
  local copies, waits for them, and re-layouts: 402 us -> 42.9 us
  waiting for transfers between devices: 509 us -> 228 us
  Pallas kernels: 0 us -> 254 us
  matrix products: 231 us -> 0 us
  blocking collectives: 75 us -> 0 us
  starting transfers between devices: 21.5 us -> 42.9 us
    unnamed x9 -> x2, other arithmetic: 377 us -> 0.01 us
    all_to_all x4 -> x0, waiting for transfers between devices: 366 us -> none  [the longest x1 170 us: body(): lax.all_to_all(grad_produced, 'expert', split_axis=0, concat_axis=1, tile...]
    pallas_call x0 -> x11, Pallas kernels: none -> 254 us  [the longest x4 126 us: expert_call(): pl.pallas_call(functools.partial(expert_kernel, experts, slots, base, dat...]
    dot_general x30 -> x0, matrix products: 231 us -> none  [the longest x1 18.8 us: body(): jnp.einsum('erd,efd->erf', grad_arrived, w_down, preferred_element_type=j...]
    ppermute x0 -> x45, waiting for transfers between devices: none -> 228 us  [the longest x5 60.3 us: across(): lax.ppermute(v, 'expert', [(j, (j + experts // 2) % experts) for j in ran...]
    convert_element_type x6 -> x1, local copies, waits for them, and re-layouts: 146 us -> 0.9 us  [body(): jnp.concatenate([slots // 128, slots % 128], axis=1).astype(f32)]
    gather x7 -> x0, local copies, waits for them, and re-layouts: 128 us -> none  [the longest x1 21 us: body(): returned_rows[pair_slot].reshape(token_rows, top_count, features)]
    reduce_scatter x4 -> x2, waiting for transfers between devices: 118 us -> 0.01 us  [scattered(): return lax.psum_scatter(v, 'dp', scatter_dimension=0, tiled=True)]
  transfers between devices with their start and end apart: 12 -> 49, of which waited for: 6 -> 26; matrix products, arithmetic and copies ran while one was open for 45% -> 12% of each run, Pallas kernels for 0% -> 32%
where the time goes in v2:
time: 645 us; the launch traced here: 640 us
  Pallas kernels  254 us (39%)
  waiting for transfers between devices  228 us (35%)
  other arithmetic  57.3 us (9%)
  local copies, waits for them, and re-layouts  42.9 us (7%)
  starting transfers between devices  42.9 us (7%)
  between operations  14.7 us (2%)
    pallas_call x4, Pallas kernels, expert_call(): pl.pallas_call(functools.partial(expert_kernel, experts, slots, base, dat...  126 us
    ppermute x5, waiting for transfers between devices, across(): lax.ppermute(v, 'expert', [(j, (j + experts // 2) % experts) for j in ran...  60.3 us
    ppermute x5, waiting for transfers between devices, shift(): return lax.ppermute(v, 'expert', [(j, to(j)) for j in range(experts)])  50.5 us
    ppermute x13, waiting for transfers between devices, dp_xor(): return lax.ppermute(v, 'dp', [(j, j ^ k) for j in range(data)])  46.8 us
    ppermute x6, waiting for transfers between devices, chip_xor(): lax.ppermute(v, 'expert', [(j, (j // 2 ^ step) * 2 + j % 2) for j in rang...  44.3 us
    pallas_call x2, Pallas kernels, weight_gradient_call(): pl.pallas_call(functools.partial(weight_gradient_kernel, data), out_shape...  36 us
    ppermute x16, waiting for transfers between devices, swap(): return lax.ppermute(v, 'expert', [(j, j ^ 1) for j in range(experts)])  26.2 us
    pallas_call x1, Pallas kernels, attend_back_call(): pl.pallas_call(functools.partial(attend_back_kernel, rows, 128), out_shap...  25 us
  transfers between devices with their start and end apart: 49, of which 26 were waited for; matrix products, arithmetic and copies ran while one was open for 12% of the time, Pallas kernels for 32%

profile of v2, /device:TPU:0, one launch (start us, length us, event | category | flops | bytes accessed | tf_op | source)
XLA Modules:
  0.0 640.4 jit_solution(15431284765116655944)
XLA Ops:
  23.7 9.9 %scatter_custom_fusion = s32[2560]{0:T(1024)S(1)} fusion(s32[2560]{0:T(1024)S(1)} %fusion.13, s32[2560]{0:T(1024)S(1)} %iota.7, s32[]{:T(128)} %constant.119.clone.1), kind=kCustom, calls=%fused_computation.79 | custom fusion | bytes 10244 | tf_op jit(solution)/shard_map/scatter | solution.py:774
  34.1 10.4 %collective-permute-done.1.refs_5_.refs_3_.refs_6_ = bf16[384,1792]{1,0:T(8,128)(2,1)S(1)} collective-permute-done((bf16[384,1792]{1,0:T(8,128)(2,1)}, bf16[384,1792]{1,0:T(8,128)(2,1)S(1)}, u32[]{:S(2)}, u32[]{:S(2)}) %collective-permute-start.1) | collective-permute-done | bytes 1376288 | tf_op jit(solution)/shard_map/ppermute | solution.py:837
  59.9 18.1 %collective-permute-done.4 = bf16[288,1536]{1,0:T(8,128)(2,1)} collective-permute-done((bf16[288,1536]{1,0:T(8,128)(2,1)}, bf16[288,1536]{1,0:T(8,128)(2,1)}, u32[]{:S(2)}, u32[]{:S(2)}) %collective-permute-start.4) | collective-permute-done | bytes 884768 | tf_op jit(solution)/shard_map/ppermute | solution.py:831
  95.0 18.8 %attend.1 = (bf16[640,1536]{1,0:T(8,128)(2,1)}, bf16[640,2048]{1,0:T(8,128)(2,1)}, bf16[640,1536]{1,0:T(8,128)(2,1)}, f32[640,128]{1,0:T(8,128)}) custom-call(s32[2]{0:T(128)} %pad_add_fusion.place, bf16[640,1536]{1,0:T(8,128)(2,1)} %tokens.5, f32[1,1536]{1,0:T(1,128)} %reshape.138.gain, s32[1,640]{1,0:T(1,128)} %segment_row.3, s32[640,1]{1,0:T(8,128)} %copy.78.segment_col, ...), custom_call_target="tpu_custom_call" | custom-call | flops 1000 | bytes 1000 | tf_op jit(solution)/shard_map/attend/pallas_call | solution.py:498
  113.8 17.1 %collective-permute-done.10.refs_6_ = bf16[288,1536]{1,0:T(8,128)(2,1)} collective-permute-done((bf16[288,1536]{1,0:T(8,128)(2,1)}, bf16[288,1536]{1,0:T(8,128)(2,1)}, u32[]{:S(2)}, u32[]{:S(2)}) %collective-permute-start.10) | collective-permute-done | bytes 884768 | tf_op jit(solution)/shard_map/ppermute | solution.py:831
  131.0 11.9 %route.1 = (f32[640,1536]{1,0:T(8,128)}, bf16[640,1664]{1,0:T(8,128)(2,1)}) custom-call(s32[2]{0:T(128)} %pad_add_fusion.place, bf16[640,1536]{1,0:T(8,128)(2,1)} %get-tuple-element.99.mixture, bf16[640,1536]{1,0:T(8,128)(2,1)} %tokens.5, f32[1,1536]{1,0:T(1,128)} %reshape.140.gain, bf16[1536,128]{1,0:T(8,128)(2,1)} %pad.13.router_weight, ...), custom_call_target="tpu_custom_call" | custom-call | flops 1000 | bytes 1000 | tf_op jit(solution)/shard_map/route/pallas_call | solution.py:624
  152.0 31.3 %expert_rows.4 = (bf16[1,640,1536]{2,1,0:T(8,128)(2,1)}, bf16[1,640,1536]{2,1,0:T(8,128)(2,1)}, bf16[1,640,1664]{2,1,0:T(8,128)(2,1)}, bf16[1,640,1664]{2,1,0:T(...) custom-call(s32[3]{0:T(128)} %pad_add_fusion.1.refs_0_, ...), custom_call_target="tpu_custom_call" | custom-call | flops 1000 | bytes 1000 | tf_op jit(solution)/shard_map/expert_rows/pallas_call | solution.py:290
  188.6 31.9 %expert_rows.5 = (bf16[1,640,1536]{2,1,0:T(8,128)(2,1)}, bf16[1,640,1536]{2,1,0:T(8,128)(2,1)}, bf16[1,640,1664]{2,1,0:T(8,128)(2,1)}, bf16[1,640,1664]{2,1,0:T(...) custom-call(s32[3]{0:T(128)} %pad_add_fusion.1.refs_0_, ...), custom_call_target="tpu_custom_call", output_to_operand_aliasing={{0}: (10, {}), {1}: (11, {}), {2}: (12, {}), {3}: (13, {})} | custom-call | flops 17179869184 | bytes 31457280 | tf_op jit(solution)/shard_map/expert_rows/pallas_call | solution.py:290
  226.1 31.7 %expert_rows.6 = (bf16[1,640,1536]{2,1,0:T(8,128)(2,1)}, bf16[1,640,1536]{2,1,0:T(8,128)(2,1)}, bf16[1,640,1664]{2,1,0:T(8,128)(2,1)}, bf16[1,640,1664]{2,1,0:T(...) custom-call(s32[3]{0:T(128)} %pad_add_fusion.1.refs_0_, ...), custom_call_target="tpu_custom_call", output_to_operand_aliasing={{4}: (10, {}), {5}: (11, {}), {6}: (12, {}), {7}: (13, {}),... | custom-call | flops 1000 | bytes 1000 | tf_op jit(solution)/shard_map/expert_rows/pallas_call | solution.py:290
  257.8 17.9 %expert_weight_gradients.2 = bf16[2304,1536]{1,0:T(8,128)(2,1)} custom-call(bf16[1,1472,1536]{2,1,0:T(8,128)(2,1)} %get-tuple-element.127.x_in, bf16[1,1472,768]{2,1,0:T(8,128)(2,1)} %get-tuple-element.128.gg_in, bf16[1,1472,768]{2,1,0:T(8,128)(2,1)} %get-tuple-element.129.gu_in, bf16[1,1472,768]{2,1,0:T(8,128)(2,1)} %get-tuple-element.130.h_in, ...), custom_call_target="tpu_custom_call" | custom-call | flops 1000 | bytes 1000 | tf_op jit(solution)/shard_map/expert_weight_gradients/pallas_call | solution.py:378
  275.7 31.3 %expert_rows.7 = (bf16[1,640,1536]{2,1,0:T(8,128)(2,1)}, bf16[1,640,1536]{2,1,0:T(8,128)(2,1)}, bf16[1,640,1664]{2,1,0:T(8,128)(2,1)}, bf16[1,640,1664]{2,1,0:T(...) custom-call(s32[3]{0:T(128)} %pad_add_fusion.1.refs_0_, ...), custom_call_target="tpu_custom_call", output_to_operand_aliasing={{0}: (8, {}), {1}: (9, {}), {2}: (10, {}), {3}: (11, {}), {... | custom-call | flops 1000 | bytes 1000 | tf_op jit(solution)/shard_map/expert_rows/pallas_call | solution.py:290
  315.5 18.1 %expert_weight_gradients.3 = bf16[2304,1536]{1,0:T(8,128)(2,1)} custom-call(bf16[1,1472,1536]{2,1,0:T(8,128)(2,1)} %get-tuple-element.162.x_in, bf16[1,1472,768]{2,1,0:T(8,128)(2,1)} %get-tuple-element.163.gg_in, bf16[1,1472,768]{2,1,0:T(8,128)(2,1)} %get-tuple-element.164.gu_in, bf16[1,1472,768]{2,1,0:T(8,128)(2,1)} %get-tuple-element.165.h_in, ...), custom_call_target="tpu_custom_call" | custom-call | flops 1000 | bytes 1000 | tf_op jit(solution)/shard_map/expert_weight_gradients/pallas_call | solution.py:378
  333.6 30.0 %collective-permute-done.23.refs_2_ = bf16[640,1664]{1,0:T(8,128)(2,1)} collective-permute-done((bf16[640,1664]{1,0:T(8,128)(2,1)}, bf16[640,1664]{1,0:T(8,128)(2,1)}, u32[]{:S(2)}, u32[]{:S(2)}) %collective-permute-start.23) | collective-permute-done | bytes 2129952 | tf_op jit(solution)/shard_map/ppermute | solution.py:828
  369.6 25.0 %collective-permute-done.24 = bf16[192,1536]{1,0:T(8,128)(2,1)S(1)} collective-permute-done((bf16[192,1536]{1,0:T(8,128)(2,1)S(1)}, bf16[192,1536]{1,0:T(8,128)(2,1)S(1)}, u32[]{:S(2)}, u32[]{:S(2)}) %collective-permute-start.24) | collective-permute-done | bytes 589856 | tf_op jit(solution)/shard_map/ppermute | solution.py:831
  398.3 21.7 %branch.1 = (f32[640,1536]{1,0:T(8,128)}, bf16[640,1536]{1,0:T(8,128)(2,1)}, bf16[1536,1536]{1,0:T(8,128)(2,1)}, f32[1,1536]{1,0:T(1,128)}, f32[128,1536]{1,0:T(8,128)}) custom-call(s32[2]{0:T(128)} %pad_add_fusion.place, bf16[640,1536]{1,0:T(8,128)(2,1)} %cotangent.1, f32[640,1536]{1,0:T(8,128)} %get-tuple-element.100.hidden, ...), custom_call_target="tpu_custom_call" | custom-call | flops 1000 | bytes 1000 | tf_op jit(solution)/shard_map/branch/pallas_call | solution.py:703
  420.0 25.0 %attend_back.1 = (bf16[640,2048]{1,0:T(8,128)(2,1)}, bf16[1536,2048]{1,0:T(8,128)(2,1)}) custom-call(s32[1,640]{1,0:T(1,128)} %segment_row.3, s32[640,1]{1,0:T(8,128)} %copy.78.segment_col, s32[1,640]{1,0:T(1,128)} %pad_row.3, bf16[640,2048]{1,0:T(8,128)(2,1)} %get-tuple-element.139.qkv, f32[640,128]{1,0:T(8,128)} %get-tuple-element.140.totals, ...), custom_call_target="tpu_custom_call" | custom-call | flops 1000 | bytes 1000 | tf_op jit(solution)/shard_map/attend_back/pallas_call | solution.py:569
  452.4 7.2 %collective-permute-done.27 = bf16[1536,768]{1,0:T(8,128)(2,1)} collective-permute-done((bf16[1536,768]{1,0:T(8,128)(2,1)}, bf16[1536,768]{1,0:T(8,128)(2,1)}, u32[]{:S(2)}, u32[]{:S(2)}) %collective-permute-start.27) | collective-permute-done | bytes 2359328 | tf_op jit(solution)/shard_map/ppermute | solution.py:821
  473.8 15.0 %input_grad.1 = (f32[640,1536]{1,0:T(8,128)}, f32[1,1536]{1,0:T(1,128)}) custom-call(s32[2]{0:T(128)} %pad_add_fusion.place, bf16[640,1536]{1,0:T(8,128)(2,1)} %tokens.5, f32[1,1536]{1,0:T(1,128)} %reshape.138.gain, bf16[640,2048]{1,0:T(8,128)(2,1)} %get-tuple-element.145.grad, f32[640,1536]{1,0:T(8,128)} %get-tuple-element.146.grad_hidden, ...), custom_call_target="tpu_custom_call" | custom-call | flops 1000 | bytes 1000 | tf_op jit(solution)/shard_map/input_grad/pallas_call | solution.py:753
  488.8 13.5 %collective-permute-done.30 = bf16[1,2,384,896]{3,2,1,0:T(8,128)(2,1)} collective-permute-done((bf16[1,2,384,896]{3,2,1,0:T(8,128)(2,1)}, bf16[1,2,384,896]{3,2,1,0:T(8,128)(2,1)}, u32[]{:S(2)}, u32[]{:S(2)}) %collective-permute-start.30) | collective-permute-done | bytes 1376288 | tf_op jit(solution)/shard_map/ppermute | solution.py:837
  517.6 19.6 %collective-permute-done.26 = bf16[320,1536]{1,0:T(8,128)(2,1)} collective-permute-done((bf16[320,1536]{1,0:T(8,128)(2,1)}, bf16[320,1536]{1,0:T(8,128)(2,1)}, u32[]{:S(2)}, u32[]{:S(2)}) %collective-permute-start.26) | collective-permute-done | bytes 983072 | tf_op jit(solution)/shard_map/ppermute | solution.py:828
  545.8 13.1 %collective-permute-done.39 = bf16[192,1792]{1,0:T(8,128)(2,1)S(1)} collective-permute-done((bf16[192,1792]{1,0:T(8,128)(2,1)S(1)}, bf16[192,1792]{1,0:T(8,128)(2,1)S(1)}, u32[]{:S(2)}, u32[]{:S(2)}) %collective-permute-start.39) | collective-permute-done | bytes 688160 | tf_op jit(solution)/shard_map/ppermute | solution.py:834
  559.6 16.1 %collective-permute-done.40 = bf16[96,1792]{1,0:T(8,128)(2,1)S(1)} collective-permute-done((bf16[96,1792]{1,0:T(8,128)(2,1)S(1)}, bf16[96,1792]{1,0:T(8,128)(2,1)S(1)}, u32[]{:S(2)}, u32[]{:S(2)}) %collective-permute-start.40) | collective-permute-done | bytes 344096 | tf_op jit(solution)/shard_map/ppermute | solution.py:834
  576.9 10.3 %collective-permute-done.41 = bf16[96,1792]{1,0:T(8,128)(2,1)S(1)} collective-permute-done((bf16[96,1792]{1,0:T(8,128)(2,1)S(1)}, bf16[96,1792]{1,0:T(8,128)(2,1)S(1)}, u32[]{:S(2)}, u32[]{:S(2)}) %collective-permute-start.41) | collective-permute-done | bytes 344096 | tf_op jit(solution)/shard_map/ppermute | solution.py:834
  588.8 7.0 %collective-permute-done.35 = f32[10,1536]{1,0:T(8,128)S(1)} collective-permute-done((f32[10,1536]{1,0:T(8,128)S(1)}, f32[10,1536]{1,0:T(8,128)S(1)}, u32[]{:S(2)}, u32[]{:S(2)}) %collective-permute-start.35) | collective-permute-done | bytes 61472 | tf_op jit(solution)/shard_map/ppermute | solution.py:837
  (234 shorter events, 173.9 us)
Async XLA Ops:
  7.2 181.4 %all-gather.3.cloned.1.call-start = ((), (), s32[]{:S(2)}) async-start(), calls=%async_computation.2 | async-start | bytes 4423680 | tf_op jit(solution)/shard_map/all_gather | solution.py:880
  11.2 33.4 %collective-permute-start.1 = (bf16[384,1792]{1,0:T(8,128)(2,1)}, bf16[384,1792]{1,0:T(8,128)(2,1)S(1)}, u32[]{:S(2)}, u32[]{:S(2)}) collective-permute-start(bf16[384,1792]{1,0:T(8,128)(2,1)} %pad_maximum_fusion.3), channel_id=1, source_target_pairs={{0,16},{8,24},{16,0},{24,8},{1,17},{9,25},{17,1},{25,9},{2,18},{10... | collective-permute-start | bytes 4128776 | tf_op jit(solution)/shard_map/ppermute | solution.py:837
  14.2 33.1 %collective-permute-start = (bf16[384,1792]{1,0:T(8,128)(2,1)}, bf16[384,1792]{1,0:T(8,128)(2,1)S(1)}, u32[]{:S(2)}, u32[]{:S(2)}) collective-permute-start(bf16[384,1792]{1,0:T(8,128)(2,1)} %pad_maximum_fusion.3), channel_id=1, source_target_pairs={{0,8},{8,0},{16,24},{24,16},{1,9},{9,1},{17,25},{25,17},{2,10},{10... | collective-permute-start | bytes 4128776 | tf_op jit(solution)/shard_map/ppermute | solution.py:837
  15.7 63.3 %collective-permute-start.5 = (bf16[640,1536]{1,0:T(8,128)(2,1)}, bf16[640,1536]{1,0:T(8,128)(2,1)}, u32[]{:S(2)}, u32[]{:S(2)}) collective-permute-start(bf16[640,1536]{1,0:T(8,128)(2,1)} %cotangent.1), channel_id=1, source_target_pairs={{0,2},{1,3},{2,0},{3,1},{4,6},{5,7},{6,4},{7,5},{8,10},{9,11},{10,... | collective-permute-start | bytes 5898248 | tf_op jit(solution)/shard_map/ppermute | solution.py:828
  21.1 57.0 %collective-permute-start.4 = (bf16[288,1536]{1,0:T(8,128)(2,1)}, bf16[288,1536]{1,0:T(8,128)(2,1)}, u32[]{:S(2)}, u32[]{:S(2)}) collective-permute-start(bf16[288,1536]{1,0:T(8,128)(2,1)} %get-tuple-element.188), channel_id=1, source_target_pairs={{0,4},{1,5},{2,6},{3,7},{4,0},{5,1},{6,2},{7,3},{8,12},{9,13},{10,... | collective-permute-start | bytes 2654216 | tf_op jit(solution)/shard_map/ppermute | solution.py:831
  45.5 33.4 %collective-permute-start.2 = (bf16[192,1792]{1,0:T(8,128)(2,1)}, bf16[192,1792]{1,0:T(8,128)(2,1)S(1)}, u32[]{:S(2)}, u32[]{:S(2)}) collective-permute-start(bf16[192,1792]{1,0:T(8,128)(2,1)} %slice.124), channel_id=1, source_target_pairs={{0,8},{8,0},{16,24},{24,16},{1,9},{9,1},{17,25},{25,17},{2,10},{10... | collective-permute-start | bytes 2064392 | tf_op jit(solution)/shard_map/ppermute | solution.py:837
  48.2 30.8 %collective-permute-start.3 = (bf16[192,1792]{1,0:T(8,128)(2,1)}, bf16[192,1792]{1,0:T(8,128)(2,1)}, u32[]{:S(2)}, u32[]{:S(2)}) collective-permute-start(bf16[192,1792]{1,0:T(8,128)(2,1)} %slice.125), channel_id=1, source_target_pairs={{0,16},{8,24},{16,0},{24,8},{1,17},{9,25},{17,1},{25,9},{2,18},{10... | collective-permute-start | bytes 2064392 | tf_op jit(solution)/shard_map/ppermute | solution.py:837
  88.3 275.3 %reduce-scatter.3.cloned.1.call-start = ((), (), s32[]{:S(2)}) async-start(), calls=%async_computation.3 | async-start | bytes 8847360 | tf_op jit(solution)/shard_map/reduce_scatter | solution.py:926
  88.5 42.4 %collective-permute-start.11 = (bf16[640,1536]{1,0:T(8,128)(2,1)}, bf16[640,1536]{1,0:T(8,128)(2,1)}, u32[]{:S(2)}, u32[]{:S(2)}) collective-permute-start(bf16[640,1536]{1,0:T(8,128)(2,1)} %cotangent.1), channel_id=1, source_target_pairs={{0,1},{1,0},{2,3},{3,2},{4,5},{5,4},{6,7},{7,6},{8,9},{9,8},{10,11... | collective-permute-start | bytes 5898248 | tf_op jit(solution)/shard_map/ppermute | solution.py:821
  88.7 42.2 %collective-permute-start.12 = (bf16[640,1536]{1,0:T(8,128)(2,1)}, bf16[640,1536]{1,0:T(8,128)(2,1)S(1)}, u32[]{:S(2)}, u32[]{:S(2)}) collective-permute-start(bf16[640,1536]{1,0:T(8,128)(2,1)} %collective-permute-done.5.refs_3_), channel_id=1, source_target_pairs={{0,1},{1,0},{2,3},{3,2},{4,5},{5,4},{6,7},{7,6},{8,9},{9,8},{10,11... | collective-permute-start | bytes 5898248 | tf_op jit(solution)/shard_map/ppermute | solution.py:821
  89.1 41.9 %collective-permute-start.10 = (bf16[288,1536]{1,0:T(8,128)(2,1)}, bf16[288,1536]{1,0:T(8,128)(2,1)}, u32[]{:S(2)}, u32[]{:S(2)}) collective-permute-start(bf16[288,1536]{1,0:T(8,128)(2,1)} %get-tuple-element.96), channel_id=1, source_target_pairs={{0,4},{1,5},{2,6},{3,7},{4,0},{5,1},{6,2},{7,3},{8,12},{9,13},{10,... | collective-permute-start | bytes 2654216 | tf_op jit(solution)/shard_map/ppermute | solution.py:831
  147.4 36.0 %collective-permute-start.14 = (bf16[288,1536]{1,0:T(8,128)(2,1)}, bf16[288,1536]{1,0:T(8,128)(2,1)S(1)}, u32[]{:S(2)}, u32[]{:S(2)}) collective-permute-start(bf16[288,1536]{1,0:T(8,128)(2,1)} %collective-permute-done.10.refs_6_), channel_id=1, source_target_pairs={{0,8},{8,0},{16,24},{24,16},{1,9},{9,1},{17,25},{25,17},{2,10},{10... | collective-permute-start | bytes 2654216 | tf_op jit(solution)/shard_map/ppermute | solution.py:837
  147.9 40.7 %collective-permute-start.15 = (bf16[288,1536]{1,0:T(8,128)(2,1)}, bf16[288,1536]{1,0:T(8,128)(2,1)}, u32[]{:S(2)}, u32[]{:S(2)}) collective-permute-start(bf16[288,1536]{1,0:T(8,128)(2,1)} %collective-permute-done.10.refs_6_), channel_id=1, source_target_pairs={{0,16},{8,24},{16,0},{24,8},{1,17},{9,25},{17,1},{25,9},{2,18},{10... | collective-permute-start | bytes 2654216 | tf_op jit(solution)/shard_map/ppermute | solution.py:837
  148.7 39.9 %collective-permute-start.16 = (bf16[288,1536]{1,0:T(8,128)(2,1)}, bf16[288,1536]{1,0:T(8,128)(2,1)}, u32[]{:S(2)}, u32[]{:S(2)}) collective-permute-start(bf16[288,1536]{1,0:T(8,128)(2,1)} %collective-permute-done.10.refs_6_), channel_id=1, source_target_pairs={{0,24},{8,16},{16,8},{24,0},{1,25},{9,17},{17,9},{25,1},{2,26},{10... | collective-permute-start | bytes 2654216 | tf_op jit(solution)/shard_map/ppermute | solution.py:837
  150.9 69.6 %collective-permute-start.18 = (bf16[640,1664]{1,0:T(8,128)(2,1)}, bf16[640,1664]{1,0:T(8,128)(2,1)S(1)}, u32[]{:S(2)}, u32[]{:S(2)}) collective-permute-start(bf16[640,1664]{1,0:T(8,128)(2,1)} %get-tuple-element.101.refs_1_.payload), channel_id=1, source_target_pairs={{0,2},{1,3},{2,0},{3,1},{4,6},{5,7},{6,4},{7,5},{8,10},{9,11},{10,... | collective-permute-start | bytes 6389768 | tf_op jit(solution)/shard_map/ppermute | solution.py:828
  275.7 234.7 %reduce-scatter.5.cloned.1.call-start = ((), (), s32[]{:S(2)}) async-start(), calls=%async_computation.4 | async-start | bytes 8847360 | tf_op jit(solution)/shard_map/reduce_scatter | solution.py:926
  314.9 48.7 %collective-permute-start.23 = (bf16[640,1664]{1,0:T(8,128)(2,1)}, bf16[640,1664]{1,0:T(8,128)(2,1)}, u32[]{:S(2)}, u32[]{:S(2)}) collective-permute-start(bf16[640,1664]{1,0:T(8,128)(2,1)} %fusion), channel_id=1, source_target_pairs={{0,2},{1,3},{2,0},{3,1},{4,6},{5,7},{6,4},{7,5},{8,10},{9,11},{10,... | collective-permute-start | bytes 6389768 | tf_op jit(solution)/shard_map/ppermute | solution.py:828
  363.6 257.5 %all-gather.5.cloned.1.call-start = ((), (), s32[]{:S(2)}) async-start(), calls=%async_computation.5 | async-start | bytes 8847360 | tf_op jit(solution)/shard_map/all_gather | solution.py:1005
  365.4 29.2 %collective-permute-start.24 = (bf16[192,1536]{1,0:T(8,128)(2,1)S(1)}, bf16[192,1536]{1,0:T(8,128)(2,1)S(1)}, u32[]{:S(2)}, u32[]{:S(2)}) collective-permute-start(bf16[192,1536]{1,0:T(8,128)(2,1)S(1)} %get-tuple-element.136), channel_id=1, source_target_pairs={{0,4},{1,5},{2,6},{3,7},{4,0},{5,1},{6,2},{7,3},{8,12},{9,13},{10,... | collective-permute-start | bytes 1769480 | tf_op jit(solution)/shard_map/ppermute | solution.py:831
  394.6 50.4 %collective-permute-start.25 = (bf16[320,1536]{1,0:T(8,128)(2,1)S(1)}, bf16[320,1536]{1,0:T(8,128)(2,1)S(1)}, u32[]{:S(2)}, u32[]{:S(2)}) collective-permute-start(bf16[320,1536]{1,0:T(8,128)(2,1)S(1)} %get-tuple-element.137), channel_id=1, source_target_pairs={{0,2},{1,3},{2,0},{3,1},{4,6},{5,7},{6,4},{7,5},{8,10},{9,11},{10,... | collective-permute-start | bytes 2949128 | tf_op jit(solution)/shard_map/ppermute | solution.py:828
  394.9 50.1 %collective-permute-start.28 = (bf16[192,1536]{1,0:T(8,128)(2,1)S(1)}, bf16[192,1536]{1,0:T(8,128)(2,1)}, u32[]{:S(2)}, u32[]{:S(2)}) collective-permute-start(bf16[192,1536]{1,0:T(8,128)(2,1)S(1)} %get-tuple-element.153), channel_id=1, source_target_pairs={{0,4},{1,5},{2,6},{3,7},{4,0},{5,1},{6,2},{7,3},{8,12},{9,13},{10,... | collective-permute-start | bytes 1769480 | tf_op jit(solution)/shard_map/ppermute | solution.py:831
  469.8 32.5 %collective-permute-start.30 = (bf16[1,2,384,896]{3,2,1,0:T(8,128)(2,1)}, bf16[1,2,384,896]{3,2,1,0:T(8,128)(2,1)}, u32[]{:S(2)}, u32[]{:S(2)}) collective-permute-start(bf16[1,2,384,896]{3,2,1,0:T(8,128)(2,1)} %constant_dynamic-slice_fusion.4), channel_id=1, source_target_pairs={{0,16},{8,24},{16,0},{24,8},{1,17},{9,25},{17,1},{25,9},{2,18},{10... | collective-permute-start | bytes 4128776 | tf_op jit(solution)/shard_map/ppermute | solution.py:837
  472.3 32.3 %collective-permute-start.32 = (bf16[2,1,384,896]{3,2,1,0:T(8,128)(2,1)}, bf16[2,1,384,896]{3,2,1,0:T(8,128)(2,1)}, u32[]{:S(2)}, u32[]{:S(2)}) collective-permute-start(bf16[2,1,384,896]{3,2,1,0:T(8,128)(2,1)} %constant_dynamic-slice_fusion.2), channel_id=1, source_target_pairs={{0,8},{8,0},{16,24},{24,16},{1,9},{9,1},{17,25},{25,17},{2,10},{10... | collective-permute-start | bytes 4128776 | tf_op jit(solution)/shard_map/ppermute | solution.py:837
  472.9 37.5 %collective-permute-start.44 = (bf16[192,1536]{1,0:T(8,128)(2,1)S(1)}, bf16[192,1536]{1,0:T(8,128)(2,1)}, u32[]{:S(2)}, u32[]{:S(2)}) collective-permute-start(bf16[192,1536]{1,0:T(8,128)(2,1)S(1)} %get-tuple-element.168), channel_id=1, source_target_pairs={{0,4},{1,5},{2,6},{3,7},{4,0},{5,1},{6,2},{7,3},{8,12},{9,13},{10,... | collective-permute-start | bytes 1769480 | tf_op jit(solution)/shard_map/ppermute | solution.py:831
  (57 other events, 722.6 us)
Sparse Core Ops, SparseCore 0:
  88.4 46.6 all-gather.2
  275.8 76.8 reduce-scatter.2
  363.8 76.8 reduce-scatter.4
  514.3 83.1 all-gather.4

commit v3 on v2

--- a/solution.py
+++ b/solution.py
@@ -49,16 +49,17 @@
     return pltpu.CompilerParams(vmem_limit_bytes=60 * MIB)
 
 
-def expert_kernel(experts, slots, base, data, pieces, chunks, n_weights, n_prev, n_saved, rows, *refs):
+def expert_kernel(experts, slots, base, data, pieces, chunks, cuts, n_weights, n_prev, n_saved, rows, *refs):
     count = len(slots)
-    hosted, sources, refs = refs[0], refs[1:1 + 4 * chunks], refs[1 + 4 * chunks:]
-    sources = [sources[4 * i:4 * i + 4] for i in range(chunks)]
+    each = 2 + 2 * len(cuts)
+    hosted, sources, refs = refs[0], refs[1:1 + each * chunks], refs[1 + each * chunks:]
+    sources = [sources[each * i:each * (i + 1)] for i in range(chunks)]
     weight_refs, refs = refs[:n_weights], refs[n_weights:]
     prev, refs = refs[:n_prev], refs[n_prev + n_saved:]
     po_same, po_other, pg_same, pg_other, x_out, gp_out, h_out, gg_out, gu_out = refs[:9]
     (wg, wu, wd, nbuf, cbuf, x, gp, gc, sc, h, gg, gu, dmat, dtmat, gcol, vcol, tail_t,
      w_sem, in_sem, act_sem, p_sem) = refs[9:]
-    tokens, features = sources[0][2].shape
+    tokens, features = sources[0][0].shape[0], sources[0][2].shape[1]
     extra = sources[0][0].shape[1] - features
     ff = wg.shape[2]
     wide = features // 2
@@ -93,7 +94,8 @@
         ])
 
     def input_copies(index):
-        targets = (nbuf.at[0], nbuf.at[1], cbuf.at[0], cbuf.at[1])
+        parts = [cbuf.at[q, pl.ds(first, size)] for q in range(2) for first, size in cuts]
+        targets = [nbuf.at[0], nbuf.at[1]] + parts
         return [
             pltpu.make_async_copy(source, target, in_sem.at[i])
             for i, (source, target) in enumerate(zip(sources[index], targets))
@@ -271,7 +273,12 @@
 
 def expert_call(hosted, slots, sources, weights, prev, saved, base, total, experts, rows, data, pieces, cost):
     chunks = len(sources)
-    tokens, features = sources[0][2].shape
+    tokens, features = sources[0][0].shape[0], sources[0][2][0].shape[1]
+    cuts, first = [], 0
+    for part in sources[0][2]:
+        cuts.append((first, part.shape[0]))
+        first += part.shape[0]
+    flat = [v for same, other, *parts in sources for v in (same, other, *parts[0], *parts[1])]
     ff = weights[0].shape[1] if slots[0] == 0 else weights[0].shape[1] // 2
     wide_n = sources[0][0].shape[1]
     extra = wide_n - features
@@ -285,13 +292,13 @@
         + [act_f, act_f, act_h, act_h, act_h]
     )
     many = 2 * rows
-    first_prev = 1 + 4 * chunks + len(weights)
+    first_prev = 1 + len(flat) + len(weights)
     first_saved = first_prev + len(prev)
     return pl.pallas_call(
         functools.partial(
-            expert_kernel, experts, slots, base, data, pieces, chunks, len(weights), len(prev), len(saved), rows),
+            expert_kernel, experts, slots, base, data, pieces, chunks, tuple(cuts), len(weights), len(prev), len(saved), rows),
         out_shape=out_shape,
-        in_specs=specs("s" + "a" * (4 * chunks + len(weights) + len(prev) + len(saved))),
+        in_specs=specs("s" + "a" * (len(flat) + len(weights) + len(prev) + len(saved))),
         out_specs=specs("a" * 9),
         input_output_aliases={
             **{first_prev + i: i for i in range(len(prev))},
@@ -316,14 +323,14 @@
             pltpu.VMEM((count, many, 128), f32),
             pltpu.VMEM((extra, tokens), f32),
             pltpu.SemaphoreType.DMA((count, 3 * max(1, len(pieces)))),
-            pltpu.SemaphoreType.DMA((4,)),
+            pltpu.SemaphoreType.DMA((max(4, 2 + 2 * len(cuts)),)),
             pltpu.SemaphoreType.DMA((count, 5)),
             pltpu.SemaphoreType.DMA((4,)),
         ],
         compiler_params=params(),
         cost_estimate=cost,
         name="expert_rows",
-    )(hosted, *[v for group in sources for v in group], *weights, *prev, *saved)
+    )(hosted, *flat, *weights, *prev, *saved)
 
 
 def weight_gradient_kernel(data, x_in, gg_in, gu_in, h_in, gp_in, out, x, gg, gu, h, gp, wide, down, sem, out_sem):
@@ -397,6 +404,30 @@
     )(x, gg, gu, h, gp)
 
 
+def widened_kernel(whole, gate, up, down):
+    tall, ff = gate.shape
+    gate[...] = whole[:tall, :ff].astype(f32)
+    up[...] = whole[:tall, ff:].astype(f32)
+    down[...] = whole[tall:, :].astype(f32)
+
+
+def widened(whole, data):
+    rows, features = whole.shape[0] // data, whole.shape[1]
+    ff = features // 2
+    tall = rows * 2 // 3
+    blocks = [(tall, ff), (tall, ff), (rows - tall, features)]
+    return pl.pallas_call(
+        widened_kernel,
+        grid=(data,),
+        in_specs=[pl.BlockSpec((rows, features), lambda d: (d, 0))],
+        out_specs=[pl.BlockSpec(block, lambda d: (d, 0)) for block in blocks],
+        out_shape=[jax.ShapeDtypeStruct((data * block[0], block[1]), f32) for block in blocks],
+        compiler_params=params(),
+        cost_estimate=COST,
+        name="widened",
+    )(whole)
+
+
 epsilon = 1e-06
 neg_fill = -1e30
 QUERY_HEADS = 12
@@ -489,7 +520,7 @@
                 mixture[rows, lanes((c * GROUP + g) * HEAD_SIZE, HEAD_SIZE)] = mixed[g * block:(g + 1) * block]
 
 
-def attend_call(place, tokens, gain, segments, pads, own, pieces):
+def attend_call(place, tokens, gain, segments, segment_columns, pads, own, pieces):
     rows, features = tokens.shape
     width = (QUERY_HEADS + 2 * KEY_VALUE_HEADS) * HEAD_SIZE
     mixed = QUERY_HEADS * HEAD_SIZE
@@ -510,11 +541,11 @@
         compiler_params=params(),
         cost_estimate=COST,
         name="attend",
-    )(place, tokens, gain, segments, segments.reshape(rows, 1), pads, *own, *flat)
-
-
-def attend_back_kernel(tokens_total, block, segment_row, segment_col, pad_row, qkv, totals, given, normed,
-                       grad, local, grad_keys, grad_values):
+    )(place, tokens, gain, segments, segment_columns, pads, *own, *flat)
+
+
+def attend_back_kernel(tokens_total, block, place, segment_row, segment_col, pad_row, qkv, totals, given, normed,
+                       grad, keep, give, grad_keys, grad_values):
     width = QUERY_HEADS * HEAD_SIZE
     kv_width = KEY_VALUE_HEADS * HEAD_SIZE
     segment_of_row, segment_of_col, pad = segment_row[...], segment_col[...], pad_row[...]
@@ -559,23 +590,25 @@
     @pl.loop(0, normed.shape[1] // tall)
     def _(tile):
         cols = lanes(tile * tall, tall)
-        local[pl.ds(pl.multiple_of(tile * tall, tall), tall), :] = mm_tn(normed[:, cols], grad[...]).astype(bf16)
-
-
-def attend_back_call(segments, pads, qkv, totals, given, normed):
+        at = pl.ds(pl.multiple_of(tile * tall, tall), tall)
+        for core, out in ((place[1], keep), (1 - place[1], give)):
+            out[at, :] = mm_tn(normed[:, cols], grad[:, lanes(core * keep.shape[1], keep.shape[1])]).astype(bf16)
+
+
+def attend_back_call(place, segments, segment_columns, pads, qkv, totals, given, normed):
     rows, width = qkv.shape
     features = normed.shape[1]
     shape = jax.ShapeDtypeStruct
     return pl.pallas_call(
         functools.partial(attend_back_kernel, rows, 128),
-        out_shape=[shape((rows, width), bf16), shape((features, width), bf16)],
-        in_specs=specs("v" * 7),
-        out_specs=specs("vv"),
+        out_shape=[shape((rows, width), bf16)] + [shape((features, width // 2), bf16)] * 2,
+        in_specs=specs("s" + "v" * 7),
+        out_specs=specs("vvv"),
         scratch_shapes=[pltpu.VMEM((rows, HEAD_SIZE), f32), pltpu.VMEM((rows, HEAD_SIZE), f32)],
         compiler_params=params(),
         cost_estimate=COST,
         name="attend_back",
-    )(segments, segments.reshape(rows, 1), pads, qkv, totals, given, normed)
+    )(place, segments, segment_columns, pads, qkv, totals, given, normed)
 
 
 def route_kernel(experts, n_own, n_pairs, place, mixture, tokens, gain, router_weight, slots, *refs):
@@ -642,7 +675,7 @@
     own = refs[:n_own]
     flat = refs[n_own:n_own + 2 * n_pairs]
     pieces = [(flat[2 * k], flat[2 * k + 1]) for k in range(n_pairs)]
-    grad_hidden, given, local_out, local_gain, local_router, weight, branch, sem = refs[n_own + 2 * n_pairs:]
+    grad_hidden, given, keep, give, local_gain, local_router, weight, branch, sem = refs[n_own + 2 * n_pairs:]
     copies = piece_copies(place, own, pieces, (QUERY_HEADS + 2 * KEY_VALUE_HEADS) * HEAD_SIZE // 2, weight, sem)
     for copy in copies:
         copy.start()
@@ -682,7 +715,9 @@
     @pl.loop(0, mixture.shape[1] // tall)
     def _(tile):
         cols = lanes(tile * tall, tall)
-        local_out[pl.ds(pl.multiple_of(tile * tall, tall), tall), :] = mm_tn(mixture[:, cols], branch[...]).astype(bf16)
+        at = pl.ds(pl.multiple_of(tile * tall, tall), tall)
+        for core, out in ((place[1], keep), (1 - place[1], give)):
+            out[at, :] = mm_tn(mixture[:, cols], branch[:, lanes(core * keep.shape[1], keep.shape[1])]).astype(bf16)
 
     for copy in copies:
         copy.wait()
@@ -703,11 +738,11 @@
     return pl.pallas_call(
         functools.partial(branch_kernel, experts, len(backs), len(own), len(pieces)),
         out_shape=[
-            shape((rows, features), f32), shape((rows, mixed), bf16), shape((mixed, features), bf16),
-            shape((1, features), f32), shape((extra, features), f32),
+            shape((rows, features), f32), shape((rows, mixed), bf16), shape((mixed, features // 2), bf16),
+            shape((mixed, features // 2), bf16), shape((1, features), f32), shape((extra, features), f32),
         ],
         in_specs=specs("s" + "v" * (6 + len(backs)) + "a" * (len(own) + len(flat))),
-        out_specs=specs("vvvvv"),
+        out_specs=specs("vvvvvv"),
         scratch_shapes=[
             pltpu.VMEM((mixed, features), bf16),
             pltpu.VMEM((rows, features), bf16),
@@ -764,6 +799,81 @@
         cost_estimate=COST,
         name="input_grad",
     )(place, tokens, gain, grad, grad_hidden, *own, *flat)
+
+
+def fold_first_kernel(place, keep, got, keep_a, give_a, keep_b, give_b):
+    rows, quart = keep_a.shape[1], keep_a.shape[2]
+    high, low = lax.div(place[0], 2), lax.rem(place[0], 2)
+
+    def total(high_bit, low_bit, first):
+        at = pl.ds(pl.multiple_of((high_bit * 2 + low_bit) * rows, 16), rows)
+        cols = slice(first, first + quart)
+        return (keep[at, cols].astype(f32) + got[at, cols].astype(f32)).astype(bf16)
+
+    for bit in range(2):
+        keep_a[bit] = total(high, bit, 0)
+        give_a[bit] = total(1 - high, bit, 0)
+        keep_b[bit] = total(bit, low, quart)
+        give_b[bit] = total(bit, 1 - low, quart)
+
+
+def fold_first(place, keep, got, data):
+    rows, quart = keep.shape[0] // data, keep.shape[1] // 2
+    return pl.pallas_call(
+        fold_first_kernel,
+        out_shape=[jax.ShapeDtypeStruct((2, rows, quart), bf16)] * 4,
+        in_specs=specs("svv"),
+        out_specs=specs("vvvv"),
+        compiler_params=params(),
+        cost_estimate=COST,
+        name="fold_first",
+    )(place, keep, got)
+
+
+def fold_second_kernel(place, keep_a, got_a, keep_b, got_b, next_a, give_a, next_b, give_b):
+    high, low = lax.div(place[0], 2), lax.rem(place[0], 2)
+    for bit, keep, got, kept, give in ((low, keep_a, got_a, next_a, give_a), (high, keep_b, got_b, next_b, give_b)):
+        kept[...] = (keep[bit].astype(f32) + got[bit].astype(f32)).astype(bf16)
+        give[...] = (keep[1 - bit].astype(f32) + got[1 - bit].astype(f32)).astype(bf16)
+
+
+def fold_second(place, keep_a, got_a, keep_b, got_b):
+    return pl.pallas_call(
+        fold_second_kernel,
+        out_shape=[jax.ShapeDtypeStruct(keep_a.shape[1:], bf16)] * 4,
+        in_specs=specs("svvvv"),
+        out_specs=specs("vvvv"),
+        compiler_params=params(),
+        cost_estimate=COST,
+        name="fold_second",
+    )(place, keep_a, got_a, keep_b, got_b)
+
+
+def joined_kernel(place, mine, other, *outs):
+    half = mine.shape[1]
+    first = 0
+    for out in outs:
+        done = 0
+        while done < out.shape[1]:
+            at = first + done
+            size = min(out.shape[1] - done, half - at % half)
+            cols = slice(at % half, at % half + size)
+            own = place[1] == at // half
+            out[:, done:done + size] = jnp.where(own, mine[:, cols], other[:, cols]).astype(f32)
+            done += size
+        first += out.shape[1]
+
+
+def joined(place, mine, other, widths):
+    return pl.pallas_call(
+        joined_kernel,
+        out_shape=[jax.ShapeDtypeStruct((mine.shape[0], width), f32) for width in widths],
+        in_specs=specs("svv"),
+        out_specs=specs("v" * len(widths)),
+        compiler_params=params(),
+        cost_estimate=COST,
+        name="joined",
+    )(place, mine, other)
 
 
 def pair_slots(routes, order_row, experts, capacity):
@@ -854,10 +964,11 @@
     quarter = jnp.concatenate(
         [jnp.concatenate([dp_part(own[0]), dp_part(own[1])], axis=1), dp_part(own[2])], axis=0
     )
-    part_rows = quarter.shape[0] // 2
+    part_rows = quarter.shape[0] * 11 // 18
     crossed_one = across(quarter[:part_rows])
 
-    cot_far_same = [shift(cotangent, k) for k in range(1, half)]
+    token_half = token_rows // 2
+    cot_first = [shift(cotangent[:token_half], k) for k in range(1, half)]
 
     qkv_own = [w_query, key_weight, value_weight]
     qkv_half = (query_width + 2 * kv_width) // 2
@@ -872,44 +983,52 @@
     )
     router_weight = jnp.pad(w_router, ((0, 0), (0, extra - experts)))
     router_weight_three = jnp.pad(jnp.concatenate([w_router] * 3, axis=1), ((0, 0), (0, extra - 3 * experts)))
-    ready = after(got, crossed_one, cot_far_same, slot_columns, router_weight, router_weight_three)
+    gain_one = norm_attn.reshape(1, features)
+    gain_two = norm_moe.reshape(1, features)
+    segment_columns = document_index.reshape(token_rows, 1)
+    ready, gain_one, gain_two, segment_columns = after(
+        (got, gain_one, gain_two, segment_columns),
+        crossed_one, cot_first, slot_columns, router_weight, router_weight_three,
+    )
     pieces = [(v, swap(v)) for v in ready]
     crossed_two = across(after(quarter[part_rows:], crossed_one))
+    cot_second = [shift(after(cotangent[token_half:], pieces), k) for k in range(1, half)]
     cot_other = swap(after(cotangent, pieces))
-    cot_far_other = [swap(after(v, pieces)) for v in cot_far_same]
+    cot_first_other = [swap(after(v, pieces)) for v in cot_first]
     partner_one = lax.all_gather(after(crossed_one, pieces), "dp", axis=0, tiled=True)
 
-    gain_one = norm_attn.reshape(1, features)
-    gain_two = norm_moe.reshape(1, features)
-
     normed_one, qkv, mixture, totals = attend_call(
-        place, tokens, gain_one, document_index, padding_token_mask, qkv_own, pieces
+        place, tokens, gain_one, document_index, segment_columns, padding_token_mask, qkv_own, pieces
     )
     hidden_one, payload = route_call(
-        place, after(mixture, crossed_two, cot_other, cot_far_other), tokens, gain_two, router_weight,
+        place, after(mixture, crossed_two, cot_second, cot_other, cot_first_other), tokens, gain_two, router_weight,
         slot_columns, [w_out], pieces, experts,
     )
 
+    payload_other = swap(payload)
     payload_far_same = [shift(payload, k) for k in range(1, half)]
-    payload_other = swap(payload)
     total_rows = chips // 2 * 2 * slot_rows
 
     two = after(crossed_two, payload_other)
     partner = [partner_one, two] + from_dp(two)
     spread = tuple((0, d * part_rows, part_rows, (False, d), 0) for d in range(data))
-    spread += tuple((1 + k, 0, part_rows, (True, k), part_rows) for k in range(data))
+    spread += tuple((1 + k, 0, quarter.shape[0] - part_rows, (True, k), part_rows) for k in range(data))
 
     def rows_of(slot, sources, weights, prev, saved, base, cost=COST):
         return expert_call(
             hosted, (slot,), sources, weights, prev, saved, base, total_rows, experts, slot_rows, data, spread, cost
         )
 
-    one = [(payload, payload_other, cotangent, cot_other)]
+    one = [(payload, payload_other, (cotangent,), (cot_other,))]
     near = rows_of(0, one, own, [], [], 0)
     near_saved = near[4:]
     near = rows_of(1, one, partner, near[:4], [], 0, LONG)
     payload_far_other = [swap(after(v, near[0])) for v in payload_far_same]
-    many = list(zip(payload_far_same, payload_far_other, cot_far_same, cot_far_other))
+    cot_second_other = [swap(after(v, near[0])) for v in cot_second]
+    many = list(zip(
+        payload_far_same, payload_far_other, zip(cot_first, cot_second), zip(cot_first_other, cot_second_other)
+    ))
+    many = [(same, other, tuple(c_same), tuple(c_other)) for same, other, c_same, c_other in many]
     far = rows_of(1, many, partner, [], near[4:], 2 * slot_rows)
     partner_local = weight_gradient_call(far[4:], data)
     far = rows_of(0, many, own, far[:4], near_saved, 2 * slot_rows)
@@ -928,34 +1047,15 @@
     partner_sum = scattered(partner_local)
     backs, back_sums = returned(near[2], near[3], far[2], far[3])
     backs += [shift(v, half - 1 - k) for k, v in enumerate(back_sums)]
-    own_local = weight_gradient_call([after(saved[0], back_sums), *saved[1:]], data)
+    outs, out_sums = returned(near[0], after(near[1], back_sums), far[0], after(far[1], back_sums))
+    own_local = weight_gradient_call([after(saved[0], back_sums, out_sums), *saved[1:]], data)
     own_sum = scattered(after(own_local, partner_sum, backs))
-    grad_hidden, given, local_out, local_norm_moe, local_router = branch_call(
+    grad_hidden, given, out_keep, out_give, local_norm_moe, local_router = branch_call(
         place, cotangent, hidden_one, payload, gain_two, router_weight_three, mixture, backs,
         [w_out], pieces, experts,
     )
 
-    def halved(v):
-        width = v.shape[1] // 2
-        keep = core_half(v)
-        give = jnp.where(core == 0, v[:, width:], v[:, :width])
-        return (keep.astype(f32) + swap(give).astype(f32)).astype(bf16)
-
-    def fold(sides, stage, *others):
-        done = []
-        for side, order in zip(sides, ((0, 1), (1, 0))):
-            axis = order[stage]
-            bit, step = ((my_dp // 2, 2), (lax.rem(my_dp, 2), 1))[axis]
-            keep = lax.dynamic_index_in_dim(side, bit, axis, keepdims=True)
-            give = lax.dynamic_index_in_dim(side, 1 - bit, axis, keepdims=True)
-            done.append((keep.astype(f32) + after(dp_xor(give, step), *others).astype(f32)).astype(bf16))
-        return done
-
-    def sides_of(part):
-        rows, quart = part.shape[0] // data, part.shape[1] // 2
-        return [v.reshape(2, 2, rows, quart) for v in (part[:, :quart], part[:, quart:])]
-
-    def chip_sum(part):
+    def chip_sum(part, beside, middle, last):
         sizes = []
         step = 1
         chip = me // 2
@@ -964,78 +1064,89 @@
             bit = lax.rem(chip // step, 2)
             keep = lax.dynamic_slice_in_dim(part, bit * size, size, axis=0)
             give = lax.dynamic_slice_in_dim(part, (1 - bit) * size, size, axis=0)
-            part = (keep.astype(f32) + chip_xor(give, step).astype(f32)).astype(bf16)
+            part = (keep.astype(f32) + chip_xor(beside(give), step).astype(f32)).astype(bf16)
             sizes.append((step, bit))
             step *= 2
         for step, bit in reversed(sizes):
+            part = after(beside(part), *middle)
             other = chip_xor(part, step)
+            if step == 1:
+                other = after(other, *last)
             part = jnp.concatenate(
                 [jnp.where(bit == 0, part, other), jnp.where(bit == 0, other, part)], axis=0
             )
         return part
 
-    def joined(part):
-        other = swap(part)
-        first = jnp.where(core == 0, part, other)
-        second = jnp.where(core == 0, other, part)
-        return first, second
-
-    thirds = jnp.split(partner_sum, 3, axis=0)
+    first_cut, second_cut = partner_sum.shape[0] * 11 // 36, partner_sum.shape[0] * 24 // 36
+    thirds = jnp.split(partner_sum, (first_cut, second_cut), axis=0)
     arrived_one = across(after(thirds[0], backs))
-    arrived_two = across(after(thirds[1], arrived_one))
-    given, local_out = after((given, local_out), arrived_one)
-    out_half = halved(local_out)
-    outs, out_sums = returned(near[0], near[1], far[0], far[1])
-    half_rows = token_rows // 2
-    outs_one = [shift(after(v[:half_rows], arrived_one), half - 1 - k) for k, v in enumerate(out_sums)]
-    grad_qkv, local_qkv = attend_back_call(
-        document_index, padding_token_mask, qkv, totals, given, normed_one
-    )
-    local_qkv = after(local_qkv, arrived_two, outs_one)
+    arrived_two = across(after(thirds[1], arrived_one, grad_hidden))
+    given, out_give = after((given, out_give), arrived_one)
+    cuts = [0, 9 * token_rows // 40, token_rows // 2, token_rows]
+
+    def out_parts(index, *others):
+        rows = slice(cuts[index], cuts[index + 1])
+        return [shift(after(v[rows], *others), half - 1 - k) for k, v in enumerate(out_sums)]
+
+    outs_one = out_parts(0, backs)
+    outs_two = out_parts(1, arrived_one, grad_hidden, outs_one)
+    given, out_give = after((given, out_give), outs_one)
+    out_got = swap(out_give)
+    grad_qkv, qkv_keep, qkv_give = attend_back_call(
+        place, document_index, segment_columns, padding_token_mask, qkv, totals, given, normed_one
+    )
+    qkv_give, out_got = after((qkv_give, out_got), arrived_two, outs_two)
     arrived_three = across(after(thirds[2], arrived_two))
-    outs_two = [shift(after(v[half_rows:], outs_one), half - 1 - k) for k, v in enumerate(out_sums)]
-    sides = sides_of(jnp.concatenate([out_half, halved(local_qkv)], axis=1))
+    out_folds = fold_first(place, out_keep, out_got, data)
+    out_arrived = [dp_xor(out_folds[1], 2), dp_xor(out_folds[3], 1)]
+    qkv_folds = fold_first(place, qkv_keep, swap(qkv_give), data)
+    qkv_arrived = [dp_xor(qkv_folds[1], 2), dp_xor(qkv_folds[3], 1)]
     grad_tokens, local_norm_attn = input_grad_call(
-        place, tokens, gain_one, grad_qkv, grad_hidden, qkv_own, pieces
-    )
-    sides = fold(sides, 0, grad_tokens)
-    arrived_three = after(arrived_three, sides)
+        place, tokens, gain_one, after(grad_qkv, qkv_folds, out_folds), grad_hidden, qkv_own, pieces
+    )
+    qkv_arrived, out_arrived, arrived_three = after((qkv_arrived, out_arrived, arrived_three), grad_tokens)
+    outs_three = out_parts(2, arrived_three)
+    local_router = local_router[:3 * experts].reshape(3, experts, features).sum(0)
+    small = jnp.concatenate([local_router, local_norm_attn, local_norm_moe], axis=0)
+    small_steps = [swap] + [functools.partial(dp_xor, k=1 << i) for i in range(data.bit_length() - 1)]
+    small_steps += [functools.partial(chip_xor, step=1 << i) for i in range(chips.bit_length() - 1)]
+
+    def beside(large):
+        nonlocal small
+        large, small = after((large, small))
+        if small_steps:
+            small = small + small_steps.pop(0)(small)
+        return large
+
+    def folded(folds, arrived):
+        keep_a, give_a, keep_b, give_b = fold_second(place, folds[0], arrived[0], folds[2], arrived[1])
+        got_a, got_b = dp_xor(give_a, 1), dp_xor(give_b, 2)
+        return jnp.concatenate([
+            (keep.astype(f32) + got.astype(f32)).astype(bf16) for keep, got in ((keep_a, got_a), (keep_b, got_b))
+        ], axis=1)
+
+    out_part = folded(out_folds, out_arrived)
+    qkv_part = beside(folded(qkv_folds, qkv_arrived))
+    arrived_three = after(arrived_three, out_part, qkv_part)
     arrived = jnp.concatenate([arrived_one, arrived_two, arrived_three], axis=0)
     expert_sum = (own_sum.astype(f32) + arrived.astype(f32)).astype(bf16)
-    whole = lax.all_gather(expert_sum, "dp", axis=0, tiled=True).reshape(data, -1, 2 * ff)
-    tall = features // data
-    grad_gate = whole[:, :tall, :ff].reshape(1, features, ff).astype(f32)
-    grad_up = whole[:, :tall, ff:].reshape(1, features, ff).astype(f32)
-    grad_down = whole[:, tall:, :].reshape(1, ff, features).astype(f32)
-    outs_two = after(outs_two, grad_tokens)
-    sides = fold(sides, 1, outs_two)
-    outs += [jnp.concatenate([one, two], axis=0) for one, two in zip(outs_one, outs_two)]
-    rows = features // data
-    part = jnp.concatenate([v.reshape(rows, -1) for v in sides], axis=1)
-    local_norm_attn = after(local_norm_attn, part)
-    first, second = joined(chip_sum(part))
-    out_half = features // 2
-    grad_out = jnp.concatenate([first[:, :out_half], second[:, :out_half]], axis=1).astype(f32)
-    first, second = first[:, out_half:].astype(f32), second[:, out_half:].astype(f32)
-    kept = query_width - qkv_half
-    grad_query = jnp.concatenate([first, second[:, :kept]], axis=1)
-    grad_key = second[:, kept:kept + kv_width]
-    grad_value = second[:, kept + kv_width:]
-
+    whole = lax.all_gather(expert_sum, "dp", axis=0, tiled=True)
+    outs += [jnp.concatenate(v, axis=0) for v in zip(outs_one, outs_two, outs_three)]
     routed = outs[0].astype(f32)
     for part in outs[1:]:
         routed = routed + part.astype(f32)
     block_out = (hidden_one + routed).astype(bf16)
-
-    local_router = local_router[:3 * experts].reshape(3, experts, features).sum(0)
-    small = jnp.concatenate([local_router, local_norm_attn, local_norm_moe], axis=0)
-    small = small + swap(small)
-    for step in range(data.bit_length() - 1):
-        small = small + dp_xor(small, 1 << step)
-    step = 1
-    while step < chips:
-        small = small + chip_xor(small, step)
-        step *= 2
+    grad_gate, grad_up, grad_down = widened(whole, data)
+    out_part = chip_sum(out_part, lambda v: v, (), ())
+    qkv_part = chip_sum(qkv_part, beside, (block_out,), (grad_gate,))
+    (grad_out,) = joined(place, out_part, swap(out_part), (features,))
+    qkv_part = after(qkv_part, grad_out)
+    qkv_other = swap(qkv_part)
+    grad_query, grad_key, grad_value = joined(
+        place, qkv_part, qkv_other, (query_width, kv_width, kv_width)
+    )
+    while small_steps:
+        small = small + small_steps.pop(0)(small)
     grad_router = small[:experts].T
     grad_norm_attn = small[experts]
     grad_norm_moe = small[experts + 1]
@@ -1049,9 +1160,9 @@
         grad_value,
         grad_out,
         grad_router,
-        grad_gate,
-        grad_up,
-        grad_down,
+        grad_gate[None],
+        grad_up[None],
+        grad_down[None],
     )
 
 

time: 645 us -> 592 us (0.918)
  waiting for transfers between devices: 228 us -> 156 us
  Pallas kernels: 254 us -> 284 us
  other arithmetic: 57.3 us -> 31.9 us
  starting transfers between devices: 42.9 us -> 54.4 us
    ppermute x5, waiting for transfers between devices: 60.3 us -> 25 us  [across(): lax.ppermute(v, 'expert', [(j, (j + experts // 2) % experts) for j in ran...]
    pallas_call x0 -> x7, Pallas kernels: none -> 29.5 us  [the longest x2 9.28 us: fold_first(): pl.pallas_call(fold_first_kernel, out_shape=[jax.ShapeDtypeStruct((2, row...]
    ppermute x5 -> x7, waiting for transfers between devices: 50.5 us -> 31.3 us  [shift(): return lax.ppermute(v, 'expert', [(j, to(j)) for j in range(experts)])]
    ppermute x13 -> x17, waiting for transfers between devices: 46.8 us -> 29 us  [dp_xor(): return lax.ppermute(v, 'dp', [(j, j ^ k) for j in range(data)])]
    convert_element_type x12 -> x8, other arithmetic: 24.3 us -> 7.59 us  [the longest x4 4.43 us: folded(): (keep.astype(f32) + got.astype(f32)).astype(bf16)]
    ppermute x6 -> x10, starting transfers between devices: 7.17 us -> 15.6 us  [chip_xor(): lax.ppermute(v, 'expert', [(j, (j // 2 ^ step) * 2 + j % 2) for j in rang...]
    unnamed x65 -> x97, local copies, waits for them, and re-layouts: 4.95 us -> 12.8 us
    ppermute x6 -> x10, waiting for transfers between devices: 44.3 us -> 36.9 us  [chip_xor(): lax.ppermute(v, 'expert', [(j, (j // 2 ^ step) * 2 + j % 2) for j in rang...]
  transfers between devices with their start and end apart: 49 -> 61, of which waited for: 26 -> 30; matrix products, arithmetic and copies ran while one was open for 12% -> 10% of each run, Pallas kernels for 32% -> 39%
where the time goes in v3:
time: 592 us; the launch traced here: 587 us
  Pallas kernels  284 us (48%)
  waiting for transfers between devices  156 us (26%)
  starting transfers between devices  54.4 us (9%)
  local copies, waits for them, and re-layouts  46.4 us (8%)
  other arithmetic  31.9 us (5%)
  between operations  14.8 us (2%)
    pallas_call x4, Pallas kernels, expert_call(): pl.pallas_call(functools.partial(expert_kernel, experts, slots, base, dat...  127 us
    ppermute x10, waiting for transfers between devices, chip_xor(): lax.ppermute(v, 'expert', [(j, (j // 2 ^ step) * 2 + j % 2) for j in rang...  36.9 us
    pallas_call x2, Pallas kernels, weight_gradient_call(): pl.pallas_call(functools.partial(weight_gradient_kernel, data), out_shape...  35.9 us
    ppermute x18, waiting for transfers between devices, swap(): return lax.ppermute(v, 'expert', [(j, j ^ 1) for j in range(experts)])  33.4 us
    ppermute x7, waiting for transfers between devices, shift(): return lax.ppermute(v, 'expert', [(j, to(j)) for j in range(experts)])  31.3 us
    ppermute x17, waiting for transfers between devices, dp_xor(): return lax.ppermute(v, 'dp', [(j, j ^ k) for j in range(data)])  29 us
    ppermute x5, waiting for transfers between devices, across(): lax.ppermute(v, 'expert', [(j, (j + experts // 2) % experts) for j in ran...  25 us
    pallas_call x1, Pallas kernels, attend_back_call(): pl.pallas_call(functools.partial(attend_back_kernel, rows, 128), out_shap...  24.6 us
  transfers between devices with their start and end apart: 61, of which 30 were waited for; matrix products, arithmetic and copies ran while one was open for 10% of the time, Pallas kernels for 39%

profile of v3, /device:TPU:0, one launch (start us, length us, event | category | flops | bytes accessed | tf_op | source)
XLA Modules:
  0.0 587.4 jit_solution(8292793815486313612)
XLA Ops:
  24.6 9.9 %scatter_custom_fusion = s32[2560]{0:T(1024)S(1)} fusion(s32[2560]{0:T(1024)S(1)} %fusion.11, s32[2560]{0:T(1024)S(1)} %iota.7, s32[]{:T(128)} %constant.90.clone.1), kind=kCustom, calls=%fused_computation.72 | custom fusion | bytes 10244 | tf_op jit(solution)/shard_map/scatter | solution.py:884
  35.1 9.5 %collective-permute-done.1.refs_5_.refs_3_.refs_6_ = bf16[384,1792]{1,0:T(8,128)(2,1)S(1)} collective-permute-done((bf16[384,1792]{1,0:T(8,128)(2,1)}, bf16[384,1792]{1,0:T(8,128)(2,1)S(1)}, u32[]{:S(2)}, u32[]{:S(2)}) %collective-permute-start.1) | collective-permute-done | bytes 1376288 | tf_op jit(solution)/shard_map/ppermute | solution.py:947
  69.6 6.0 %collective-permute-done.8.refs_8_.refs_6_.refs_9_ = bf16[192,1792]{1,0:T(8,128)(2,1)S(1)} collective-permute-done((bf16[192,1792]{1,0:T(8,128)(2,1)S(1)}, bf16[192,1792]{1,0:T(8,128)(2,1)S(1)}, u32[]{:S(2)}, u32[]{:S(2)}) %collective-permute-start.8) | collective-permute-done | bytes 688160 | tf_op jit(solution)/shard_map/ppermute | solution.py:931
  85.9 18.9 %attend.1 = (bf16[640,1536]{1,0:T(8,128)(2,1)}, bf16[640,2048]{1,0:T(8,128)(2,1)}, bf16[640,1536]{1,0:T(8,128)(2,1)}, f32[640,128]{1,0:T(8,128)}) custom-call(s32[2]{0:T(128)} %pad_add_fusion.place, bf16[640,1536]{1,0:T(8,128)(2,1)} %tokens.5, f32[1,1536]{1,0:T(1,128)} %reshape.77.gain, s32[1,640]{1,0:T(1,128)} %segment_row.3, s32[640,1]{1,0:T(8,128)} %copy.78.segment_col, ...), custom_call_target="tpu_custom_call" | custom-call | flops 1000 | bytes 1000 | tf_op jit(solution)/shard_map/attend/pallas_call | solution.py:529
  104.8 10.7 %collective-permute-done.10.refs_6_.refs_8_ = bf16[224,1536]{1,0:T(8,128)(2,1)} collective-permute-done((bf16[224,1536]{1,0:T(8,128)(2,1)}, bf16[224,1536]{1,0:T(8,128)(2,1)}, u32[]{:S(2)}, u32[]{:S(2)}) %collective-permute-start.10) | collective-permute-done | bytes 688160 | tf_op jit(solution)/shard_map/ppermute | solution.py:941
  117.2 11.4 %route.1 = (f32[640,1536]{1,0:T(8,128)}, bf16[640,1664]{1,0:T(8,128)(2,1)}) custom-call(s32[2]{0:T(128)} %pad_add_fusion.place, bf16[640,1536]{1,0:T(8,128)(2,1)} %get-tuple-element.151.mixture, bf16[640,1536]{1,0:T(8,128)(2,1)} %tokens.5, f32[1,1536]{1,0:T(1,128)} %reshape.78.gain, bf16[1536,128]{1,0:T(8,128)(2,1)} %pad.13.router_weight, ...), custom_call_target="tpu_custom_call" | custom-call | flops 1000 | bytes 1000 | tf_op jit(solution)/shard_map/route/pallas_call | solution.py:657
  139.7 31.1 %expert_rows.4 = (bf16[1,640,1536]{2,1,0:T(8,128)(2,1)}, bf16[1,640,1536]{2,1,0:T(8,128)(2,1)}, bf16[1,640,1664]{2,1,0:T(8,128)(2,1)}, bf16[1,640,1664]{2,1,0:T(...) custom-call(s32[3]{0:T(128)} %pad_add_fusion.1.refs_0_, ...), custom_call_target="tpu_custom_call" | custom-call | flops 1000 | bytes 1000 | tf_op jit(solution)/shard_map/expert_rows/pallas_call | solution.py:297
  171.9 31.8 %expert_rows.5 = (bf16[1,640,1536]{2,1,0:T(8,128)(2,1)}, bf16[1,640,1536]{2,1,0:T(8,128)(2,1)}, bf16[1,640,1664]{2,1,0:T(8,128)(2,1)}, bf16[1,640,1664]{2,1,0:T(...) custom-call(s32[3]{0:T(128)} %pad_add_fusion.1.refs_0_, ...), custom_call_target="tpu_custom_call", output_to_operand_aliasing={{0}: (10, {}), {1}: (11, {}), {2}: (12, {}), {3}: (13, {})} | custom-call | flops 17179869184 | bytes 31457280 | tf_op jit(solution)/shard_map/expert_rows/pallas_call | solution.py:297
  211.1 31.3 %expert_rows.6 = (bf16[1,640,1536]{2,1,0:T(8,128)(2,1)}, bf16[1,640,1536]{2,1,0:T(8,128)(2,1)}, bf16[1,640,1664]{2,1,0:T(8,128)(2,1)}, bf16[1,640,1664]{2,1,0:T(...) custom-call(s32[3]{0:T(128)} %pad_add_fusion.1.refs_0_, ...), custom_call_target="tpu_custom_call", output_to_operand_aliasing={{4}: (12, {}), {5}: (13, {}), {6}: (14, {}), {7}: (15, {}),... | custom-call | flops 1000 | bytes 1000 | tf_op jit(solution)/shard_map/expert_rows/pallas_call | solution.py:297
  242.4 17.9 %expert_weight_gradients.2 = bf16[2304,1536]{1,0:T(8,128)(2,1)} custom-call(bf16[1,1472,1536]{2,1,0:T(8,128)(2,1)} %get-tuple-element.188.x_in, bf16[1,1472,768]{2,1,0:T(8,128)(2,1)} %get-tuple-element.189.gg_in, bf16[1,1472,768]{2,1,0:T(8,128)(2,1)} %get-tuple-element.190.gu_in, bf16[1,1472,768]{2,1,0:T(8,128)(2,1)} %get-tuple-element.191.h_in, ...), custom_call_target="tpu_custom_call" | custom-call | flops 1000 | bytes 1000 | tf_op jit(solution)/shard_map/expert_weight_gradients/pallas_call | solution.py:385
  260.4 32.3 %expert_rows.7 = (bf16[1,640,1536]{2,1,0:T(8,128)(2,1)}, bf16[1,640,1536]{2,1,0:T(8,128)(2,1)}, bf16[1,640,1664]{2,1,0:T(8,128)(2,1)}, bf16[1,640,1664]{2,1,0:T(...) custom-call(s32[3]{0:T(128)} %pad_add_fusion.1.refs_0_, ...), custom_call_target="tpu_custom_call", output_to_operand_aliasing={{0}: (10, {}), {1}: (11, {}), {2}: (12, {}), {3}: (13, {}),... | custom-call | flops 1000 | bytes 1000 | tf_op jit(solution)/shard_map/expert_rows/pallas_call | solution.py:297
  306.7 18.1 %expert_weight_gradients.3 = bf16[2304,1536]{1,0:T(8,128)(2,1)} custom-call(bf16[1,1472,1536]{2,1,0:T(8,128)(2,1)} %get-tuple-element.247.x_in, bf16[1,1472,768]{2,1,0:T(8,128)(2,1)} %get-tuple-element.248.gg_in, bf16[1,1472,768]{2,1,0:T(8,128)(2,1)} %get-tuple-element.249.gu_in, bf16[1,1472,768]{2,1,0:T(8,128)(2,1)} %get-tuple-element.250.h_in, ...), custom_call_target="tpu_custom_call" | custom-call | flops 1000 | bytes 1000 | tf_op jit(solution)/shard_map/expert_weight_gradients/pallas_call | solution.py:385
  324.8 25.2 %collective-permute-done.25.refs_2_ = bf16[640,1664]{1,0:T(8,128)(2,1)} collective-permute-done((bf16[640,1664]{1,0:T(8,128)(2,1)}, bf16[640,1664]{1,0:T(8,128)(2,1)}, u32[]{:S(2)}, u32[]{:S(2)}) %collective-permute-start.25) | collective-permute-done | bytes 2129952 | tf_op jit(solution)/shard_map/ppermute | solution.py:938
  352.3 22.2 %branch.1 = (f32[640,1536]{1,0:T(8,128)}, bf16[640,1536]{1,0:T(8,128)(2,1)}, bf16[1536,768]{1,0:T(8,128)(2,1)}, bf16[1536,768]{1,0:T(8,128)(2,1)}, f32[1,1536]{1,0:T(1,128)}, /*index=5*/f32[128,1536]{1,0:T(8,128)}) custom-call(s32[2]{0:T(128)} %pad_add_fusion.place, bf16[640,1536]{1,0:T(8,128)(2,1)} %cotangent.1, f32[640,1536]{1,0:T(8,128)} %get-tuple-element.153.hidden, ...), custom_call_target="tpu_custom_call" | custom-call | flops 1000 | bytes 1000 | tf_op jit(solution)/shard_map/branch/pallas_call | solution.py:738
  381.8 24.6 %attend_back.1 = (bf16[640,2048]{1,0:T(8,128)(2,1)}, bf16[1536,1024]{1,0:T(8,128)(2,1)}, bf16[1536,1024]{1,0:T(8,128)(2,1)}) custom-call(s32[2]{0:T(128)} %pad_add_fusion.place, s32[1,640]{1,0:T(1,128)} %segment_row.3, s32[640,1]{1,0:T(8,128)} %copy.78.segment_col, s32[1,640]{1,0:T(1,128)} %pad_row.3, bf16[640,2048]{1,0:T(8,128)(2,1)} %get-tuple-element.196.qkv, ...), custom_call_target="tpu_custom_call" | custom-call | flops 1000 | bytes 1000 | tf_op jit(solution)/shard_map/attend_back/pallas_call | solution.py:602
  409.2 5.9 %collective-permute-done.31.got = bf16[1536,1024]{1,0:T(8,128)(2,1)} collective-permute-done((bf16[1536,1024]{1,0:T(8,128)(2,1)}, bf16[1536,1024]{1,0:T(8,128)(2,1)}, u32[]{:S(2)}, u32[]{:S(2)}) %collective-permute-start.31) | collective-permute-done | bytes 3145760 | tf_op jit(solution)/shard_map/ppermute | solution.py:931
  430.5 14.9 %input_grad.1 = (f32[640,1536]{1,0:T(8,128)}, f32[1,1536]{1,0:T(1,128)}) custom-call(s32[2]{0:T(128)} %pad_add_fusion.place, bf16[640,1536]{1,0:T(8,128)(2,1)} %tokens.5, f32[1,1536]{1,0:T(1,128)} %reshape.77.gain, bf16[640,2048]{1,0:T(8,128)(2,1)} %get-tuple-element.221.grad, f32[640,1536]{1,0:T(8,128)} %get-tuple-element.194.grad_hidden, ...), custom_call_target="tpu_custom_call" | custom-call | flops 1000 | bytes 1000 | tf_op jit(solution)/shard_map/input_grad/pallas_call | solution.py:788
  445.4 6.1 %collective-permute-done.36 = bf16[192,1536]{1,0:T(8,128)(2,1)} collective-permute-done((bf16[192,1536]{1,0:T(8,128)(2,1)}, bf16[192,1536]{1,0:T(8,128)(2,1)}, u32[]{:S(2)}, u32[]{:S(2)}) %collective-permute-start.36) | collective-permute-done | bytes 589856 | tf_op jit(solution)/shard_map/ppermute | solution.py:941
  460.8 7.1 %collective-permute-done.39 = bf16[384,512]{1,0:T(8,128)(2,1)S(1)} collective-permute-done((bf16[384,512]{1,0:T(8,128)(2,1)}, bf16[384,512]{1,0:T(8,128)(2,1)S(1)}, u32[]{:S(2)}, u32[]{:S(2)}) %collective-permute-start.39) | collective-permute-done | bytes 393248 | tf_op jit(solution)/shard_map/ppermute | solution.py:947
  478.9 6.0 %collective-permute-done.49 = bf16[384,384]{1,0:T(8,128)(2,1)S(1)} collective-permute-done((bf16[384,384]{1,0:T(8,128)(2,1)}, bf16[384,384]{1,0:T(8,128)(2,1)S(1)}, u32[]{:S(2)}, u32[]{:S(2)}) %collective-permute-start.49) | collective-permute-done | bytes 294944 | tf_op jit(solution)/shard_map/ppermute | solution.py:947
  515.1 17.8 %collective-permute-done.53 = bf16[96,768]{1,0:T(8,128)(2,1)S(1)} collective-permute-done((bf16[96,768]{1,0:T(8,128)(2,1)S(1)}, bf16[96,768]{1,0:T(8,128)(2,1)S(1)}, u32[]{:S(2)}, u32[]{:S(2)}) %collective-permute-start.53) | collective-permute-done | bytes 147488 | tf_op jit(solution)/shard_map/ppermute | solution.py:944
  545.9 8.8 %collective-permute-done.45 = bf16[96,1024]{1,0:T(8,128)(2,1)S(1)} collective-permute-done((bf16[96,1024]{1,0:T(8,128)(2,1)S(1)}, bf16[96,1024]{1,0:T(8,128)(2,1)S(1)}, u32[]{:S(2)}, u32[]{:S(2)}) %collective-permute-start.45) | collective-permute-done | bytes 196640 | tf_op jit(solution)/shard_map/ppermute | solution.py:944
  558.6 8.4 %widened.1 = (f32[1536,768]{1,0:T(8,128)}, f32[1536,768]{1,0:T(8,128)}, f32[768,1536]{1,0:T(8,128)}) custom-call(bf16[2304,1536]{1,0:T(8,128)(2,1)} %all-gather.5.cloned.1.call-done.whole), custom_call_target="tpu_custom_call" | custom-call | flops 1000 | bytes 1000 | tf_op jit(solution)/shard_map/widened/pallas_call | solution.py:419
  569.7 5.7 collective-permute-done.47
  (287 shorter events, 190.9 us)
Async XLA Ops:
  7.2 163.7 %all-gather.3.cloned.1.call-start = ((), (), s32[]{:S(2)}) async-start(), calls=%async_computation.2 | async-start | bytes 5406720 | tf_op jit(solution)/shard_map/all_gather | solution.py:998
  11.2 33.4 %collective-permute-start.1 = (bf16[384,1792]{1,0:T(8,128)(2,1)}, bf16[384,1792]{1,0:T(8,128)(2,1)S(1)}, u32[]{:S(2)}, u32[]{:S(2)}) collective-permute-start(bf16[384,1792]{1,0:T(8,128)(2,1)} %pad_maximum_fusion), channel_id=1, source_target_pairs={{0,16},{8,24},{16,0},{24,8},{1,17},{9,25},{17,1},{25,9},{2,18},{10... | collective-permute-start | bytes 4128776 | tf_op jit(solution)/shard_map/ppermute | solution.py:947
  14.2 33.1 %collective-permute-start = (bf16[384,1792]{1,0:T(8,128)(2,1)}, bf16[384,1792]{1,0:T(8,128)(2,1)S(1)}, u32[]{:S(2)}, u32[]{:S(2)}) collective-permute-start(bf16[384,1792]{1,0:T(8,128)(2,1)} %pad_maximum_fusion), channel_id=1, source_target_pairs={{0,8},{8,0},{16,24},{24,16},{1,9},{9,1},{17,25},{25,17},{2,10},{10... | collective-permute-start | bytes 4128776 | tf_op jit(solution)/shard_map/ppermute | solution.py:947
  19.0 49.4 %collective-permute-start.4 = (bf16[352,1536]{1,0:T(8,128)(2,1)}, bf16[352,1536]{1,0:T(8,128)(2,1)}, u32[]{:S(2)}, u32[]{:S(2)}) collective-permute-start(bf16[352,1536]{1,0:T(8,128)(2,1)} %pad_maximum_fusion.1), channel_id=1, source_target_pairs={{0,4},{1,5},{2,6},{3,7},{4,0},{5,1},{6,2},{7,3},{8,12},{9,13},{10,... | collective-permute-start | bytes 3244040 | tf_op jit(solution)/shard_map/ppermute | solution.py:941
  23.0 42.6 %collective-permute-start.5 = (bf16[320,1536]{1,0:T(8,128)(2,1)}, bf16[320,1536]{1,0:T(8,128)(2,1)}, u32[]{:S(2)}, u32[]{:S(2)}) collective-permute-start(bf16[320,1536]{1,0:T(8,128)(2,1)} %get-tuple-element.271), channel_id=1, source_target_pairs={{0,2},{1,3},{2,0},{3,1},{4,6},{5,7},{6,4},{7,5},{8,10},{9,11},{10,... | collective-permute-start | bytes 2949128 | tf_op jit(solution)/shard_map/ppermute | solution.py:938
  77.8 272.2 %reduce-scatter.3.cloned.1.call-start = ((), (), s32[]{:S(2)}) async-start(), calls=%async_computation.3 | async-start | bytes 8847360 | tf_op jit(solution)/shard_map/reduce_scatter | solution.py:1045
  78.0 39.2 %collective-permute-start.12 = (bf16[640,1536]{1,0:T(8,128)(2,1)}, bf16[640,1536]{1,0:T(8,128)(2,1)}, u32[]{:S(2)}, u32[]{:S(2)}) collective-permute-start(bf16[640,1536]{1,0:T(8,128)(2,1)} %cotangent.1), channel_id=1, source_target_pairs={{0,1},{1,0},{2,3},{3,2},{4,5},{5,4},{6,7},{7,6},{8,9},{9,8},{10,11... | collective-permute-start | bytes 5898248 | tf_op jit(solution)/shard_map/ppermute | solution.py:931
  78.2 39.0 %collective-permute-start.11 = (bf16[320,1536]{1,0:T(8,128)(2,1)}, bf16[320,1536]{1,0:T(8,128)(2,1)S(1)}, u32[]{:S(2)}, u32[]{:S(2)}) collective-permute-start(bf16[320,1536]{1,0:T(8,128)(2,1)} %get-tuple-element.148), channel_id=1, source_target_pairs={{0,2},{1,3},{2,0},{3,1},{4,6},{5,7},{6,4},{7,5},{8,10},{9,11},{10,... | collective-permute-start | bytes 2949128 | tf_op jit(solution)/shard_map/ppermute | solution.py:938
  78.9 38.3 %collective-permute-start.13 = (bf16[320,1536]{1,0:T(8,128)(2,1)}, bf16[320,1536]{1,0:T(8,128)(2,1)}, u32[]{:S(2)}, u32[]{:S(2)}) collective-permute-start(bf16[320,1536]{1,0:T(8,128)(2,1)} %collective-permute-done.5.refs_3_), channel_id=1, source_target_pairs={{0,1},{1,0},{2,3},{3,2},{4,5},{5,4},{6,7},{7,6},{8,9},{9,8},{10,11... | collective-permute-start | bytes 2949128 | tf_op jit(solution)/shard_map/ppermute | solution.py:931
  81.0 34.5 %collective-permute-start.10 = (bf16[224,1536]{1,0:T(8,128)(2,1)}, bf16[224,1536]{1,0:T(8,128)(2,1)}, u32[]{:S(2)}, u32[]{:S(2)}) collective-permute-start(bf16[224,1536]{1,0:T(8,128)(2,1)} %pad_maximum_fusion.7), channel_id=1, source_target_pairs={{0,4},{1,5},{2,6},{3,7},{4,0},{5,1},{6,2},{7,3},{8,12},{9,13},{10,... | collective-permute-start | bytes 2064392 | tf_op jit(solution)/shard_map/ppermute | solution.py:941
  133.1 37.7 %collective-permute-start.15 = (bf16[224,1536]{1,0:T(8,128)(2,1)}, bf16[224,1536]{1,0:T(8,128)(2,1)S(1)}, u32[]{:S(2)}, u32[]{:S(2)}) collective-permute-start(bf16[224,1536]{1,0:T(8,128)(2,1)} %collective-permute-done.10.refs_6_.refs_8_), channel_id=1, source_target_pairs={{0,8},{8,0},{16,24},{24,16},{1,9},{9,1},{17,25},{25,17},{2,10},{10... | collective-permute-start | bytes 2064392 | tf_op jit(solution)/shard_map/ppermute | solution.py:947
  133.7 37.2 %collective-permute-start.16 = (bf16[224,1536]{1,0:T(8,128)(2,1)}, bf16[224,1536]{1,0:T(8,128)(2,1)S(1)}, u32[]{:S(2)}, u32[]{:S(2)}) collective-permute-start(bf16[224,1536]{1,0:T(8,128)(2,1)} %collective-permute-done.10.refs_6_.refs_8_), channel_id=1, source_target_pairs={{0,16},{8,24},{16,0},{24,8},{1,17},{9,25},{17,1},{25,9},{2,18},{10... | collective-permute-start | bytes 2064392 | tf_op jit(solution)/shard_map/ppermute | solution.py:947
  134.5 36.4 %collective-permute-start.17 = (bf16[224,1536]{1,0:T(8,128)(2,1)}, bf16[224,1536]{1,0:T(8,128)(2,1)}, u32[]{:S(2)}, u32[]{:S(2)}) collective-permute-start(bf16[224,1536]{1,0:T(8,128)(2,1)} %collective-permute-done.10.refs_6_.refs_8_), channel_id=1, source_target_pairs={{0,24},{8,16},{16,8},{24,0},{1,25},{9,17},{17,9},{25,1},{2,26},{10... | collective-permute-start | bytes 2064392 | tf_op jit(solution)/shard_map/ppermute | solution.py:947
  136.6 67.2 %collective-permute-start.18 = (bf16[640,1664]{1,0:T(8,128)(2,1)}, bf16[640,1664]{1,0:T(8,128)(2,1)S(1)}, u32[]{:S(2)}, u32[]{:S(2)}) collective-permute-start(bf16[640,1664]{1,0:T(8,128)(2,1)} %get-tuple-element.154.refs_1_.payload), channel_id=1, source_target_pairs={{0,2},{1,3},{2,0},{3,1},{4,6},{5,7},{6,4},{7,5},{8,10},{9,11},{10,... | collective-permute-start | bytes 6389768 | tf_op jit(solution)/shard_map/ppermute | solution.py:938
  260.3 211.0 %reduce-scatter.5.cloned.1.call-start = ((), (), s32[]{:S(2)}) async-start(), calls=%async_computation.4 | async-start | bytes 8847360 | tf_op jit(solution)/shard_map/reduce_scatter | solution.py:1045
  301.3 48.7 %collective-permute-start.25 = (bf16[640,1664]{1,0:T(8,128)(2,1)}, bf16[640,1664]{1,0:T(8,128)(2,1)}, u32[]{:S(2)}, u32[]{:S(2)}) collective-permute-start(bf16[640,1664]{1,0:T(8,128)(2,1)} %fusion), channel_id=1, source_target_pairs={{0,2},{1,3},{2,0},{3,1},{4,6},{5,7},{6,4},{7,5},{8,10},{9,11},{10,... | collective-permute-start | bytes 6389768 | tf_op jit(solution)/shard_map/ppermute | solution.py:938
  350.0 208.5 %all-gather.5.cloned.1.call-start = ((), (), s32[]{:S(2)}) async-start(), calls=%async_computation.5 | async-start | bytes 8847360 | tf_op jit(solution)/shard_map/all_gather | solution.py:1133
  378.0 31.2 %collective-permute-start.29 = (bf16[1536,768]{1,0:T(8,128)(2,1)}, bf16[1536,768]{1,0:T(8,128)(2,1)}, u32[]{:S(2)}, u32[]{:S(2)}) collective-permute-start(bf16[1536,768]{1,0:T(8,128)(2,1)} %get-tuple-element.206), channel_id=1, source_target_pairs={{0,1},{1,0},{2,3},{3,2},{4,5},{5,4},{6,7},{7,6},{8,9},{9,8},{10,11... | collective-permute-start | bytes 7077896 | tf_op jit(solution)/shard_map/ppermute | solution.py:931
  379.3 29.9 %collective-permute-start.30 = (bf16[208,1536]{1,0:T(8,128)(2,1)S(1)}, bf16[208,1536]{1,0:T(8,128)(2,1)S(1)}, u32[]{:S(2)}, u32[]{:S(2)}) collective-permute-start(bf16[208,1536]{1,0:T(8,128)(2,1)S(1)} %split.13), channel_id=1, source_target_pairs={{0,4},{1,5},{2,6},{3,7},{4,0},{5,1},{6,2},{7,3},{8,12},{9,13},{10,... | collective-permute-start | bytes 1916936 | tf_op jit(solution)/shard_map/ppermute | solution.py:941
  420.3 32.9 %collective-permute-start.32 = (bf16[2,384,512]{2,1,0:T(8,128)(2,1)}, bf16[2,384,512]{2,1,0:T(8,128)(2,1)S(1)}, u32[]{:S(2)}, u32[]{:S(2)}) collective-permute-start(bf16[2,384,512]{2,1,0:T(8,128)(2,1)} %get-tuple-element.209), channel_id=1, source_target_pairs={{0,16},{8,24},{16,0},{24,8},{1,17},{9,25},{17,1},{25,9},{2,18},{10... | collective-permute-start | bytes 2359304 | tf_op jit(solution)/shard_map/ppermute | solution.py:947
  420.9 32.3 %collective-permute-start.33 = (bf16[2,384,512]{2,1,0:T(8,128)(2,1)}, bf16[2,384,512]{2,1,0:T(8,128)(2,1)S(1)}, u32[]{:S(2)}, u32[]{:S(2)}) collective-permute-start(bf16[2,384,512]{2,1,0:T(8,128)(2,1)} %get-tuple-element.210), channel_id=1, source_target_pairs={{0,8},{8,0},{16,24},{24,16},{1,9},{9,1},{17,25},{25,17},{2,10},{10... | collective-permute-start | bytes 2359304 | tf_op jit(solution)/shard_map/ppermute | solution.py:947
  423.7 27.8 %collective-permute-start.36 = (bf16[192,1536]{1,0:T(8,128)(2,1)}, bf16[192,1536]{1,0:T(8,128)(2,1)}, u32[]{:S(2)}, u32[]{:S(2)}) collective-permute-start(bf16[192,1536]{1,0:T(8,128)(2,1)} %split.14), channel_id=1, source_target_pairs={{0,4},{1,5},{2,6},{3,7},{4,0},{5,1},{6,2},{7,3},{8,12},{9,13},{10,... | collective-permute-start | bytes 1769480 | tf_op jit(solution)/shard_map/ppermute | solution.py:941
  489.4 50.7 %collective-permute-start.22 = (bf16[640,1536]{1,0:T(8,128)(2,1)}, bf16[640,1536]{1,0:T(8,128)(2,1)}, u32[]{:S(2)}, u32[]{:S(2)}) collective-permute-start(bf16[640,1536]{1,0:T(8,128)(2,1)} %bitcast.16), channel_id=1, source_target_pairs={{0,1},{1,0},{2,3},{3,2},{4,5},{5,4},{6,7},{7,6},{8,9},{9,8},{10,11... | collective-permute-start | bytes 5898248 | tf_op jit(solution)/shard_map/ppermute | solution.py:931
  501.3 38.8 %collective-permute-start.37 = (bf16[320,1536]{1,0:T(8,128)(2,1)S(1)}, bf16[320,1536]{1,0:T(8,128)(2,1)S(1)}, u32[]{:S(2)}, u32[]{:S(2)}) collective-permute-start(bf16[320,1536]{1,0:T(8,128)(2,1)S(1)} %slice.72), channel_id=1, source_target_pairs={{0,2},{1,3},{2,0},{3,1},{4,6},{5,7},{6,4},{7,5},{8,10},{9,11},{10,... | collective-permute-start | bytes 2949128 | tf_op jit(solution)/shard_map/ppermute | solution.py:938
  (85 other events, 977.0 us)
Sparse Core Ops, SparseCore 0:
  77.9 53.0 all-gather.2
  260.5 74.3 reduce-scatter.2
  350.1 73.3 reduce-scatter.4
  474.9 79.0 all-gather.4

commit v4 on v3

--- a/solution.py
+++ b/solution.py
@@ -93,13 +93,11 @@
             for i, (source, target) in enumerate(pairs)
         ])
 
-    def input_copies(index):
-        parts = [cbuf.at[q, pl.ds(first, size)] for q in range(2) for first, size in cuts]
-        targets = [nbuf.at[0], nbuf.at[1]] + parts
-        return [
-            pltpu.make_async_copy(source, target, in_sem.at[i])
-            for i, (source, target) in enumerate(zip(sources[index], targets))
-        ]
+    def input_copies(index, q):
+        pairs = [(sources[index][q], nbuf.at[q])]
+        for part, (first, size) in zip(sources[index][2 + q * len(cuts):], cuts):
+            pairs.append((part, cbuf.at[q, pl.ds(first, size)]))
+        return [pltpu.make_async_copy(source, target, in_sem.at[q, i]) for i, (source, target) in enumerate(pairs)]
 
     def act_copies(chunk, place):
         at = pl.ds(pl.multiple_of(base + chunk * 2 * rows, 16), 2 * rows)
@@ -109,12 +107,10 @@
                 ((x, x_out), (gp, gp_out), (h, h_out), (gg, gg_out), (gu, gu_out)))
         ]
 
-    def partial_copies(chunk):
+    def partial_copies(chunk, q):
         return (
-            pltpu.make_async_copy(nbuf.at[0], pg_same.at[chunk], p_sem.at[0]),
-            pltpu.make_async_copy(nbuf.at[1], pg_other.at[chunk], p_sem.at[1]),
-            pltpu.make_async_copy(cbuf.at[0], po_same.at[chunk], p_sem.at[2]),
-            pltpu.make_async_copy(cbuf.at[1], po_other.at[chunk], p_sem.at[3]),
+            pltpu.make_async_copy(nbuf.at[q], (pg_same, pg_other)[q].at[chunk], p_sem.at[q, 0]),
+            pltpu.make_async_copy(cbuf.at[q], (po_same, po_other)[q].at[chunk], p_sem.at[q, 1]),
         )
 
     def dispatch(q):
@@ -146,9 +142,8 @@
             g = jnp.sum(jnp.where(mine, parts[place * rows:(place + 1) * rows], 0.0), axis=1, keepdims=True)
             gcol[place, q * rows:(q + 1) * rows, :] = jnp.broadcast_to(g, (rows, 128))
 
-        @pl.loop(0, 2)
-        def _(tile):
-            cols = lanes(tile * wide, wide)
+        for tile in range(2):
+            cols = slice(tile * wide, (tile + 1) * wide)
             found = mm(dmat[q], nbuf[q, :, cols]).astype(bf16)
             cot = mm(dmat[q], cbuf[q, :, cols])
             gc[q, :, cols] = cot.astype(bf16)
@@ -206,9 +201,8 @@
             tail_sum = tail_sum + nbuf[q, :, tail].astype(f32)
         nbuf[q, :, tail] = tail_sum.astype(bf16)
 
-        @pl.loop(0, 2)
-        def _(tile):
-            cols = lanes(tile * wide, wide)
+        for tile in range(2):
+            cols = slice(tile * wide, (tile + 1) * wide)
             back = mm(dtmat[q], gc[q, :, cols])
             out = mm(dtmat[q], sc[q, :, cols])
             if n_prev:
@@ -220,23 +214,24 @@
     def prev_copies(chunk):
         po0, po1, pg0, pg1 = prev
         return (
-            pltpu.make_async_copy(pg0.at[chunk], nbuf.at[0], in_sem.at[0]),
-            pltpu.make_async_copy(pg1.at[chunk], nbuf.at[1], in_sem.at[1]),
-            pltpu.make_async_copy(po0.at[chunk], cbuf.at[0], in_sem.at[2]),
-            pltpu.make_async_copy(po1.at[chunk], cbuf.at[1], in_sem.at[3]),
+            pltpu.make_async_copy(pg0.at[chunk], nbuf.at[0], in_sem.at[0, 0]),
+            pltpu.make_async_copy(pg1.at[chunk], nbuf.at[1], in_sem.at[1, 0]),
+            pltpu.make_async_copy(po0.at[chunk], cbuf.at[0], in_sem.at[0, 1]),
+            pltpu.make_async_copy(po1.at[chunk], cbuf.at[1], in_sem.at[1, 1]),
         )
 
-    for copy in input_copies(0):
-        copy.start()
+    for q in range(2):
+        for copy in input_copies(0, q):
+            copy.start()
     for copies in weight_copies:
         for copy in copies:
             copy.start()
 
     @pl.loop(0, chunks)
     def _(chunk):
-        for copy in input_copies(0):
-            copy.wait()
         for q in range(2):
+            for copy in input_copies(0, q):
+                copy.wait()
             dispatch(q)
         if n_prev:
             for copy in prev_copies(chunk):
@@ -256,19 +251,21 @@
                 copy.wait()
         for q in range(2):
             combine(q)
-        for copy in partial_copies(chunk):
-            copy.start()
+            for copy in partial_copies(chunk, q):
+                copy.start()
         for place in range(count):
             for copy in act_copies(chunk, place):
                 copy.wait()
-        for copy in partial_copies(chunk):
-            copy.wait()
+        for q in range(2):
+            for copy in partial_copies(chunk, q):
+                copy.wait()
 
         for index in range(1, chunks):
             @pl.when(chunk + 1 == index)
             def _():
-                for copy in input_copies(index):
-                    copy.start()
+                for q in range(2):
+                    for copy in input_copies(index, q):
+                        copy.start()
 
 
 def expert_call(hosted, slots, sources, weights, prev, saved, base, total, experts, rows, data, pieces, cost):
@@ -323,9 +320,9 @@
             pltpu.VMEM((count, many, 128), f32),
             pltpu.VMEM((extra, tokens), f32),
             pltpu.SemaphoreType.DMA((count, 3 * max(1, len(pieces)))),
-            pltpu.SemaphoreType.DMA((max(4, 2 + 2 * len(cuts)),)),
+            pltpu.SemaphoreType.DMA((2, 1 + len(cuts))),
             pltpu.SemaphoreType.DMA((count, 5)),
-            pltpu.SemaphoreType.DMA((4,)),
+            pltpu.SemaphoreType.DMA((2, 2)),
         ],
         compiler_params=params(),
         cost_estimate=cost,
@@ -333,16 +330,18 @@
     )(hosted, *flat, *weights, *prev, *saved)
 
 
-def weight_gradient_kernel(data, x_in, gg_in, gu_in, h_in, gp_in, out, x, gg, gu, h, gp, wide, down, sem, out_sem):
+def weight_gradient_kernel(data, x_in, gg_in, gu_in, h_in, gp_in, out, x, ggu, h, gp, wide, down, sem, out_sem):
     features, ff = x.shape[1], h.shape[1]
+    tall = 512
+    tall_f, tall_h = features // data, ff // data
+    step = tall_f + tall_h
     loads = [
         pltpu.make_async_copy(source.at[0], target, sem.at[i])
-        for i, (source, target) in enumerate(((gg_in, gg), (x_in, x), (gu_in, gu), (h_in, h), (gp_in, gp)))
+        for i, (source, target) in enumerate((
+            (gg_in, ggu.at[:, pl.ds(0, ff)]), (gu_in, ggu.at[:, pl.ds(ff, ff)]), (x_in, x), (h_in, h), (gp_in, gp)))
     ]
     for copy in loads:
         copy.start()
-    tall_f, tall_h = features // data, ff // data
-    step = tall_f + tall_h
     stores = [
         pltpu.make_async_copy(wide.at[pl.ds(d * tall_f, tall_f)], out.at[pl.ds(d * step, tall_f)], out_sem.at[2 * d])
         for d in range(data)
@@ -353,25 +352,21 @@
     ]
     for copy in loads[:3]:
         copy.wait()
-    tall = 256
 
     @pl.loop(0, features // tall)
     def _(tile):
-        cols = lanes(tile * tall, tall)
         at = pl.ds(pl.multiple_of(tile * tall, tall), tall)
-        wide[at, :ff] = mm_tn(x[:, cols], gg[...]).astype(bf16)
-        wide[at, ff:] = mm_tn(x[:, cols], gu[...]).astype(bf16)
+        wide[at, :] = mm_tn(x[:, lanes(tile * tall, tall)], ggu[...]).astype(bf16)
 
     for copy in stores[:data]:
         copy.start()
     for copy in loads[3:]:
         copy.wait()
 
-    @pl.loop(0, ff // tall)
+    @pl.loop(0, ff // (tall // 2))
     def _(tile):
-        cols = lanes(tile * tall, tall)
-        at = pl.ds(pl.multiple_of(tile * tall, tall), tall)
-        down[at, :] = mm_tn(h[:, cols], gp[...]).astype(bf16)
+        at = pl.ds(pl.multiple_of(tile * 256, 256), 256)
+        down[at, :] = mm_tn(h[:, lanes(tile * 256, 256)], gp[...]).astype(bf16)
 
     for copy in stores[data:]:
         copy.start()
@@ -389,8 +384,7 @@
         out_specs=pl.BlockSpec(memory_space=pl.ANY),
         scratch_shapes=[
             pltpu.VMEM((slots, features), bf16),
-            pltpu.VMEM((slots, ff), bf16),
-            pltpu.VMEM((slots, ff), bf16),
+            pltpu.VMEM((slots, 2 * ff), bf16),
             pltpu.VMEM((slots, ff), bf16),
             pltpu.VMEM((slots, features), bf16),
             pltpu.VMEM((features, 2 * ff), bf16),
@@ -544,11 +538,13 @@
     )(place, tokens, gain, segments, segment_columns, pads, *own, *flat)
 
 
-def attend_back_kernel(tokens_total, block, place, segment_row, segment_col, pad_row, qkv, totals, given, normed,
-                       grad, keep, give, grad_keys, grad_values):
+def attend_back_kernel(tokens_total, block, place, segment_row, segment_col, pad_row, qkv, totals, given, normed_in,
+                       grad_out, keep_out, give_out, grad_keys, grad_values, normed, grad, keep, give, sem, out_sem):
     width = QUERY_HEADS * HEAD_SIZE
     kv_width = KEY_VALUE_HEADS * HEAD_SIZE
     segment_of_row, segment_of_col, pad = segment_row[...], segment_col[...], pad_row[...]
+    normed_load = pltpu.make_async_copy(normed_in, normed, sem)
+    normed_load.start()
 
     @pl.loop(0, KEY_VALUE_HEADS)
     def _(c):
@@ -585,7 +581,17 @@
         grad[:, lanes(width + c * HEAD_SIZE, HEAD_SIZE)] = (grad_keys[...] * SCORE_SCALE).astype(bf16)
         grad[:, lanes(width + kv_width + c * HEAD_SIZE, HEAD_SIZE)] = grad_values[...].astype(bf16)
 
+    grad_store = pltpu.make_async_copy(grad, grad_out, out_sem.at[0])
+    grad_store.start()
+    normed_load.wait()
     tall = 256
+
+    def stores(tile):
+        at = pl.ds(pl.multiple_of(tile * tall, tall), tall)
+        return (
+            pltpu.make_async_copy(keep.at[at], keep_out.at[at], out_sem.at[1 + 2 * tile]),
+            pltpu.make_async_copy(give.at[at], give_out.at[at], out_sem.at[2 + 2 * tile]),
+        )
 
     @pl.loop(0, normed.shape[1] // tall)
     def _(tile):
@@ -593,6 +599,15 @@
         at = pl.ds(pl.multiple_of(tile * tall, tall), tall)
         for core, out in ((place[1], keep), (1 - place[1], give)):
             out[at, :] = mm_tn(normed[:, cols], grad[:, lanes(core * keep.shape[1], keep.shape[1])]).astype(bf16)
+        for copy in stores(tile):
+            copy.start()
+
+    grad_store.wait()
+
+    @pl.loop(0, normed.shape[1] // tall)
+    def _(tile):
+        for copy in stores(tile):
+            copy.wait()
 
 
 def attend_back_call(place, segments, segment_columns, pads, qkv, totals, given, normed):
@@ -602,9 +617,18 @@
     return pl.pallas_call(
         functools.partial(attend_back_kernel, rows, 128),
         out_shape=[shape((rows, width), bf16)] + [shape((features, width // 2), bf16)] * 2,
-        in_specs=specs("s" + "v" * 7),
-        out_specs=specs("vvv"),
-        scratch_shapes=[pltpu.VMEM((rows, HEAD_SIZE), f32), pltpu.VMEM((rows, HEAD_SIZE), f32)],
+        in_specs=specs("s" + "v" * 6 + "a"),
+        out_specs=specs("aaa"),
+        scratch_shapes=[
+            pltpu.VMEM((rows, HEAD_SIZE), f32),
+            pltpu.VMEM((rows, HEAD_SIZE), f32),
+            pltpu.VMEM((rows, features), bf16),
+            pltpu.VMEM((rows, width), bf16),
+            pltpu.VMEM((features, width // 2), bf16),
+            pltpu.VMEM((features, width // 2), bf16),
+            pltpu.SemaphoreType.DMA,
+            pltpu.SemaphoreType.DMA((1 + 2 * (features // 256),)),
+        ],
         compiler_params=params(),
         cost_estimate=COST,
         name="attend_back",
@@ -669,89 +693,160 @@
     )(place, mixture, tokens, gain, router_weight, slots, *own, *flat)
 
 
-def branch_kernel(experts, n_back, n_own, n_pairs, place, cotangent, hidden, payload, gain, router_weight,
-                  mixture, *refs):
+def branch_kernel(experts, n_back, n_own, n_pairs, place, gain, router_weight, cotangent, hidden, payload, mixture_in, *refs):
     backs, refs = refs[:n_back], refs[n_back:]
     own = refs[:n_own]
     flat = refs[n_own:n_own + 2 * n_pairs]
     pieces = [(flat[2 * k], flat[2 * k + 1]) for k in range(n_pairs)]
-    grad_hidden, given, keep, give, local_gain, local_router, weight, branch, sem = refs[n_own + 2 * n_pairs:]
+    grad_hidden, given, keep_out, give_out, local_gain, local_router = refs[n_own + 2 * n_pairs:][:6]
+    (weight, branch, mixture, cot_buf, hidden_buf, payload_buf, back_buf, keep, give, given_buf,
+     sem, mix_sem, in_sem, out_sem, sum_sem) = refs[n_own + 2 * n_pairs + 6:]
+    parts, short = cot_buf.shape[0], cot_buf.shape[1]
+    features = cot_buf.shape[2]
+    extra = payload_buf.shape[2] - features
+    wide_rows = mixture.shape[1]
+
+    def loads(part):
+        at = pl.ds(pl.multiple_of(part * short, 16), short)
+        pairs = [(ref, back_buf.at[part, i]) for i, ref in enumerate(backs)]
+        pairs += [(hidden, hidden_buf.at[part]), (payload, payload_buf.at[part]), (cotangent, cot_buf.at[part])]
+        return [
+            pltpu.make_async_copy(source.at[at], target, in_sem.at[part, i]) for i, (source, target) in enumerate(pairs)
+        ]
+
+    def hidden_store(part):
+        at = pl.ds(pl.multiple_of(part * short, 16), short)
+        return pltpu.make_async_copy(hidden_buf.at[part], grad_hidden.at[at], out_sem.at[part])
+
+    for part in range(parts):
+        for copy in loads(part):
+            copy.start()
+    mixture_load = pltpu.make_async_copy(mixture_in, mixture, mix_sem)
+    mixture_load.start()
     copies = piece_copies(place, own, pieces, (QUERY_HEADS + 2 * KEY_VALUE_HEADS) * HEAD_SIZE // 2, weight, sem)
     for copy in copies:
         copy.start()
-    rows, features = cotangent.shape
-    extra = payload.shape[1] - features
-
-    def arrived(cols):
-        total = backs[0][:, cols].astype(f32)
-        for ref in backs[1:]:
-            total = total + ref[:, cols].astype(f32)
-        return total
+    local_gain[...] = jnp.zeros_like(local_gain)
+    local_router[...] = jnp.zeros_like(local_router)
 
     def three(value):
         width = value.shape[1]
         return (value + pltpu.roll(value, width - experts, 1)
                 + pltpu.roll(value, width - 2 * experts, 1))
 
-    lane = lax.broadcasted_iota(jnp.int32, (rows, extra), 1)
-    router = jnp.where(lane < experts, three(payload[:, features:].astype(f32)), 0.0)
-    select = jnp.where(lane < experts, three(arrived(slice(features, features + extra))), 0.0)
-    logits = router * (select - jnp.sum(router * select, axis=1, keepdims=True))
-    high, middle, low = split_three(logits)
-    packed = high.astype(f32) + pltpu.roll(middle.astype(f32), experts, 1)
-    packed = (packed + pltpu.roll(low.astype(f32), 2 * experts, 1)).astype(bf16)
-    grad_normed = arrived(slice(0, features)) + mm_nt(packed, router_weight[...])
-    local_router[...] = mm_tn(packed, payload[:, :features])
-    value = hidden[...]
-    inverse = lax.rsqrt(jnp.mean(value * value, axis=1, keepdims=True) + epsilon)
-    along = grad_normed * value
-    local_gain[...] = jnp.sum(along * inverse, axis=0, keepdims=True)
-    mean = jnp.mean(along * gain[...], axis=1, keepdims=True)
-    total = cotangent[...].astype(f32) + inverse * (grad_normed * gain[...]) - value * (inverse * inverse * inverse * mean)
-    grad_hidden[...] = total
-    branch[...] = total.astype(bf16)
+    @pl.loop(0, parts)
+    def _(part):
+        for copy in loads(part):
+            copy.wait()
+
+        def arrived(cols):
+            total = back_buf[part, 0, :, cols].astype(f32)
+            for i in range(1, n_back):
+                total = total + back_buf[part, i, :, cols].astype(f32)
+            return total
+
+        lane = lax.broadcasted_iota(jnp.int32, (short, extra), 1)
+        router = jnp.where(lane < experts, three(payload_buf[part, :, features:].astype(f32)), 0.0)
+        select = jnp.where(lane < experts, three(arrived(slice(features, features + extra))), 0.0)
+        logits = router * (select - jnp.sum(router * select, axis=1, keepdims=True))
+        high, middle, low = split_three(logits)
+        packed = high.astype(f32) + pltpu.roll(middle.astype(f32), experts, 1)
+        packed = (packed + pltpu.roll(low.astype(f32), 2 * experts, 1)).astype(bf16)
+        grad_normed = arrived(slice(0, features)) + mm_nt(packed, router_weight[...])
+        local_router[...] += mm_tn(packed, payload_buf[part, :, :features])
+        value = hidden_buf[part]
+        inverse = lax.rsqrt(jnp.mean(value * value, axis=1, keepdims=True) + epsilon)
+        along = grad_normed * value
+        local_gain[...] += jnp.sum(along * inverse, axis=0, keepdims=True)
+        mean = jnp.mean(along * gain[...], axis=1, keepdims=True)
+        total = (cot_buf[part].astype(f32) + inverse * (grad_normed * gain[...])
+                 - value * (inverse * inverse * inverse * mean))
+        hidden_buf[part] = total
+        branch[pl.ds(pl.multiple_of(part * short, 16), short), :] = total.astype(bf16)
+        hidden_store(part).start()
+
+    mixture_load.wait()
     tall = 256
 
-    @pl.loop(0, mixture.shape[1] // tall)
+    def sum_stores(tile):
+        at = pl.ds(pl.multiple_of(tile * tall, tall), tall)
+        return (
+            pltpu.make_async_copy(keep.at[at], keep_out.at[at], sum_sem.at[tile, 0]),
+            pltpu.make_async_copy(give.at[at], give_out.at[at], sum_sem.at[tile, 1]),
+        )
+
+    @pl.loop(0, wide_rows // tall)
     def _(tile):
         cols = lanes(tile * tall, tall)
         at = pl.ds(pl.multiple_of(tile * tall, tall), tall)
         for core, out in ((place[1], keep), (1 - place[1], give)):
             out[at, :] = mm_tn(mixture[:, cols], branch[:, lanes(core * keep.shape[1], keep.shape[1])]).astype(bf16)
+        for copy in sum_stores(tile):
+            copy.start()
 
     for copy in copies:
         copy.wait()
-    wide = mixture.shape[1] // 2
+    wide = wide_rows // 2
+
+    def given_store(tile):
+        cols = lanes(tile * wide, wide)
+        return pltpu.make_async_copy(given_buf.at[:, cols], given.at[:, cols], out_sem.at[parts + tile])
 
     @pl.loop(0, 2)
     def _(tile):
         at = pl.ds(pl.multiple_of(tile * wide, 128), wide)
-        given[:, lanes(tile * wide, wide)] = mm_nt(branch[...], weight[at, :]).astype(bf16)
+        given_buf[:, lanes(tile * wide, wide)] = mm_nt(branch[...], weight[at, :]).astype(bf16)
+        given_store(tile).start()
+
+    for part in range(parts):
+        hidden_store(part).wait()
+
+    @pl.loop(0, wide_rows // tall)
+    def _(tile):
+        for copy in sum_stores(tile):
+            copy.wait()
+
+    for tile in range(2):
+        given_store(tile).wait()
 
 
 def branch_call(place, cotangent, hidden, payload, gain, router_weight, mixture, backs, own, pieces, experts):
     rows, features = cotangent.shape
-    extra = payload.shape[1] - features
+    wide_n = payload.shape[1]
     mixed = mixture.shape[1]
+    parts = 4
+    short = rows // parts
     flat = [part for pair in pieces for part in pair]
     shape = jax.ShapeDtypeStruct
     return pl.pallas_call(
         functools.partial(branch_kernel, experts, len(backs), len(own), len(pieces)),
         out_shape=[
             shape((rows, features), f32), shape((rows, mixed), bf16), shape((mixed, features // 2), bf16),
-            shape((mixed, features // 2), bf16), shape((1, features), f32), shape((extra, features), f32),
+            shape((mixed, features // 2), bf16), shape((1, features), f32), shape((wide_n - features, features), f32),
         ],
-        in_specs=specs("s" + "v" * (6 + len(backs)) + "a" * (len(own) + len(flat))),
-        out_specs=specs("vvvvvv"),
+        in_specs=specs("svv" + "a" * (4 + len(backs) + len(own) + len(flat))),
+        out_specs=specs("aaaavv"),
         scratch_shapes=[
             pltpu.VMEM((mixed, features), bf16),
             pltpu.VMEM((rows, features), bf16),
+            pltpu.VMEM((rows, mixed), bf16),
+            pltpu.VMEM((parts, short, features), bf16),
+            pltpu.VMEM((parts, short, features), f32),
+            pltpu.VMEM((parts, short, wide_n), bf16),
+            pltpu.VMEM((parts, len(backs), short, wide_n), bf16),
+            pltpu.VMEM((mixed, features // 2), bf16),
+            pltpu.VMEM((mixed, features // 2), bf16),
+            pltpu.VMEM((rows, mixed), bf16),
             pltpu.SemaphoreType.DMA((len(own) + len(flat),)),
+            pltpu.SemaphoreType.DMA,
+            pltpu.SemaphoreType.DMA((parts, len(backs) + 3)),
+            pltpu.SemaphoreType.DMA((parts + 2,)),
+            pltpu.SemaphoreType.DMA((mixed // 256, 2)),
         ],
         compiler_params=params(),
         cost_estimate=COST,
         name="branch",
-    )(place, cotangent, hidden, payload, gain, router_weight, mixture, *backs, *own, *flat)
+    )(place, gain, router_weight, cotangent, hidden, payload, mixture, *backs, *own, *flat)
 
 
 def input_grad_kernel(n_own, n_pairs, place, tokens, gain, grad, grad_hidden, *refs):
@@ -986,13 +1081,14 @@
     gain_one = norm_attn.reshape(1, features)
     gain_two = norm_moe.reshape(1, features)
     segment_columns = document_index.reshape(token_rows, 1)
-    ready, gain_one, gain_two, segment_columns = after(
-        (got, gain_one, gain_two, segment_columns),
+    quarter_rest, cot_rest = quarter[part_rows:], cotangent[token_half:]
+    ready, gain_one, gain_two, segment_columns, quarter_rest, cot_rest = after(
+        (got, gain_one, gain_two, segment_columns, quarter_rest, cot_rest),
         crossed_one, cot_first, slot_columns, router_weight, router_weight_three,
     )
     pieces = [(v, swap(v)) for v in ready]
-    crossed_two = across(after(quarter[part_rows:], crossed_one))
-    cot_second = [shift(after(cotangent[token_half:], pieces), k) for k in range(1, half)]
+    crossed_two = across(quarter_rest)
+    cot_second = [shift(after(cot_rest, pieces), k) for k in range(1, half)]
     cot_other = swap(after(cotangent, pieces))
     cot_first_other = [swap(after(v, pieces)) for v in cot_first]
     partner_one = lax.all_gather(after(crossed_one, pieces), "dp", axis=0, tiled=True)
@@ -1055,34 +1151,26 @@
         [w_out], pieces, experts,
     )
 
-    def chip_sum(part, beside, middle, last):
-        sizes = []
-        step = 1
-        chip = me // 2
-        while step < chips:
+    stages = chips.bit_length() - 1
+
+    def chip_stage(part, stage, *others):
+        there = stage < stages
+        step = 1 << (stage if there else 2 * stages - 1 - stage)
+        bit = lax.rem(me // 2 // step, 2)
+        if there:
             size = part.shape[0] // 2
-            bit = lax.rem(chip // step, 2)
             keep = lax.dynamic_slice_in_dim(part, bit * size, size, axis=0)
             give = lax.dynamic_slice_in_dim(part, (1 - bit) * size, size, axis=0)
-            part = (keep.astype(f32) + chip_xor(beside(give), step).astype(f32)).astype(bf16)
-            sizes.append((step, bit))
-            step *= 2
-        for step, bit in reversed(sizes):
-            part = after(beside(part), *middle)
-            other = chip_xor(part, step)
-            if step == 1:
-                other = after(other, *last)
-            part = jnp.concatenate(
-                [jnp.where(bit == 0, part, other), jnp.where(bit == 0, other, part)], axis=0
-            )
-        return part
-
-    first_cut, second_cut = partner_sum.shape[0] * 11 // 36, partner_sum.shape[0] * 24 // 36
-    thirds = jnp.split(partner_sum, (first_cut, second_cut), axis=0)
+            return (keep.astype(f32) + chip_xor(after(give, *others), step).astype(f32)).astype(bf16)
+        other = chip_xor(after(part, *others), step)
+        return jnp.concatenate([jnp.where(bit == 0, part, other), jnp.where(bit == 0, other, part)], axis=0)
+
+    rows = partner_sum.shape[0]
+    thirds = jnp.split(partner_sum, (11 * rows // 36, 22 * rows // 36, 31 * rows // 36), axis=0)
     arrived_one = across(after(thirds[0], backs))
     arrived_two = across(after(thirds[1], arrived_one, grad_hidden))
     given, out_give = after((given, out_give), arrived_one)
-    cuts = [0, 9 * token_rows // 40, token_rows // 2, token_rows]
+    cuts = [0, 9 * token_rows // 40, 18 * token_rows // 40, 27 * token_rows // 40, token_rows]
 
     def out_parts(index, *others):
         rows = slice(cuts[index], cuts[index + 1])
@@ -1097,56 +1185,64 @@
     )
     qkv_give, out_got = after((qkv_give, out_got), arrived_two, outs_two)
     arrived_three = across(after(thirds[2], arrived_two))
+    outs_three = out_parts(2, arrived_two, outs_two)
     out_folds = fold_first(place, out_keep, out_got, data)
     out_arrived = [dp_xor(out_folds[1], 2), dp_xor(out_folds[3], 1)]
     qkv_folds = fold_first(place, qkv_keep, swap(qkv_give), data)
     qkv_arrived = [dp_xor(qkv_folds[1], 2), dp_xor(qkv_folds[3], 1)]
     grad_tokens, local_norm_attn = input_grad_call(
-        place, tokens, gain_one, after(grad_qkv, qkv_folds, out_folds), grad_hidden, qkv_own, pieces
-    )
-    qkv_arrived, out_arrived, arrived_three = after((qkv_arrived, out_arrived, arrived_three), grad_tokens)
-    outs_three = out_parts(2, arrived_three)
+        place, tokens, gain_one, after(grad_qkv, qkv_folds, out_folds, arrived_three, outs_three), grad_hidden, qkv_own, pieces
+    )
+    arrived_four = across(after(thirds[3], arrived_three))
+    qkv_arrived, out_arrived = after((qkv_arrived, out_arrived), grad_tokens)
     local_router = local_router[:3 * experts].reshape(3, experts, features).sum(0)
     small = jnp.concatenate([local_router, local_norm_attn, local_norm_moe], axis=0)
-    small_steps = [swap] + [functools.partial(dp_xor, k=1 << i) for i in range(data.bit_length() - 1)]
-    small_steps += [functools.partial(chip_xor, step=1 << i) for i in range(chips.bit_length() - 1)]
-
-    def beside(large):
-        nonlocal small
-        large, small = after((large, small))
-        if small_steps:
-            small = small + small_steps.pop(0)(small)
-        return large
-
-    def folded(folds, arrived):
-        keep_a, give_a, keep_b, give_b = fold_second(place, folds[0], arrived[0], folds[2], arrived[1])
+    def folded(keep_a, give_a, keep_b, give_b):
         got_a, got_b = dp_xor(give_a, 1), dp_xor(give_b, 2)
         return jnp.concatenate([
             (keep.astype(f32) + got.astype(f32)).astype(bf16) for keep, got in ((keep_a, got_a), (keep_b, got_b))
         ], axis=1)
 
-    out_part = folded(out_folds, out_arrived)
-    qkv_part = beside(folded(qkv_folds, qkv_arrived))
-    arrived_three = after(arrived_three, out_part, qkv_part)
-    arrived = jnp.concatenate([arrived_one, arrived_two, arrived_three], axis=0)
+    qkv_folds = fold_second(place, qkv_folds[0], qkv_arrived[0], qkv_folds[2], qkv_arrived[1])
+    outs_four = out_parts(3, grad_tokens)
+    qkv_part = folded(*qkv_folds)
+    out_part = folded(*fold_second(place, out_folds[0], out_arrived[0], out_folds[2], out_arrived[1]))
+    arrived = jnp.concatenate([arrived_one, arrived_two, arrived_three, arrived_four], axis=0)
     expert_sum = (own_sum.astype(f32) + arrived.astype(f32)).astype(bf16)
+    expert_sum, out_part, qkv_part = after((expert_sum, out_part, qkv_part))
     whole = lax.all_gather(expert_sum, "dp", axis=0, tiled=True)
-    outs += [jnp.concatenate(v, axis=0) for v in zip(outs_one, outs_two, outs_three)]
+    for stage in range(2 * stages):
+        ahead = chip_stage(qkv_part, stage, *([outs_four] if stage == 2 else []))
+        if stage:
+            out_part = chip_stage(out_part, stage - 1, qkv_part)
+        qkv_part = ahead
+        if stage == 1:
+            small, qkv_part = after((small, qkv_part))
+    outs += [jnp.concatenate(v, axis=0) for v in zip(outs_one, outs_two, outs_three, outs_four)]
     routed = outs[0].astype(f32)
     for part in outs[1:]:
         routed = routed + part.astype(f32)
     block_out = (hidden_one + routed).astype(bf16)
-    grad_gate, grad_up, grad_down = widened(whole, data)
-    out_part = chip_sum(out_part, lambda v: v, (), ())
-    qkv_part = chip_sum(qkv_part, beside, (block_out,), (grad_gate,))
-    (grad_out,) = joined(place, out_part, swap(out_part), (features,))
-    qkv_part = after(qkv_part, grad_out)
+    out_part = chip_stage(out_part, 2 * stages - 1, qkv_part)
     qkv_other = swap(qkv_part)
+    small = small + swap(small)
+    arrived = [dp_xor(small, k) for k in range(1, data)]
     grad_query, grad_key, grad_value = joined(
         place, qkv_part, qkv_other, (query_width, kv_width, kv_width)
     )
-    while small_steps:
-        small = small + small_steps.pop(0)(small)
+    arrived, grad_query, block_out = after((arrived, grad_query, block_out))
+    for value in arrived:
+        small = small + value
+    (grad_out,) = joined(place, out_part, swap(out_part), (features,))
+    if chips <= 4:
+        arrived, grad_out = after(([chip_xor(small, k) for k in range(1, chips)], grad_out))
+        for value in arrived:
+            small = small + value
+    else:
+        for step in range(stages):
+            small = small + chip_xor(small, 1 << step)
+    whole, small, grad_out = after((whole, small, grad_out))
+    grad_gate, grad_up, grad_down = widened(whole, data)
     grad_router = small[:experts].T
     grad_norm_attn = small[experts]
     grad_norm_moe = small[experts + 1]

time: 592 us -> 575 us (0.971)
  Pallas kernels: 284 us -> 262 us
  starting transfers between devices: 54.4 us -> 62.2 us
  other arithmetic: 31.9 us -> 25.5 us
    ppermute x7 -> x8, waiting for transfers between devices: 31.3 us -> 50.7 us  [shift(): return lax.ppermute(v, 'expert', [(j, to(j)) for j in range(experts)])]
    pallas_call x4, Pallas kernels: 127 us -> 108 us  [expert_call(): pl.pallas_call(functools.partial(expert_kernel, experts, slots, base, dat...]
    ppermute x17 -> x18, waiting for transfers between devices: 29 us -> 13.3 us  [dp_xor(): return lax.ppermute(v, 'dp', [(j, j ^ k) for j in range(data)])]
    ppermute x10 -> x11, waiting for transfers between devices: 36.9 us -> 45.7 us  [chip_xor(): lax.ppermute(v, 'expert', [(j, (j // 2 ^ step) * 2 + j % 2) for j in rang...]
    unnamed x97 -> x95, local copies, waits for them, and re-layouts: 12.8 us -> 8.69 us
    ppermute x5 -> x6, waiting for transfers between devices: 25 us -> 22.1 us  [across(): lax.ppermute(v, 'expert', [(j, (j + experts // 2) % experts) for j in ran...]
    ppermute x17 -> x18, starting transfers between devices: 20.6 us -> 21.4 us  [dp_xor(): return lax.ppermute(v, 'dp', [(j, j ^ k) for j in range(data)])]
    ppermute x10 -> x11, starting transfers between devices: 15.6 us -> 16.1 us  [chip_xor(): lax.ppermute(v, 'expert', [(j, (j // 2 ^ step) * 2 + j % 2) for j in rang...]
  transfers between devices with their start and end apart: 61 -> 65, of which waited for: 30 -> 32; matrix products, arithmetic and copies ran while one was open for 10% -> 9% of each run, Pallas kernels for 39% -> 37%
where the time goes in v4:
time: 575 us; the launch traced here: 566 us
  Pallas kernels  262 us (46%)
  waiting for transfers between devices  161 us (28%)
  starting transfers between devices  62.2 us (11%)
  local copies, waits for them, and re-layouts  41.1 us (7%)
  other arithmetic  25.5 us (4%)
  between operations  14.8 us (3%)
    pallas_call x4, Pallas kernels, expert_call(): pl.pallas_call(functools.partial(expert_kernel, experts, slots, base, dat...  108 us
    ppermute x8, waiting for transfers between devices, shift(): return lax.ppermute(v, 'expert', [(j, to(j)) for j in range(experts)])  50.7 us
    ppermute x11, waiting for transfers between devices, chip_xor(): lax.ppermute(v, 'expert', [(j, (j // 2 ^ step) * 2 + j % 2) for j in rang...  45.7 us
    pallas_call x2, Pallas kernels, weight_gradient_call(): pl.pallas_call(functools.partial(weight_gradient_kernel, data), out_shape...  34.7 us
    ppermute x18, waiting for transfers between devices, swap(): return lax.ppermute(v, 'expert', [(j, j ^ 1) for j in range(experts)])  28.6 us
    pallas_call x1, Pallas kernels, attend_back_call(): pl.pallas_call(functools.partial(attend_back_kernel, rows, 128), out_shap...  22.4 us
    ppermute x6, waiting for transfers between devices, across(): lax.ppermute(v, 'expert', [(j, (j + experts // 2) % experts) for j in ran...  22.1 us
    ppermute x18, starting transfers between devices, dp_xor(): return lax.ppermute(v, 'dp', [(j, j ^ k) for j in range(data)])  21.4 us
  transfers between devices with their start and end apart: 65, of which 32 were waited for; matrix products, arithmetic and copies ran while one was open for 9% of the time, Pallas kernels for 37%

profile of v4, /device:TPU:0, one launch (start us, length us, event | category | flops | bytes accessed | tf_op | source)
XLA Modules:
  0.0 565.9 jit_solution(4524204390430027712)
XLA Ops:
  24.7 9.9 %scatter_custom_fusion = s32[2560]{0:T(1024)S(1)} fusion(s32[2560]{0:T(1024)S(1)} %fusion.9, s32[2560]{0:T(1024)S(1)} %iota.7, s32[]{:T(128)} %constant.110.clone.1), kind=kCustom, calls=%fused_computation.68 | custom fusion | bytes 10244 | tf_op jit(solution)/shard_map/scatter | solution.py:979
  40.2 5.8 %collective-permute-done.1.refs_5_.refs_3_.refs_6_ = bf16[384,1792]{1,0:T(8,128)(2,1)S(1)} collective-permute-done((bf16[384,1792]{1,0:T(8,128)(2,1)}, bf16[384,1792]{1,0:T(8,128)(2,1)S(1)}, u32[]{:S(2)}, u32[]{:S(2)}) %collective-permute-start.1) | collective-permute-done | bytes 1376288 | tf_op jit(solution)/shard_map/ppermute | solution.py:1042
  58.5 7.1 %collective-permute-done.5.refs_3_ = bf16[320,1536]{1,0:T(8,128)(2,1)} collective-permute-done((bf16[320,1536]{1,0:T(8,128)(2,1)}, bf16[320,1536]{1,0:T(8,128)(2,1)}, u32[]{:S(2)}, u32[]{:S(2)}) %collective-permute-start.5) | collective-permute-done | bytes 983072 | tf_op jit(solution)/shard_map/ppermute | solution.py:1033
  69.7 6.0 %collective-permute-done.8.refs_8_.refs_6_.refs_9_ = bf16[192,1792]{1,0:T(8,128)(2,1)S(1)} collective-permute-done((bf16[192,1792]{1,0:T(8,128)(2,1)S(1)}, bf16[192,1792]{1,0:T(8,128)(2,1)S(1)}, u32[]{:S(2)}, u32[]{:S(2)}) %collective-permute-start.8) | collective-permute-done | bytes 688160 | tf_op jit(solution)/shard_map/ppermute | solution.py:1026
  83.8 19.3 %attend.1 = (bf16[640,1536]{1,0:T(8,128)(2,1)}, bf16[640,2048]{1,0:T(8,128)(2,1)}, bf16[640,1536]{1,0:T(8,128)(2,1)}, f32[640,128]{1,0:T(8,128)}) custom-call(s32[2]{0:T(128)} %pad_add_fusion.place, bf16[640,1536]{1,0:T(8,128)(2,1)} %tokens.5, f32[1,1536]{1,0:T(1,128)} %reshape.77.gain, s32[1,640]{1,0:T(1,128)} %segment_row.3, s32[640,1]{1,0:T(8,128)} %copy.78.segment_col, ...), custom_call_target="tpu_custom_call" | custom-call | flops 1000 | bytes 1000 | tf_op jit(solution)/shard_map/attend/pallas_call | solution.py:523
  103.1 12.3 %collective-permute-done.10.refs_6_.refs_8_ = bf16[224,1536]{1,0:T(8,128)(2,1)} collective-permute-done((bf16[224,1536]{1,0:T(8,128)(2,1)}, bf16[224,1536]{1,0:T(8,128)(2,1)}, u32[]{:S(2)}, u32[]{:S(2)}) %collective-permute-start.10) | collective-permute-done | bytes 688160 | tf_op jit(solution)/shard_map/ppermute | solution.py:1036
  117.1 12.2 %route.1 = (f32[640,1536]{1,0:T(8,128)}, bf16[640,1664]{1,0:T(8,128)(2,1)}) custom-call(s32[2]{0:T(128)} %pad_add_fusion.place, bf16[640,1536]{1,0:T(8,128)(2,1)} %get-tuple-element.162.mixture.mixture_in, bf16[640,1536]{1,0:T(8,128)(2,1)} %tokens.5, f32[1,1536]{1,0:T(1,128)} %reshape.78.gain, bf16[1536,128]{1,0:T(8,128)(2,1)} %pad.13.router_weight, ...), custom_call_target="tpu_custom_call" | custom-call | flops 1000 | bytes 1000 | tf_op jit(solution)/shard_map/route/pallas_call | solution.py:681
  140.3 26.1 %expert_rows.4 = (bf16[1,640,1536]{2,1,0:T(8,128)(2,1)}, bf16[1,640,1536]{2,1,0:T(8,128)(2,1)}, bf16[1,640,1664]{2,1,0:T(8,128)(2,1)}, bf16[1,640,1664]{2,1,0:T(...) custom-call(s32[3]{0:T(128)} %pad_add_fusion.1.refs_0_, ...), custom_call_target="tpu_custom_call" | custom-call | flops 1000 | bytes 1000 | tf_op jit(solution)/shard_map/expert_rows/pallas_call | solution.py:294
  167.6 27.9 %expert_rows.5 = (bf16[1,640,1536]{2,1,0:T(8,128)(2,1)}, bf16[1,640,1536]{2,1,0:T(8,128)(2,1)}, bf16[1,640,1664]{2,1,0:T(8,128)(2,1)}, bf16[1,640,1664]{2,1,0:T(...) custom-call(s32[3]{0:T(128)} %pad_add_fusion.1.refs_0_, ...), custom_call_target="tpu_custom_call", output_to_operand_aliasing={{0}: (10, {}), {1}: (11, {}), {2}: (12, {}), {3}: (13, {})} | custom-call | flops 17179869184 | bytes 31457280 | tf_op jit(solution)/shard_map/expert_rows/pallas_call | solution.py:294
  202.8 27.8 %expert_rows.6 = (bf16[1,640,1536]{2,1,0:T(8,128)(2,1)}, bf16[1,640,1536]{2,1,0:T(8,128)(2,1)}, bf16[1,640,1664]{2,1,0:T(8,128)(2,1)}, bf16[1,640,1664]{2,1,0:T(...) custom-call(s32[3]{0:T(128)} %pad_add_fusion.1.refs_0_, ...), custom_call_target="tpu_custom_call", output_to_operand_aliasing={{4}: (12, {}), {5}: (13, {}), {6}: (14, {}), {7}: (15, {}),... | custom-call | flops 1000 | bytes 1000 | tf_op jit(solution)/shard_map/expert_rows/pallas_call | solution.py:294
  230.6 17.3 %expert_weight_gradients.2 = bf16[2304,1536]{1,0:T(8,128)(2,1)} custom-call(bf16[1,1472,1536]{2,1,0:T(8,128)(2,1)} %get-tuple-element.197.x_in, bf16[1,1472,768]{2,1,0:T(8,128)(2,1)} %get-tuple-element.198.gg_in, bf16[1,1472,768]{2,1,0:T(8,128)(2,1)} %get-tuple-element.199.gu_in, bf16[1,1472,768]{2,1,0:T(8,128)(2,1)} %get-tuple-element.200.h_in, ...), custom_call_target="tpu_custom_call" | custom-call | flops 1000 | bytes 1000 | tf_op jit(solution)/shard_map/expert_weight_gradients/pallas_call | solution.py:380
  248.1 25.9 %expert_rows.7 = (bf16[1,640,1536]{2,1,0:T(8,128)(2,1)}, bf16[1,640,1536]{2,1,0:T(8,128)(2,1)}, bf16[1,640,1664]{2,1,0:T(8,128)(2,1)}, bf16[1,640,1664]{2,1,0:T(...) custom-call(s32[3]{0:T(128)} %pad_add_fusion.1.refs_0_, ...), custom_call_target="tpu_custom_call", output_to_operand_aliasing={{0}: (10, {}), {1}: (11, {}), {2}: (12, {}), {3}: (13, {}),... | custom-call | flops 1000 | bytes 1000 | tf_op jit(solution)/shard_map/expert_rows/pallas_call | solution.py:294
  288.0 17.4 %expert_weight_gradients.3 = bf16[2304,1536]{1,0:T(8,128)(2,1)} custom-call(bf16[1,1472,1536]{2,1,0:T(8,128)(2,1)} %get-tuple-element.235.x_in, bf16[1,1472,768]{2,1,0:T(8,128)(2,1)} %get-tuple-element.236.gg_in, bf16[1,1472,768]{2,1,0:T(8,128)(2,1)} %get-tuple-element.237.gu_in, bf16[1,1472,768]{2,1,0:T(8,128)(2,1)} %get-tuple-element.238.h_in, ...), custom_call_target="tpu_custom_call" | custom-call | flops 1000 | bytes 1000 | tf_op jit(solution)/shard_map/expert_weight_gradients/pallas_call | solution.py:380
  305.4 26.5 %collective-permute-done.23.refs_2_ = bf16[640,1664]{1,0:T(8,128)(2,1)} collective-permute-done((bf16[640,1664]{1,0:T(8,128)(2,1)}, bf16[640,1664]{1,0:T(8,128)(2,1)}, u32[]{:S(2)}, u32[]{:S(2)}) %collective-permute-start.23) | collective-permute-done | bytes 2129952 | tf_op jit(solution)/shard_map/ppermute | solution.py:1033
  337.7 20.4 %branch.1 = (f32[640,1536]{1,0:T(8,128)}, bf16[640,1536]{1,0:T(8,128)(2,1)}, bf16[1536,768]{1,0:T(8,128)(2,1)}, bf16[1536,768]{1,0:T(8,128)(2,1)}, f32[1,1536]{1,0:T(1,128)}, /*index=5*/f32[128,1536]{1,0:T(8,128)}) custom-call(s32[2]{0:T(128)} %pad_add_fusion.place, f32[1,1536]{1,0:T(1,128)} %reshape.78.gain, bf16[1536,128]{1,0:T(8,128)(2,1)} %pad.14.router_weight, ...), custom_call_target="tpu_custom_call" | custom-call | flops 1000 | bytes 1000 | tf_op jit(solution)/shard_map/branch/pallas_call | solution.py:821
  362.8 22.4 %attend_back.1 = (bf16[640,2048]{1,0:T(8,128)(2,1)}, bf16[1536,1024]{1,0:T(8,128)(2,1)}, bf16[1536,1024]{1,0:T(8,128)(2,1)}) custom-call(s32[2]{0:T(128)} %pad_add_fusion.place, s32[1,640]{1,0:T(1,128)} %segment_row.3, s32[640,1]{1,0:T(8,128)} %copy.78.segment_col, s32[1,640]{1,0:T(1,128)} %pad_row.3, bf16[640,2048]{1,0:T(8,128)(2,1)} %get-tuple-element.193.qkv, ...), custom_call_target="tpu_custom_call" | custom-call | flops 1000 | bytes 1000 | tf_op jit(solution)/shard_map/attend_back/pallas_call | solution.py:617
  392.7 5.3 fold_first.2
  410.2 12.4 %collective-permute-done.32 = bf16[144,1536]{1,0:T(8,128)(2,1)} collective-permute-done((bf16[144,1536]{1,0:T(8,128)(2,1)}, bf16[144,1536]{1,0:T(8,128)(2,1)}, u32[]{:S(2)}, u32[]{:S(2)}) %collective-permute-start.32) | collective-permute-done | bytes 442400 | tf_op jit(solution)/shard_map/ppermute | solution.py:1033
  422.6 14.9 %input_grad.1 = (f32[640,1536]{1,0:T(8,128)}, f32[1,1536]{1,0:T(1,128)}) custom-call(s32[2]{0:T(128)} %pad_add_fusion.place, bf16[640,1536]{1,0:T(8,128)(2,1)} %tokens.5, f32[1,1536]{1,0:T(1,128)} %reshape.77.gain, bf16[640,2048]{1,0:T(8,128)(2,1)} %get-tuple-element.231.grad, f32[640,1536]{1,0:T(8,128)} %get-tuple-element.215.grad_hidden, ...), custom_call_target="tpu_custom_call" | custom-call | flops 1000 | bytes 1000 | tf_op jit(solution)/shard_map/input_grad/pallas_call | solution.py:883
  452.3 5.9 %collective-permute-done.41 = bf16[384,512]{1,0:T(8,128)(2,1)S(1)} collective-permute-done((bf16[384,512]{1,0:T(8,128)(2,1)}, bf16[384,512]{1,0:T(8,128)(2,1)S(1)}, u32[]{:S(2)}, u32[]{:S(2)}) %collective-permute-start.41) | collective-permute-done | bytes 393248 | tf_op jit(solution)/shard_map/ppermute | solution.py:1042
  467.2 11.4 %collective-permute-done.42 = bf16[192,1024]{1,0:T(8,128)(2,1)} collective-permute-done((bf16[192,1024]{1,0:T(8,128)(2,1)}, bf16[192,1024]{1,0:T(8,128)(2,1)}, u32[]{:S(2)}, u32[]{:S(2)}) %collective-permute-start.42) | collective-permute-done | bytes 393248 | tf_op jit(solution)/shard_map/ppermute | solution.py:1039
  482.1 11.3 %collective-permute-done.43 = bf16[96,1024]{1,0:T(8,128)(2,1)S(1)} collective-permute-done((bf16[96,1024]{1,0:T(8,128)(2,1)S(1)}, bf16[96,1024]{1,0:T(8,128)(2,1)S(1)}, u32[]{:S(2)}, u32[]{:S(2)}) %collective-permute-start.43) | collective-permute-done | bytes 196640 | tf_op jit(solution)/shard_map/ppermute | solution.py:1039
  501.3 7.1 %collective-permute-done.49 = bf16[96,1024]{1,0:T(8,128)(2,1)S(1)} collective-permute-done((bf16[96,1024]{1,0:T(8,128)(2,1)S(1)}, bf16[96,1024]{1,0:T(8,128)(2,1)S(1)}, u32[]{:S(2)}, u32[]{:S(2)}) %collective-permute-start.49) | collective-permute-done | bytes 196640 | tf_op jit(solution)/shard_map/ppermute | solution.py:1039
  550.8 8.4 %widened.1 = (f32[1536,768]{1,0:T(8,128)}, f32[1536,768]{1,0:T(8,128)}, f32[768,1536]{1,0:T(8,128)}) custom-call(bf16[2304,1536]{1,0:T(8,128)(2,1)} %all-gather.5.cloned.1.call-done.whole), custom_call_target="tpu_custom_call" | custom-call | flops 1000 | bytes 1000 | tf_op jit(solution)/shard_map/widened/pallas_call | solution.py:413
  (291 shorter events, 190.2 us)
Async XLA Ops:
  7.2 159.3 %all-gather.3.cloned.1.call-start = ((), (), s32[]{:S(2)}) async-start(), calls=%async_computation.2 | async-start | bytes 5406720 | tf_op jit(solution)/shard_map/all_gather | solution.py:1094
  11.2 36.1 %collective-permute-start = (bf16[384,1792]{1,0:T(8,128)(2,1)}, bf16[384,1792]{1,0:T(8,128)(2,1)S(1)}, u32[]{:S(2)}, u32[]{:S(2)}) collective-permute-start(bf16[384,1792]{1,0:T(8,128)(2,1)} %pad_maximum_fusion), channel_id=1, source_target_pairs={{0,8},{8,0},{16,24},{24,16},{1,9},{9,1},{17,25},{25,17},{2,10},{10... | collective-permute-start | bytes 4128776 | tf_op jit(solution)/shard_map/ppermute | solution.py:1042
  14.2 31.9 %collective-permute-start.1 = (bf16[384,1792]{1,0:T(8,128)(2,1)}, bf16[384,1792]{1,0:T(8,128)(2,1)S(1)}, u32[]{:S(2)}, u32[]{:S(2)}) collective-permute-start(bf16[384,1792]{1,0:T(8,128)(2,1)} %pad_maximum_fusion), channel_id=1, source_target_pairs={{0,16},{8,24},{16,0},{24,8},{1,17},{9,25},{17,1},{25,9},{2,18},{10... | collective-permute-start | bytes 4128776 | tf_op jit(solution)/shard_map/ppermute | solution.py:1042
  19.0 49.5 %collective-permute-start.4 = (bf16[352,1536]{1,0:T(8,128)(2,1)}, bf16[352,1536]{1,0:T(8,128)(2,1)}, u32[]{:S(2)}, u32[]{:S(2)}) collective-permute-start(bf16[352,1536]{1,0:T(8,128)(2,1)} %pad_maximum_fusion.1), channel_id=1, source_target_pairs={{0,4},{1,5},{2,6},{3,7},{4,0},{5,1},{6,2},{7,3},{8,12},{9,13},{10,... | collective-permute-start | bytes 3244040 | tf_op jit(solution)/shard_map/ppermute | solution.py:1036
  23.1 42.6 %collective-permute-start.5 = (bf16[320,1536]{1,0:T(8,128)(2,1)}, bf16[320,1536]{1,0:T(8,128)(2,1)}, u32[]{:S(2)}, u32[]{:S(2)}) collective-permute-start(bf16[320,1536]{1,0:T(8,128)(2,1)} %get-tuple-element.291), channel_id=1, source_target_pairs={{0,2},{1,3},{2,0},{3,1},{4,6},{5,7},{6,4},{7,5},{8,10},{9,11},{10,... | collective-permute-start | bytes 2949128 | tf_op jit(solution)/shard_map/ppermute | solution.py:1033
  77.9 254.0 %reduce-scatter.3.cloned.1.call-start = ((), (), s32[]{:S(2)}) async-start(), calls=%async_computation.3 | async-start | bytes 8847360 | tf_op jit(solution)/shard_map/reduce_scatter | solution.py:1141
  77.9 39.2 %collective-permute-start.12 = (bf16[640,1536]{1,0:T(8,128)(2,1)}, bf16[640,1536]{1,0:T(8,128)(2,1)}, u32[]{:S(2)}, u32[]{:S(2)}) collective-permute-start(bf16[640,1536]{1,0:T(8,128)(2,1)} %cotangent.1), channel_id=1, source_target_pairs={{0,1},{1,0},{2,3},{3,2},{4,5},{5,4},{6,7},{7,6},{8,9},{9,8},{10,11... | collective-permute-start | bytes 5898248 | tf_op jit(solution)/shard_map/ppermute | solution.py:1026
  78.1 39.0 %collective-permute-start.11 = (bf16[320,1536]{1,0:T(8,128)(2,1)}, bf16[320,1536]{1,0:T(8,128)(2,1)S(1)}, u32[]{:S(2)}, u32[]{:S(2)}) collective-permute-start(bf16[320,1536]{1,0:T(8,128)(2,1)} %get-tuple-element.159), channel_id=1, source_target_pairs={{0,2},{1,3},{2,0},{3,1},{4,6},{5,7},{6,4},{7,5},{8,10},{9,11},{10,... | collective-permute-start | bytes 2949128 | tf_op jit(solution)/shard_map/ppermute | solution.py:1033
  78.8 38.3 %collective-permute-start.13 = (bf16[320,1536]{1,0:T(8,128)(2,1)}, bf16[320,1536]{1,0:T(8,128)(2,1)S(1)}, u32[]{:S(2)}, u32[]{:S(2)}) collective-permute-start(bf16[320,1536]{1,0:T(8,128)(2,1)} %collective-permute-done.5.refs_3_), channel_id=1, source_target_pairs={{0,1},{1,0},{2,3},{3,2},{4,5},{5,4},{6,7},{7,6},{8,9},{9,8},{10,11... | collective-permute-start | bytes 2949128 | tf_op jit(solution)/shard_map/ppermute | solution.py:1026
  78.9 36.5 %collective-permute-start.10 = (bf16[224,1536]{1,0:T(8,128)(2,1)}, bf16[224,1536]{1,0:T(8,128)(2,1)}, u32[]{:S(2)}, u32[]{:S(2)}) collective-permute-start(bf16[224,1536]{1,0:T(8,128)(2,1)} %pad_maximum_fusion.6), channel_id=1, source_target_pairs={{0,4},{1,5},{2,6},{3,7},{4,0},{5,1},{6,2},{7,3},{8,12},{9,13},{10,... | collective-permute-start | bytes 2064392 | tf_op jit(solution)/shard_map/ppermute | solution.py:1036
  133.8 32.6 %collective-permute-start.15 = (bf16[224,1536]{1,0:T(8,128)(2,1)}, bf16[224,1536]{1,0:T(8,128)(2,1)S(1)}, u32[]{:S(2)}, u32[]{:S(2)}) collective-permute-start(bf16[224,1536]{1,0:T(8,128)(2,1)} %collective-permute-done.10.refs_6_.refs_8_), channel_id=1, source_target_pairs={{0,8},{8,0},{16,24},{24,16},{1,9},{9,1},{17,25},{25,17},{2,10},{10... | collective-permute-start | bytes 2064392 | tf_op jit(solution)/shard_map/ppermute | solution.py:1042
  134.4 32.2 %collective-permute-start.16 = (bf16[224,1536]{1,0:T(8,128)(2,1)}, bf16[224,1536]{1,0:T(8,128)(2,1)S(1)}, u32[]{:S(2)}, u32[]{:S(2)}) collective-permute-start(bf16[224,1536]{1,0:T(8,128)(2,1)} %collective-permute-done.10.refs_6_.refs_8_), channel_id=1, source_target_pairs={{0,16},{8,24},{16,0},{24,8},{1,17},{9,25},{17,1},{25,9},{2,18},{10... | collective-permute-start | bytes 2064392 | tf_op jit(solution)/shard_map/ppermute | solution.py:1042
  135.2 31.4 %collective-permute-start.17 = (bf16[224,1536]{1,0:T(8,128)(2,1)}, bf16[224,1536]{1,0:T(8,128)(2,1)}, u32[]{:S(2)}, u32[]{:S(2)}) collective-permute-start(bf16[224,1536]{1,0:T(8,128)(2,1)} %collective-permute-done.10.refs_6_.refs_8_), channel_id=1, source_target_pairs={{0,24},{8,16},{16,8},{24,0},{1,25},{9,17},{17,9},{25,1},{2,26},{10... | collective-permute-start | bytes 2064392 | tf_op jit(solution)/shard_map/ppermute | solution.py:1042
  137.3 58.1 %collective-permute-start.19 = (bf16[640,1664]{1,0:T(8,128)(2,1)}, bf16[640,1664]{1,0:T(8,128)(2,1)S(1)}, u32[]{:S(2)}, u32[]{:S(2)}) collective-permute-start(bf16[640,1664]{1,0:T(8,128)(2,1)} %get-tuple-element.164.refs_1_.payload), channel_id=1, source_target_pairs={{0,2},{1,3},{2,0},{3,1},{4,6},{5,7},{6,4},{7,5},{8,10},{9,11},{10,... | collective-permute-start | bytes 6389768 | tf_op jit(solution)/shard_map/ppermute | solution.py:1033
  247.9 211.8 %reduce-scatter.5.cloned.1.call-start = ((), (), s32[]{:S(2)}) async-start(), calls=%async_computation.4 | async-start | bytes 8847360 | tf_op jit(solution)/shard_map/reduce_scatter | solution.py:1141
  282.6 49.2 %collective-permute-start.23 = (bf16[640,1664]{1,0:T(8,128)(2,1)}, bf16[640,1664]{1,0:T(8,128)(2,1)}, u32[]{:S(2)}, u32[]{:S(2)}) collective-permute-start(bf16[640,1664]{1,0:T(8,128)(2,1)} %fusion), channel_id=1, source_target_pairs={{0,2},{1,3},{2,0},{3,1},{4,6},{5,7},{6,4},{7,5},{8,10},{9,11},{10,... | collective-permute-start | bytes 6389768 | tf_op jit(solution)/shard_map/ppermute | solution.py:1033
  331.9 217.7 %all-gather.5.cloned.1.call-start = ((), (), s32[]{:S(2)}) async-start(), calls=%async_computation.5 | async-start | bytes 8847360 | tf_op jit(solution)/shard_map/all_gather | solution.py:1213
  359.6 27.1 %collective-permute-start.27 = (bf16[1536,768]{1,0:T(8,128)(2,1)}, bf16[1536,768]{1,0:T(8,128)(2,1)}, u32[]{:S(2)}, u32[]{:S(2)}) collective-permute-start(bf16[1536,768]{1,0:T(8,128)(2,1)} %get-tuple-element.214), channel_id=1, source_target_pairs={{0,1},{1,0},{2,3},{3,2},{4,5},{5,4},{6,7},{7,6},{8,9},{9,8},{10,11... | collective-permute-start | bytes 7077896 | tf_op jit(solution)/shard_map/ppermute | solution.py:1026
  398.0 39.5 %collective-permute-start.34 = (bf16[2,384,512]{2,1,0:T(8,128)(2,1)}, bf16[2,384,512]{2,1,0:T(8,128)(2,1)S(1)}, u32[]{:S(2)}, u32[]{:S(2)}) collective-permute-start(bf16[2,384,512]{2,1,0:T(8,128)(2,1)} %get-tuple-element.220), channel_id=1, source_target_pairs={{0,16},{8,24},{16,0},{24,8},{1,17},{9,25},{17,1},{25,9},{2,18},{10... | collective-permute-start | bytes 2359304 | tf_op jit(solution)/shard_map/ppermute | solution.py:1042
  398.3 39.2 %collective-permute-start.35 = (bf16[2,384,512]{2,1,0:T(8,128)(2,1)}, bf16[2,384,512]{2,1,0:T(8,128)(2,1)S(1)}, u32[]{:S(2)}, u32[]{:S(2)}) collective-permute-start(bf16[2,384,512]{2,1,0:T(8,128)(2,1)} %get-tuple-element.222), channel_id=1, source_target_pairs={{0,8},{8,0},{16,24},{24,16},{1,9},{9,1},{17,25},{25,17},{2,10},{10... | collective-permute-start | bytes 2359304 | tf_op jit(solution)/shard_map/ppermute | solution.py:1042
  404.1 33.4 %collective-permute-start.36 = (bf16[2,384,384]{2,1,0:T(8,128)(2,1)}, bf16[2,384,384]{2,1,0:T(8,128)(2,1)}, u32[]{:S(2)}, u32[]{:S(2)}) collective-permute-start(bf16[2,384,384]{2,1,0:T(8,128)(2,1)} %get-tuple-element.226), channel_id=1, source_target_pairs={{0,16},{8,24},{16,0},{24,8},{1,17},{9,25},{17,1},{25,9},{2,18},{10... | collective-permute-start | bytes 1769480 | tf_op jit(solution)/shard_map/ppermute | solution.py:1042
  405.6 31.9 %collective-permute-start.37 = (bf16[2,384,384]{2,1,0:T(8,128)(2,1)}, bf16[2,384,384]{2,1,0:T(8,128)(2,1)}, u32[]{:S(2)}, u32[]{:S(2)}) collective-permute-start(bf16[2,384,384]{2,1,0:T(8,128)(2,1)} %get-tuple-element.228), channel_id=1, source_target_pairs={{0,8},{8,0},{16,24},{24,16},{1,9},{9,1},{17,25},{25,17},{2,10},{10... | collective-permute-start | bytes 1769480 | tf_op jit(solution)/shard_map/ppermute | solution.py:1042
  465.7 63.5 %collective-permute-start.52 = (bf16[640,1536]{1,0:T(8,128)(2,1)}, bf16[640,1536]{1,0:T(8,128)(2,1)}, u32[]{:S(2)}, u32[]{:S(2)}) collective-permute-start(bf16[640,1536]{1,0:T(8,128)(2,1)} %bitcast.76), channel_id=1, source_target_pairs={{0,1},{1,0},{2,3},{3,2},{4,5},{5,4},{6,7},{7,6},{8,9},{9,8},{10,11... | collective-permute-start | bytes 5898248 | tf_op jit(solution)/shard_map/ppermute | solution.py:1026
  466.6 29.7 %collective-permute-start.48 = (bf16[208,1536]{1,0:T(8,128)(2,1)S(1)}, bf16[208,1536]{1,0:T(8,128)(2,1)S(1)}, u32[]{:S(2)}, u32[]{:S(2)}) collective-permute-start(bf16[208,1536]{1,0:T(8,128)(2,1)S(1)} %slice.77), channel_id=1, source_target_pairs={{0,2},{1,3},{2,0},{3,1},{4,6},{5,7},{6,4},{7,5},{8,10},{9,11},{10,... | collective-permute-start | bytes 1916936 | tf_op jit(solution)/shard_map/ppermute | solution.py:1033
  (88 other events, 963.5 us)
Sparse Core Ops, SparseCore 0:
  78.0 53.0 all-gather.2
  248.0 76.8 reduce-scatter.2
  332.0 81.4 reduce-scatter.4
  463.4 79.3 all-gather.4

commit v5 on v4

--- a/solution.py
+++ b/solution.py
@@ -107,10 +107,13 @@
                 ((x, x_out), (gp, gp_out), (h, h_out), (gg, gg_out), (gu, gu_out)))
         ]
 
-    def partial_copies(chunk, q):
+    def partial_copies(chunk, q, tile):
+        wide_cols = pl.ds(0, wide) if tile == 0 else pl.ds(wide, wide + extra)
+        cols = pl.ds(tile * wide, wide)
         return (
-            pltpu.make_async_copy(nbuf.at[q], (pg_same, pg_other)[q].at[chunk], p_sem.at[q, 0]),
-            pltpu.make_async_copy(cbuf.at[q], (po_same, po_other)[q].at[chunk], p_sem.at[q, 1]),
+            pltpu.make_async_copy(
+                nbuf.at[q, :, wide_cols], (pg_same, pg_other)[q].at[chunk, :, wide_cols], p_sem.at[q, tile, 0]),
+            pltpu.make_async_copy(cbuf.at[q, :, cols], (po_same, po_other)[q].at[chunk, :, cols], p_sem.at[q, tile, 1]),
         )
 
     def dispatch(q):
@@ -184,7 +187,7 @@
                 back = mm_nt(gg[place, at, :], wg[place, cols, :]) + mm_nt(gu[place, at, :], wu[place, cols, :])
                 gc[q, own, cols] = back.astype(bf16)
 
-    def combine(q):
+    def combine(chunk, q):
         at = slice(q * rows, (q + 1) * rows)
         lane = lax.broadcasted_iota(jnp.int32, (rows, extra), 1)
         payload = []
@@ -210,6 +213,8 @@
                 out = out + cbuf[q, :, cols].astype(f32)
             nbuf[q, :, cols] = back.astype(bf16)
             cbuf[q, :, cols] = out.astype(bf16)
+            for copy in partial_copies(chunk, q, tile):
+                copy.start()
 
     def prev_copies(chunk):
         po0, po1, pg0, pg1 = prev
@@ -220,19 +225,33 @@
             pltpu.make_async_copy(po1.at[chunk], cbuf.at[1], in_sem.at[1, 1]),
         )
 
-    for q in range(2):
-        for copy in input_copies(0, q):
+    late = max(slots) == 0
+    for copy in input_copies(0, 0):
+        copy.start()
+    if not late:
+        for copy in input_copies(0, 1):
             copy.start()
-    for copies in weight_copies:
-        for copy in copies:
-            copy.start()
+        for copies in weight_copies:
+            for copy in copies:
+                copy.start()
 
     @pl.loop(0, chunks)
     def _(chunk):
-        for q in range(2):
-            for copy in input_copies(0, q):
-                copy.wait()
-            dispatch(q)
+        for copy in input_copies(0, 0):
+            copy.wait()
+
+        @pl.when((chunk == 0) & late)
+        def _():
+            for copy in input_copies(0, 1):
+                copy.start()
+            for copies in weight_copies:
+                for copy in copies:
+                    copy.start()
+
+        dispatch(0)
+        for copy in input_copies(0, 1):
+            copy.wait()
+        dispatch(1)
         if n_prev:
             for copy in prev_copies(chunk):
                 copy.start()
@@ -250,15 +269,14 @@
             for copy in prev_copies(chunk):
                 copy.wait()
         for q in range(2):
-            combine(q)
-            for copy in partial_copies(chunk, q):
-                copy.start()
+            combine(chunk, q)
         for place in range(count):
             for copy in act_copies(chunk, place):
                 copy.wait()
         for q in range(2):
-            for copy in partial_copies(chunk, q):
-                copy.wait()
+            for tile in range(2):
+                for copy in partial_copies(chunk, q, tile):
+                    copy.wait()
 
         for index in range(1, chunks):
             @pl.when(chunk + 1 == index)
@@ -322,7 +340,7 @@
             pltpu.SemaphoreType.DMA((count, 3 * max(1, len(pieces)))),
             pltpu.SemaphoreType.DMA((2, 1 + len(cuts))),
             pltpu.SemaphoreType.DMA((count, 5)),
-            pltpu.SemaphoreType.DMA((2, 2)),
+            pltpu.SemaphoreType.DMA((2, 2, 2)),
         ],
         compiler_params=params(),
         cost_estimate=cost,
@@ -340,7 +358,7 @@
         for i, (source, target) in enumerate((
             (gg_in, ggu.at[:, pl.ds(0, ff)]), (gu_in, ggu.at[:, pl.ds(ff, ff)]), (x_in, x), (h_in, h), (gp_in, gp)))
     ]
-    for copy in loads:
+    for copy in loads[:3]:
         copy.start()
     stores = [
         pltpu.make_async_copy(wide.at[pl.ds(d * tall_f, tall_f)], out.at[pl.ds(d * step, tall_f)], out_sem.at[2 * d])
@@ -352,6 +370,8 @@
     ]
     for copy in loads[:3]:
         copy.wait()
+    for copy in loads[3:]:
+        copy.start()
 
     @pl.loop(0, features // tall)
     def _(tile):
@@ -1059,7 +1079,7 @@
     quarter = jnp.concatenate(
         [jnp.concatenate([dp_part(own[0]), dp_part(own[1])], axis=1), dp_part(own[2])], axis=0
     )
-    part_rows = quarter.shape[0] * 11 // 18
+    part_rows = quarter.shape[0] * 25 // 36
     crossed_one = across(quarter[:part_rows])
 
     token_half = token_rows // 2

time: 575 us -> 573 us (level)
  starting transfers between devices: 62.2 us -> 54.8 us
  waiting for transfers between devices: 161 us -> 167 us
  transfers between devices with their start and end apart: 65 -> 65, of which waited for: 32 -> 31; matrix products, arithmetic and copies ran while one was open for 9% -> 9% of each run, Pallas kernels for 37% -> 37%
where the time goes in v5:
time: 573 us; the launch traced here: 564 us
  Pallas kernels  259 us (45%)
  waiting for transfers between devices  167 us (29%)
  starting transfers between devices  54.8 us (10%)
  local copies, waits for them, and re-layouts  42 us (7%)
  other arithmetic  26.1 us (5%)
  between operations  14.8 us (3%)
    pallas_call x4, Pallas kernels, expert_call(): pl.pallas_call(functools.partial(expert_kernel, experts, slots, base, dat...  105 us
    ppermute x11, waiting for transfers between devices, chip_xor(): lax.ppermute(v, 'expert', [(j, (j // 2 ^ step) * 2 + j % 2) for j in rang...  49.4 us
    ppermute x8, waiting for transfers between devices, shift(): return lax.ppermute(v, 'expert', [(j, to(j)) for j in range(experts)])  48.7 us
    pallas_call x2, Pallas kernels, weight_gradient_call(): pl.pallas_call(functools.partial(weight_gradient_kernel, data), out_shape...  34.8 us
    ppermute x18, waiting for transfers between devices, swap(): return lax.ppermute(v, 'expert', [(j, j ^ 1) for j in range(experts)])  30.7 us
    ppermute x6, waiting for transfers between devices, across(): lax.ppermute(v, 'expert', [(j, (j + experts // 2) % experts) for j in ran...  23.6 us
    pallas_call x1, Pallas kernels, attend_back_call(): pl.pallas_call(functools.partial(attend_back_kernel, rows, 128), out_shap...  22.5 us
    ppermute x18, starting transfers between devices, dp_xor(): return lax.ppermute(v, 'dp', [(j, j ^ k) for j in range(data)])  21 us
  transfers between devices with their start and end apart: 65, of which 31 were waited for; matrix products, arithmetic and copies ran while one was open for 9% of the time, Pallas kernels for 37%

profile of v5, /device:TPU:0, one launch (start us, length us, event | category | flops | bytes accessed | tf_op | source)
XLA Modules:
  0.0 564.1 jit_solution(57900982865482855)
XLA Ops:
  25.0 9.9 %scatter_custom_fusion = s32[2560]{0:T(1024)S(1)} fusion(s32[2560]{0:T(1024)S(1)} %fusion.9, s32[2560]{0:T(1024)S(1)} %iota.7, s32[]{:T(128)} %constant.110.clone.1), kind=kCustom, calls=%fused_computation.68 | custom fusion | bytes 10244 | tf_op jit(solution)/shard_map/scatter | solution.py:999
  37.4 8.6 %collective-permute-done.1.refs_5_.refs_3_.refs_6_ = bf16[384,1792]{1,0:T(8,128)(2,1)S(1)} collective-permute-done((bf16[384,1792]{1,0:T(8,128)(2,1)}, bf16[384,1792]{1,0:T(8,128)(2,1)S(1)}, u32[]{:S(2)}, u32[]{:S(2)}) %collective-permute-start.1) | collective-permute-done | bytes 1376288 | tf_op jit(solution)/shard_map/ppermute | solution.py:1062
  62.7 6.5 %collective-permute-done.5.refs_3_ = bf16[320,1536]{1,0:T(8,128)(2,1)} collective-permute-done((bf16[320,1536]{1,0:T(8,128)(2,1)}, bf16[320,1536]{1,0:T(8,128)(2,1)}, u32[]{:S(2)}, u32[]{:S(2)}) %collective-permute-start.5) | collective-permute-done | bytes 983072 | tf_op jit(solution)/shard_map/ppermute | solution.py:1053
  69.1 6.0 %collective-permute-done.4 = bf16[400,1536]{1,0:T(8,128)(2,1)} collective-permute-done((bf16[400,1536]{1,0:T(8,128)(2,1)}, bf16[400,1536]{1,0:T(8,128)(2,1)}, u32[]{:S(2)}, u32[]{:S(2)}) %collective-permute-start.4) | collective-permute-done | bytes 1228832 | tf_op jit(solution)/shard_map/ppermute | solution.py:1056
  76.2 6.0 %collective-permute-done.8.refs_8_.refs_6_.refs_9_ = bf16[192,1792]{1,0:T(8,128)(2,1)S(1)} collective-permute-done((bf16[192,1792]{1,0:T(8,128)(2,1)S(1)}, bf16[192,1792]{1,0:T(8,128)(2,1)S(1)}, u32[]{:S(2)}, u32[]{:S(2)}) %collective-permute-start.8) | collective-permute-done | bytes 688160 | tf_op jit(solution)/shard_map/ppermute | solution.py:1046
  90.5 19.4 %attend.1 = (bf16[640,1536]{1,0:T(8,128)(2,1)}, bf16[640,2048]{1,0:T(8,128)(2,1)}, bf16[640,1536]{1,0:T(8,128)(2,1)}, f32[640,128]{1,0:T(8,128)}) custom-call(s32[2]{0:T(128)} %pad_add_fusion.place, bf16[640,1536]{1,0:T(8,128)(2,1)} %tokens.5, f32[1,1536]{1,0:T(1,128)} %reshape.78.gain, s32[1,640]{1,0:T(1,128)} %segment_row.3, s32[640,1]{1,0:T(8,128)} %copy.78.segment_col, ...), custom_call_target="tpu_custom_call" | custom-call | flops 1000 | bytes 1000 | tf_op jit(solution)/shard_map/attend/pallas_call | solution.py:543
  109.9 9.0 %collective-permute-done.10.refs_6_.refs_8_ = bf16[176,1536]{1,0:T(8,128)(2,1)S(1)} collective-permute-done((bf16[176,1536]{1,0:T(8,128)(2,1)}, bf16[176,1536]{1,0:T(8,128)(2,1)S(1)}, u32[]{:S(2)}, u32[]{:S(2)}) %collective-permute-start.10) | collective-permute-done | bytes 540704 | tf_op jit(solution)/shard_map/ppermute | solution.py:1056
  120.6 12.2 %route.1 = (f32[640,1536]{1,0:T(8,128)}, bf16[640,1664]{1,0:T(8,128)(2,1)}) custom-call(s32[2]{0:T(128)} %pad_add_fusion.place, bf16[640,1536]{1,0:T(8,128)(2,1)} %get-tuple-element.162.mixture.mixture_in, bf16[640,1536]{1,0:T(8,128)(2,1)} %tokens.5, f32[1,1536]{1,0:T(1,128)} %reshape.79.gain, bf16[1536,128]{1,0:T(8,128)(2,1)} %pad.13.router_weight, ...), custom_call_target="tpu_custom_call" | custom-call | flops 1000 | bytes 1000 | tf_op jit(solution)/shard_map/route/pallas_call | solution.py:701
  143.9 25.2 %expert_rows.4 = (bf16[1,640,1536]{2,1,0:T(8,128)(2,1)}, bf16[1,640,1536]{2,1,0:T(8,128)(2,1)}, bf16[1,640,1664]{2,1,0:T(8,128)(2,1)}, bf16[1,640,1664]{2,1,0:T(...) custom-call(s32[3]{0:T(128)} %pad_add_fusion.1.refs_0_, ...), custom_call_target="tpu_custom_call" | custom-call | flops 1000 | bytes 1000 | tf_op jit(solution)/shard_map/expert_rows/pallas_call | solution.py:312
  169.9 26.9 %expert_rows.5 = (bf16[1,640,1536]{2,1,0:T(8,128)(2,1)}, bf16[1,640,1536]{2,1,0:T(8,128)(2,1)}, bf16[1,640,1664]{2,1,0:T(8,128)(2,1)}, bf16[1,640,1664]{2,1,0:T(...) custom-call(s32[3]{0:T(128)} %pad_add_fusion.1.refs_0_, ...), custom_call_target="tpu_custom_call", output_to_operand_aliasing={{0}: (10, {}), {1}: (11, {}), {2}: (12, {}), {3}: (13, {})} | custom-call | flops 17179869184 | bytes 31457280 | tf_op jit(solution)/shard_map/expert_rows/pallas_call | solution.py:312
  204.2 26.8 %expert_rows.6 = (bf16[1,640,1536]{2,1,0:T(8,128)(2,1)}, bf16[1,640,1536]{2,1,0:T(8,128)(2,1)}, bf16[1,640,1664]{2,1,0:T(8,128)(2,1)}, bf16[1,640,1664]{2,1,0:T(...) custom-call(s32[3]{0:T(128)} %pad_add_fusion.1.refs_0_, ...), custom_call_target="tpu_custom_call", output_to_operand_aliasing={{4}: (12, {}), {5}: (13, {}), {6}: (14, {}), {7}: (15, {}),... | custom-call | flops 1000 | bytes 1000 | tf_op jit(solution)/shard_map/expert_rows/pallas_call | solution.py:312
  231.0 17.3 %expert_weight_gradients.2 = bf16[2304,1536]{1,0:T(8,128)(2,1)} custom-call(bf16[1,1472,1536]{2,1,0:T(8,128)(2,1)} %get-tuple-element.197.x_in, bf16[1,1472,768]{2,1,0:T(8,128)(2,1)} %get-tuple-element.198.gg_in, bf16[1,1472,768]{2,1,0:T(8,128)(2,1)} %get-tuple-element.199.gu_in, bf16[1,1472,768]{2,1,0:T(8,128)(2,1)} %get-tuple-element.200.h_in, ...), custom_call_target="tpu_custom_call" | custom-call | flops 1000 | bytes 1000 | tf_op jit(solution)/shard_map/expert_weight_gradients/pallas_call | solution.py:400
  248.6 25.9 %expert_rows.7 = (bf16[1,640,1536]{2,1,0:T(8,128)(2,1)}, bf16[1,640,1536]{2,1,0:T(8,128)(2,1)}, bf16[1,640,1664]{2,1,0:T(8,128)(2,1)}, bf16[1,640,1664]{2,1,0:T(...) custom-call(s32[3]{0:T(128)} %pad_add_fusion.1.refs_0_, ...), custom_call_target="tpu_custom_call", output_to_operand_aliasing={{0}: (10, {}), {1}: (11, {}), {2}: (12, {}), {3}: (13, {}),... | custom-call | flops 1000 | bytes 1000 | tf_op jit(solution)/shard_map/expert_rows/pallas_call | solution.py:312
  288.3 17.5 %expert_weight_gradients.3 = bf16[2304,1536]{1,0:T(8,128)(2,1)} custom-call(bf16[1,1472,1536]{2,1,0:T(8,128)(2,1)} %get-tuple-element.235.x_in, bf16[1,1472,768]{2,1,0:T(8,128)(2,1)} %get-tuple-element.236.gg_in, bf16[1,1472,768]{2,1,0:T(8,128)(2,1)} %get-tuple-element.237.gu_in, bf16[1,1472,768]{2,1,0:T(8,128)(2,1)} %get-tuple-element.238.h_in, ...), custom_call_target="tpu_custom_call" | custom-call | flops 1000 | bytes 1000 | tf_op jit(solution)/shard_map/expert_weight_gradients/pallas_call | solution.py:400
  305.8 26.1 %collective-permute-done.23.refs_2_ = bf16[640,1664]{1,0:T(8,128)(2,1)} collective-permute-done((bf16[640,1664]{1,0:T(8,128)(2,1)}, bf16[640,1664]{1,0:T(8,128)(2,1)}, u32[]{:S(2)}, u32[]{:S(2)}) %collective-permute-start.23) | collective-permute-done | bytes 2129952 | tf_op jit(solution)/shard_map/ppermute | solution.py:1053
  336.1 20.4 %branch.1 = (f32[640,1536]{1,0:T(8,128)}, bf16[640,1536]{1,0:T(8,128)(2,1)}, bf16[1536,768]{1,0:T(8,128)(2,1)}, bf16[1536,768]{1,0:T(8,128)(2,1)}, f32[1,1536]{1,0:T(1,128)}, /*index=5*/f32[128,1536]{1,0:T(8,128)}) custom-call(s32[2]{0:T(128)} %pad_add_fusion.place, f32[1,1536]{1,0:T(1,128)} %reshape.79.gain, bf16[1536,128]{1,0:T(8,128)(2,1)} %pad.14.router_weight, ...), custom_call_target="tpu_custom_call" | custom-call | flops 1000 | bytes 1000 | tf_op jit(solution)/shard_map/branch/pallas_call | solution.py:841
  361.5 22.5 %attend_back.1 = (bf16[640,2048]{1,0:T(8,128)(2,1)}, bf16[1536,1024]{1,0:T(8,128)(2,1)}, bf16[1536,1024]{1,0:T(8,128)(2,1)}) custom-call(s32[2]{0:T(128)} %pad_add_fusion.place, s32[1,640]{1,0:T(1,128)} %segment_row.3, s32[640,1]{1,0:T(8,128)} %copy.78.segment_col, s32[1,640]{1,0:T(1,128)} %pad_row.3, bf16[640,2048]{1,0:T(8,128)(2,1)} %get-tuple-element.193.qkv, ...), custom_call_target="tpu_custom_call" | custom-call | flops 1000 | bytes 1000 | tf_op jit(solution)/shard_map/attend_back/pallas_call | solution.py:637
  409.3 12.4 %collective-permute-done.32 = bf16[144,1536]{1,0:T(8,128)(2,1)} collective-permute-done((bf16[144,1536]{1,0:T(8,128)(2,1)}, bf16[144,1536]{1,0:T(8,128)(2,1)}, u32[]{:S(2)}, u32[]{:S(2)}) %collective-permute-start.32) | collective-permute-done | bytes 442400 | tf_op jit(solution)/shard_map/ppermute | solution.py:1053
  421.7 14.9 %input_grad.1 = (f32[640,1536]{1,0:T(8,128)}, f32[1,1536]{1,0:T(1,128)}) custom-call(s32[2]{0:T(128)} %pad_add_fusion.place, bf16[640,1536]{1,0:T(8,128)(2,1)} %tokens.5, f32[1,1536]{1,0:T(1,128)} %reshape.78.gain, bf16[640,2048]{1,0:T(8,128)(2,1)} %get-tuple-element.231.grad, f32[640,1536]{1,0:T(8,128)} %get-tuple-element.215.grad_hidden, ...), custom_call_target="tpu_custom_call" | custom-call | flops 1000 | bytes 1000 | tf_op jit(solution)/shard_map/input_grad/pallas_call | solution.py:903
  451.3 5.4 collective-permute-done.41
  465.0 11.4 %collective-permute-done.42 = bf16[192,1024]{1,0:T(8,128)(2,1)} collective-permute-done((bf16[192,1024]{1,0:T(8,128)(2,1)}, bf16[192,1024]{1,0:T(8,128)(2,1)}, u32[]{:S(2)}, u32[]{:S(2)}) %collective-permute-start.42) | collective-permute-done | bytes 393248 | tf_op jit(solution)/shard_map/ppermute | solution.py:1059
  479.7 11.4 %collective-permute-done.43 = bf16[96,1024]{1,0:T(8,128)(2,1)S(1)} collective-permute-done((bf16[96,1024]{1,0:T(8,128)(2,1)S(1)}, bf16[96,1024]{1,0:T(8,128)(2,1)S(1)}, u32[]{:S(2)}, u32[]{:S(2)}) %collective-permute-start.43) | collective-permute-done | bytes 196640 | tf_op jit(solution)/shard_map/ppermute | solution.py:1059
  499.3 6.9 %collective-permute-done.49 = bf16[96,1024]{1,0:T(8,128)(2,1)S(1)} collective-permute-done((bf16[96,1024]{1,0:T(8,128)(2,1)S(1)}, bf16[96,1024]{1,0:T(8,128)(2,1)S(1)}, u32[]{:S(2)}, u32[]{:S(2)}) %collective-permute-start.49) | collective-permute-done | bytes 196640 | tf_op jit(solution)/shard_map/ppermute | solution.py:1059
  549.0 8.4 %widened.1 = (f32[1536,768]{1,0:T(8,128)}, f32[1536,768]{1,0:T(8,128)}, f32[768,1536]{1,0:T(8,128)}) custom-call(bf16[2304,1536]{1,0:T(8,128)(2,1)} %all-gather.5.cloned.1.call-done.whole), custom_call_target="tpu_custom_call" | custom-call | flops 1000 | bytes 1000 | tf_op jit(solution)/shard_map/widened/pallas_call | solution.py:433
  (283 shorter events, 192.5 us)
Async XLA Ops:
  7.2 161.9 %all-gather.3.cloned.1.call-start = ((), (), s32[]{:S(2)}) async-start(), calls=%async_computation.2 | async-start | bytes 6144000 | tf_op jit(solution)/shard_map/all_gather | solution.py:1114
  11.2 36.1 %collective-permute-start = (bf16[384,1792]{1,0:T(8,128)(2,1)}, bf16[384,1792]{1,0:T(8,128)(2,1)S(1)}, u32[]{:S(2)}, u32[]{:S(2)}) collective-permute-start(bf16[384,1792]{1,0:T(8,128)(2,1)} %pad_maximum_fusion), channel_id=1, source_target_pairs={{0,8},{8,0},{16,24},{24,16},{1,9},{9,1},{17,25},{25,17},{2,10},{10... | collective-permute-start | bytes 4128776 | tf_op jit(solution)/shard_map/ppermute | solution.py:1062
  14.2 31.9 %collective-permute-start.1 = (bf16[384,1792]{1,0:T(8,128)(2,1)}, bf16[384,1792]{1,0:T(8,128)(2,1)S(1)}, u32[]{:S(2)}, u32[]{:S(2)}) collective-permute-start(bf16[384,1792]{1,0:T(8,128)(2,1)} %pad_maximum_fusion), channel_id=1, source_target_pairs={{0,16},{8,24},{16,0},{24,8},{1,17},{9,25},{17,1},{25,9},{2,18},{10... | collective-permute-start | bytes 4128776 | tf_op jit(solution)/shard_map/ppermute | solution.py:1062
  19.4 55.7 %collective-permute-start.4 = (bf16[400,1536]{1,0:T(8,128)(2,1)}, bf16[400,1536]{1,0:T(8,128)(2,1)}, u32[]{:S(2)}, u32[]{:S(2)}) collective-permute-start(bf16[400,1536]{1,0:T(8,128)(2,1)} %pad_maximum_fusion.1), channel_id=1, source_target_pairs={{0,4},{1,5},{2,6},{3,7},{4,0},{5,1},{6,2},{7,3},{8,12},{9,13},{10,... | collective-permute-start | bytes 3686408 | tf_op jit(solution)/shard_map/ppermute | solution.py:1056
  23.4 45.7 %collective-permute-start.5 = (bf16[320,1536]{1,0:T(8,128)(2,1)}, bf16[320,1536]{1,0:T(8,128)(2,1)}, u32[]{:S(2)}, u32[]{:S(2)}) collective-permute-start(bf16[320,1536]{1,0:T(8,128)(2,1)} %get-tuple-element.291), channel_id=1, source_target_pairs={{0,2},{1,3},{2,0},{3,1},{4,6},{5,7},{6,4},{7,5},{8,10},{9,11},{10,... | collective-permute-start | bytes 2949128 | tf_op jit(solution)/shard_map/ppermute | solution.py:1053
  47.0 28.2 %collective-permute-start.2 = (bf16[192,1792]{1,0:T(8,128)(2,1)}, bf16[192,1792]{1,0:T(8,128)(2,1)S(1)}, u32[]{:S(2)}, u32[]{:S(2)}) collective-permute-start(bf16[192,1792]{1,0:T(8,128)(2,1)} %slice.76), channel_id=1, source_target_pairs={{0,8},{8,0},{16,24},{24,16},{1,9},{9,1},{17,25},{25,17},{2,10},{10... | collective-permute-start | bytes 2064392 | tf_op jit(solution)/shard_map/ppermute | solution.py:1062
  84.5 247.4 %reduce-scatter.3.cloned.1.call-start = ((), (), s32[]{:S(2)}) async-start(), calls=%async_computation.3 | async-start | bytes 8847360 | tf_op jit(solution)/shard_map/reduce_scatter | solution.py:1161
  84.6 36.0 %collective-permute-start.12 = (bf16[640,1536]{1,0:T(8,128)(2,1)}, bf16[640,1536]{1,0:T(8,128)(2,1)}, u32[]{:S(2)}, u32[]{:S(2)}) collective-permute-start(bf16[640,1536]{1,0:T(8,128)(2,1)} %cotangent.1), channel_id=1, source_target_pairs={{0,1},{1,0},{2,3},{3,2},{4,5},{5,4},{6,7},{7,6},{8,9},{9,8},{10,11... | collective-permute-start | bytes 5898248 | tf_op jit(solution)/shard_map/ppermute | solution.py:1046
  84.8 35.8 %collective-permute-start.11 = (bf16[320,1536]{1,0:T(8,128)(2,1)}, bf16[320,1536]{1,0:T(8,128)(2,1)S(1)}, u32[]{:S(2)}, u32[]{:S(2)}) collective-permute-start(bf16[320,1536]{1,0:T(8,128)(2,1)} %get-tuple-element.159), channel_id=1, source_target_pairs={{0,2},{1,3},{2,0},{3,1},{4,6},{5,7},{6,4},{7,5},{8,10},{9,11},{10,... | collective-permute-start | bytes 2949128 | tf_op jit(solution)/shard_map/ppermute | solution.py:1053
  85.5 35.2 %collective-permute-start.13 = (bf16[320,1536]{1,0:T(8,128)(2,1)}, bf16[320,1536]{1,0:T(8,128)(2,1)S(1)}, u32[]{:S(2)}, u32[]{:S(2)}) collective-permute-start(bf16[320,1536]{1,0:T(8,128)(2,1)} %collective-permute-done.5.refs_3_), channel_id=1, source_target_pairs={{0,1},{1,0},{2,3},{3,2},{4,5},{5,4},{6,7},{7,6},{8,9},{9,8},{10,11... | collective-permute-start | bytes 2949128 | tf_op jit(solution)/shard_map/ppermute | solution.py:1046
  85.5 33.4 %collective-permute-start.10 = (bf16[176,1536]{1,0:T(8,128)(2,1)}, bf16[176,1536]{1,0:T(8,128)(2,1)S(1)}, u32[]{:S(2)}, u32[]{:S(2)}) collective-permute-start(bf16[176,1536]{1,0:T(8,128)(2,1)} %dynamic-slice_bitcast_fusion.3), channel_id=1, source_target_pairs={{0,4},{1,5},{2,6},{3,7},{4,0},{5,1},{6,2},{7,3},{8,12},{9,13},{10,... | collective-permute-start | bytes 1622024 | tf_op jit(solution)/shard_map/ppermute | solution.py:1056
  137.3 31.8 %collective-permute-start.15 = (bf16[176,1536]{1,0:T(8,128)(2,1)S(1)}, bf16[176,1536]{1,0:T(8,128)(2,1)S(1)}, u32[]{:S(2)}, u32[]{:S(2)}) collective-permute-start(bf16[176,1536]{1,0:T(8,128)(2,1)S(1)} %collective-permute-done.10.refs_6_.refs_8_), channel_id=1, source_target_pairs={{0,8},{8,0},{16,24},{24,16},{1,9},{9,1},{17,25},{25,17},{2,10},{10... | collective-permute-start | bytes 1622024 | tf_op jit(solution)/shard_map/ppermute | solution.py:1062
  137.8 31.3 %collective-permute-start.16 = (bf16[176,1536]{1,0:T(8,128)(2,1)S(1)}, bf16[176,1536]{1,0:T(8,128)(2,1)}, u32[]{:S(2)}, u32[]{:S(2)}) collective-permute-start(bf16[176,1536]{1,0:T(8,128)(2,1)S(1)} %collective-permute-done.10.refs_6_.refs_8_), channel_id=1, source_target_pairs={{0,16},{8,24},{16,0},{24,8},{1,17},{9,25},{17,1},{25,9},{2,18},{10... | collective-permute-start | bytes 1622024 | tf_op jit(solution)/shard_map/ppermute | solution.py:1062
  138.7 30.4 %collective-permute-start.17 = (bf16[176,1536]{1,0:T(8,128)(2,1)S(1)}, bf16[176,1536]{1,0:T(8,128)(2,1)}, u32[]{:S(2)}, u32[]{:S(2)}) collective-permute-start(bf16[176,1536]{1,0:T(8,128)(2,1)S(1)} %collective-permute-done.10.refs_6_.refs_8_), channel_id=1, source_target_pairs={{0,24},{8,16},{16,8},{24,0},{1,25},{9,17},{17,9},{25,1},{2,26},{10... | collective-permute-start | bytes 1622024 | tf_op jit(solution)/shard_map/ppermute | solution.py:1062
  140.8 56.0 %collective-permute-start.19 = (bf16[640,1664]{1,0:T(8,128)(2,1)}, bf16[640,1664]{1,0:T(8,128)(2,1)S(1)}, u32[]{:S(2)}, u32[]{:S(2)}) collective-permute-start(bf16[640,1664]{1,0:T(8,128)(2,1)} %get-tuple-element.164.refs_1_.payload), channel_id=1, source_target_pairs={{0,2},{1,3},{2,0},{3,1},{4,6},{5,7},{6,4},{7,5},{8,10},{9,11},{10,... | collective-permute-start | bytes 6389768 | tf_op jit(solution)/shard_map/ppermute | solution.py:1053
  248.4 209.1 %reduce-scatter.5.cloned.1.call-start = ((), (), s32[]{:S(2)}) async-start(), calls=%async_computation.4 | async-start | bytes 8847360 | tf_op jit(solution)/shard_map/reduce_scatter | solution.py:1161
  283.2 48.7 %collective-permute-start.23 = (bf16[640,1664]{1,0:T(8,128)(2,1)}, bf16[640,1664]{1,0:T(8,128)(2,1)}, u32[]{:S(2)}, u32[]{:S(2)}) collective-permute-start(bf16[640,1664]{1,0:T(8,128)(2,1)} %fusion), channel_id=1, source_target_pairs={{0,2},{1,3},{2,0},{3,1},{4,6},{5,7},{6,4},{7,5},{8,10},{9,11},{10,... | collective-permute-start | bytes 6389768 | tf_op jit(solution)/shard_map/ppermute | solution.py:1053
  331.9 215.8 %all-gather.5.cloned.1.call-start = ((), (), s32[]{:S(2)}) async-start(), calls=%async_computation.5 | async-start | bytes 8847360 | tf_op jit(solution)/shard_map/all_gather | solution.py:1233
  396.6 40.0 %collective-permute-start.34 = (bf16[2,384,512]{2,1,0:T(8,128)(2,1)}, bf16[2,384,512]{2,1,0:T(8,128)(2,1)S(1)}, u32[]{:S(2)}, u32[]{:S(2)}) collective-permute-start(bf16[2,384,512]{2,1,0:T(8,128)(2,1)} %get-tuple-element.220), channel_id=1, source_target_pairs={{0,16},{8,24},{16,0},{24,8},{1,17},{9,25},{17,1},{25,9},{2,18},{10... | collective-permute-start | bytes 2359304 | tf_op jit(solution)/shard_map/ppermute | solution.py:1062
  396.8 39.8 %collective-permute-start.35 = (bf16[2,384,512]{2,1,0:T(8,128)(2,1)}, bf16[2,384,512]{2,1,0:T(8,128)(2,1)S(1)}, u32[]{:S(2)}, u32[]{:S(2)}) collective-permute-start(bf16[2,384,512]{2,1,0:T(8,128)(2,1)} %get-tuple-element.222), channel_id=1, source_target_pairs={{0,8},{8,0},{16,24},{24,16},{1,9},{9,1},{17,25},{25,17},{2,10},{10... | collective-permute-start | bytes 2359304 | tf_op jit(solution)/shard_map/ppermute | solution.py:1062
  402.2 34.3 %collective-permute-start.36 = (bf16[2,384,384]{2,1,0:T(8,128)(2,1)}, bf16[2,384,384]{2,1,0:T(8,128)(2,1)}, u32[]{:S(2)}, u32[]{:S(2)}) collective-permute-start(bf16[2,384,384]{2,1,0:T(8,128)(2,1)} %get-tuple-element.226), channel_id=1, source_target_pairs={{0,16},{8,24},{16,0},{24,8},{1,17},{9,25},{17,1},{25,9},{2,18},{10... | collective-permute-start | bytes 1769480 | tf_op jit(solution)/shard_map/ppermute | solution.py:1062
  403.1 33.5 %collective-permute-start.37 = (bf16[2,384,384]{2,1,0:T(8,128)(2,1)}, bf16[2,384,384]{2,1,0:T(8,128)(2,1)}, u32[]{:S(2)}, u32[]{:S(2)}) collective-permute-start(bf16[2,384,384]{2,1,0:T(8,128)(2,1)} %get-tuple-element.228), channel_id=1, source_target_pairs={{0,8},{8,0},{16,24},{24,16},{1,9},{9,1},{17,25},{25,17},{2,10},{10... | collective-permute-start | bytes 1769480 | tf_op jit(solution)/shard_map/ppermute | solution.py:1062
  463.4 64.9 %collective-permute-start.52 = (bf16[640,1536]{1,0:T(8,128)(2,1)}, bf16[640,1536]{1,0:T(8,128)(2,1)}, u32[]{:S(2)}, u32[]{:S(2)}) collective-permute-start(bf16[640,1536]{1,0:T(8,128)(2,1)} %bitcast.78), channel_id=1, source_target_pairs={{0,1},{1,0},{2,3},{3,2},{4,5},{5,4},{6,7},{7,6},{8,9},{9,8},{10,11... | collective-permute-start | bytes 5898248 | tf_op jit(solution)/shard_map/ppermute | solution.py:1046
  464.4 28.8 %collective-permute-start.48 = (bf16[208,1536]{1,0:T(8,128)(2,1)S(1)}, bf16[208,1536]{1,0:T(8,128)(2,1)S(1)}, u32[]{:S(2)}, u32[]{:S(2)}) collective-permute-start(bf16[208,1536]{1,0:T(8,128)(2,1)S(1)} %slice.81), channel_id=1, source_target_pairs={{0,2},{1,3},{2,0},{3,1},{4,6},{5,7},{6,4},{7,5},{8,10},{9,11},{10,... | collective-permute-start | bytes 1916936 | tf_op jit(solution)/shard_map/ppermute | solution.py:1053
  (84 other events, 1038.0 us)
Sparse Core Ops, SparseCore 0:
  84.7 60.1 all-gather.2
  248.5 74.3 reduce-scatter.2
  332.0 78.4 reduce-scatter.4
  461.2 79.5 all-gather.4

commit v6 on v5

--- a/solution.py
+++ b/solution.py
@@ -419,23 +419,41 @@
 
 
 def widened_kernel(whole, gate, up, down):
-    tall, ff = gate.shape
-    gate[...] = whole[:tall, :ff].astype(f32)
-    up[...] = whole[:tall, ff:].astype(f32)
-    down[...] = whole[tall:, :].astype(f32)
+    ff = gate.shape[1]
+    third = lax.rem(pl.program_id(0), 3)
+
+    @pl.when(third < 2)
+    def _():
+        gate[...] = whole[:, :ff].astype(f32)
+        up[...] = whole[:, ff:].astype(f32)
+
+    @pl.when(third == 2)
+    def _():
+        down[...] = whole[...].astype(f32)
 
 
 def widened(whole, data):
     rows, features = whole.shape[0] // data, whole.shape[1]
     ff = features // 2
-    tall = rows * 2 // 3
-    blocks = [(tall, ff), (tall, ff), (rows - tall, features)]
+    unit = rows // 3
+
+    def wide_block(i):
+        return (i // 3 * 2 + jnp.minimum(i % 3, 1), 0)
+
     return pl.pallas_call(
         widened_kernel,
-        grid=(data,),
-        in_specs=[pl.BlockSpec((rows, features), lambda d: (d, 0))],
-        out_specs=[pl.BlockSpec(block, lambda d: (d, 0)) for block in blocks],
-        out_shape=[jax.ShapeDtypeStruct((data * block[0], block[1]), f32) for block in blocks],
+        grid=(3 * data,),
+        in_specs=[pl.BlockSpec((unit, features), lambda i: (i, 0))],
+        out_specs=[
+            pl.BlockSpec((unit, ff), wide_block),
+            pl.BlockSpec((unit, ff), wide_block),
+            pl.BlockSpec((unit, features), lambda i: (i // 3, 0)),
+        ],
+        out_shape=[
+            jax.ShapeDtypeStruct((2 * data * unit, ff), f32),
+            jax.ShapeDtypeStruct((2 * data * unit, ff), f32),
+            jax.ShapeDtypeStruct((data * unit, features), f32),
+        ],
         compiler_params=params(),
         cost_estimate=COST,
         name="widened",

time: 573 us -> 577 us (level)
  transfers between devices with their start and end apart: 65 -> 65, of which waited for: 31 -> 31; matrix products, arithmetic and copies ran while one was open for 9% -> 9% of each run, Pallas kernels for 37% -> 36%
where the time goes in v6:
time: 577 us; the launch traced here: 568 us
  Pallas kernels  263 us (46%)
  waiting for transfers between devices  167 us (29%)
  starting transfers between devices  54.8 us (9%)
  local copies, waits for them, and re-layouts  42 us (7%)
  other arithmetic  26.1 us (5%)
  between operations  14.8 us (3%)
    pallas_call x4, Pallas kernels, expert_call(): pl.pallas_call(functools.partial(expert_kernel, experts, slots, base, dat...  105 us
    ppermute x11, waiting for transfers between devices, chip_xor(): lax.ppermute(v, 'expert', [(j, (j // 2 ^ step) * 2 + j % 2) for j in rang...  49.4 us
    ppermute x8, waiting for transfers between devices, shift(): return lax.ppermute(v, 'expert', [(j, to(j)) for j in range(experts)])  48.7 us
    pallas_call x2, Pallas kernels, weight_gradient_call(): pl.pallas_call(functools.partial(weight_gradient_kernel, data), out_shape...  34.8 us
    ppermute x18, waiting for transfers between devices, swap(): return lax.ppermute(v, 'expert', [(j, j ^ 1) for j in range(experts)])  30.7 us
    ppermute x6, waiting for transfers between devices, across(): lax.ppermute(v, 'expert', [(j, (j + experts // 2) % experts) for j in ran...  23.6 us
    pallas_call x1, Pallas kernels, attend_back_call(): pl.pallas_call(functools.partial(attend_back_kernel, rows, 128), out_shap...  22.5 us
    ppermute x18, starting transfers between devices, dp_xor(): return lax.ppermute(v, 'dp', [(j, j ^ k) for j in range(data)])  21 us
  transfers between devices with their start and end apart: 65, of which 31 were waited for; matrix products, arithmetic and copies ran while one was open for 9% of the time, Pallas kernels for 36%

profile of v6, /device:TPU:0, one launch (start us, length us, event | category | flops | bytes accessed | tf_op | source)
XLA Modules:
  0.0 567.7 jit_solution(12600443317640114423)
XLA Ops:
  25.0 9.9 %scatter_custom_fusion = s32[2560]{0:T(1024)S(1)} fusion(s32[2560]{0:T(1024)S(1)} %fusion.9, s32[2560]{0:T(1024)S(1)} %iota.7, s32[]{:T(128)} %constant.110.clone.1), kind=kCustom, calls=%fused_computation.68 | custom fusion | bytes 10244 | tf_op jit(solution)/shard_map/scatter | solution.py:1017
  37.4 8.6 %collective-permute-done.1.refs_5_.refs_3_.refs_6_ = bf16[384,1792]{1,0:T(8,128)(2,1)S(1)} collective-permute-done((bf16[384,1792]{1,0:T(8,128)(2,1)}, bf16[384,1792]{1,0:T(8,128)(2,1)S(1)}, u32[]{:S(2)}, u32[]{:S(2)}) %collective-permute-start.1) | collective-permute-done | bytes 1376288 | tf_op jit(solution)/shard_map/ppermute | solution.py:1080
  62.7 6.5 %collective-permute-done.5.refs_3_ = bf16[320,1536]{1,0:T(8,128)(2,1)} collective-permute-done((bf16[320,1536]{1,0:T(8,128)(2,1)}, bf16[320,1536]{1,0:T(8,128)(2,1)}, u32[]{:S(2)}, u32[]{:S(2)}) %collective-permute-start.5) | collective-permute-done | bytes 983072 | tf_op jit(solution)/shard_map/ppermute | solution.py:1071
  69.1 6.0 %collective-permute-done.4 = bf16[400,1536]{1,0:T(8,128)(2,1)} collective-permute-done((bf16[400,1536]{1,0:T(8,128)(2,1)}, bf16[400,1536]{1,0:T(8,128)(2,1)}, u32[]{:S(2)}, u32[]{:S(2)}) %collective-permute-start.4) | collective-permute-done | bytes 1228832 | tf_op jit(solution)/shard_map/ppermute | solution.py:1074
  76.2 6.0 %collective-permute-done.8.refs_8_.refs_6_.refs_9_ = bf16[192,1792]{1,0:T(8,128)(2,1)S(1)} collective-permute-done((bf16[192,1792]{1,0:T(8,128)(2,1)S(1)}, bf16[192,1792]{1,0:T(8,128)(2,1)S(1)}, u32[]{:S(2)}, u32[]{:S(2)}) %collective-permute-start.8) | collective-permute-done | bytes 688160 | tf_op jit(solution)/shard_map/ppermute | solution.py:1064
  90.5 19.4 %attend.1 = (bf16[640,1536]{1,0:T(8,128)(2,1)}, bf16[640,2048]{1,0:T(8,128)(2,1)}, bf16[640,1536]{1,0:T(8,128)(2,1)}, f32[640,128]{1,0:T(8,128)}) custom-call(s32[2]{0:T(128)} %pad_add_fusion.place, bf16[640,1536]{1,0:T(8,128)(2,1)} %tokens.5, f32[1,1536]{1,0:T(1,128)} %reshape.78.gain, s32[1,640]{1,0:T(1,128)} %segment_row.3, s32[640,1]{1,0:T(8,128)} %copy.78.segment_col, ...), custom_call_target="tpu_custom_call" | custom-call | flops 1000 | bytes 1000 | tf_op jit(solution)/shard_map/attend/pallas_call | solution.py:561
  109.9 9.0 %collective-permute-done.10.refs_6_.refs_8_ = bf16[176,1536]{1,0:T(8,128)(2,1)S(1)} collective-permute-done((bf16[176,1536]{1,0:T(8,128)(2,1)}, bf16[176,1536]{1,0:T(8,128)(2,1)S(1)}, u32[]{:S(2)}, u32[]{:S(2)}) %collective-permute-start.10) | collective-permute-done | bytes 540704 | tf_op jit(solution)/shard_map/ppermute | solution.py:1074
  120.6 12.2 %route.1 = (f32[640,1536]{1,0:T(8,128)}, bf16[640,1664]{1,0:T(8,128)(2,1)}) custom-call(s32[2]{0:T(128)} %pad_add_fusion.place, bf16[640,1536]{1,0:T(8,128)(2,1)} %get-tuple-element.162.mixture.mixture_in, bf16[640,1536]{1,0:T(8,128)(2,1)} %tokens.5, f32[1,1536]{1,0:T(1,128)} %reshape.79.gain, bf16[1536,128]{1,0:T(8,128)(2,1)} %pad.13.router_weight, ...), custom_call_target="tpu_custom_call" | custom-call | flops 1000 | bytes 1000 | tf_op jit(solution)/shard_map/route/pallas_call | solution.py:719
  143.9 25.2 %expert_rows.4 = (bf16[1,640,1536]{2,1,0:T(8,128)(2,1)}, bf16[1,640,1536]{2,1,0:T(8,128)(2,1)}, bf16[1,640,1664]{2,1,0:T(8,128)(2,1)}, bf16[1,640,1664]{2,1,0:T(...) custom-call(s32[3]{0:T(128)} %pad_add_fusion.1.refs_0_, ...), custom_call_target="tpu_custom_call" | custom-call | flops 1000 | bytes 1000 | tf_op jit(solution)/shard_map/expert_rows/pallas_call | solution.py:312
  169.9 26.9 %expert_rows.5 = (bf16[1,640,1536]{2,1,0:T(8,128)(2,1)}, bf16[1,640,1536]{2,1,0:T(8,128)(2,1)}, bf16[1,640,1664]{2,1,0:T(8,128)(2,1)}, bf16[1,640,1664]{2,1,0:T(...) custom-call(s32[3]{0:T(128)} %pad_add_fusion.1.refs_0_, ...), custom_call_target="tpu_custom_call", output_to_operand_aliasing={{0}: (10, {}), {1}: (11, {}), {2}: (12, {}), {3}: (13, {})} | custom-call | flops 17179869184 | bytes 31457280 | tf_op jit(solution)/shard_map/expert_rows/pallas_call | solution.py:312
  204.2 26.8 %expert_rows.6 = (bf16[1,640,1536]{2,1,0:T(8,128)(2,1)}, bf16[1,640,1536]{2,1,0:T(8,128)(2,1)}, bf16[1,640,1664]{2,1,0:T(8,128)(2,1)}, bf16[1,640,1664]{2,1,0:T(...) custom-call(s32[3]{0:T(128)} %pad_add_fusion.1.refs_0_, ...), custom_call_target="tpu_custom_call", output_to_operand_aliasing={{4}: (12, {}), {5}: (13, {}), {6}: (14, {}), {7}: (15, {}),... | custom-call | flops 1000 | bytes 1000 | tf_op jit(solution)/shard_map/expert_rows/pallas_call | solution.py:312
  231.0 17.3 %expert_weight_gradients.2 = bf16[2304,1536]{1,0:T(8,128)(2,1)} custom-call(bf16[1,1472,1536]{2,1,0:T(8,128)(2,1)} %get-tuple-element.197.x_in, bf16[1,1472,768]{2,1,0:T(8,128)(2,1)} %get-tuple-element.198.gg_in, bf16[1,1472,768]{2,1,0:T(8,128)(2,1)} %get-tuple-element.199.gu_in, bf16[1,1472,768]{2,1,0:T(8,128)(2,1)} %get-tuple-element.200.h_in, ...), custom_call_target="tpu_custom_call" | custom-call | flops 1000 | bytes 1000 | tf_op jit(solution)/shard_map/expert_weight_gradients/pallas_call | solution.py:400
  248.6 25.9 %expert_rows.7 = (bf16[1,640,1536]{2,1,0:T(8,128)(2,1)}, bf16[1,640,1536]{2,1,0:T(8,128)(2,1)}, bf16[1,640,1664]{2,1,0:T(8,128)(2,1)}, bf16[1,640,1664]{2,1,0:T(...) custom-call(s32[3]{0:T(128)} %pad_add_fusion.1.refs_0_, ...), custom_call_target="tpu_custom_call", output_to_operand_aliasing={{0}: (10, {}), {1}: (11, {}), {2}: (12, {}), {3}: (13, {}),... | custom-call | flops 1000 | bytes 1000 | tf_op jit(solution)/shard_map/expert_rows/pallas_call | solution.py:312
  288.3 17.5 %expert_weight_gradients.3 = bf16[2304,1536]{1,0:T(8,128)(2,1)} custom-call(bf16[1,1472,1536]{2,1,0:T(8,128)(2,1)} %get-tuple-element.235.x_in, bf16[1,1472,768]{2,1,0:T(8,128)(2,1)} %get-tuple-element.236.gg_in, bf16[1,1472,768]{2,1,0:T(8,128)(2,1)} %get-tuple-element.237.gu_in, bf16[1,1472,768]{2,1,0:T(8,128)(2,1)} %get-tuple-element.238.h_in, ...), custom_call_target="tpu_custom_call" | custom-call | flops 1000 | bytes 1000 | tf_op jit(solution)/shard_map/expert_weight_gradients/pallas_call | solution.py:400
  305.8 26.1 %collective-permute-done.23.refs_2_ = bf16[640,1664]{1,0:T(8,128)(2,1)} collective-permute-done((bf16[640,1664]{1,0:T(8,128)(2,1)}, bf16[640,1664]{1,0:T(8,128)(2,1)}, u32[]{:S(2)}, u32[]{:S(2)}) %collective-permute-start.23) | collective-permute-done | bytes 2129952 | tf_op jit(solution)/shard_map/ppermute | solution.py:1071
  336.1 20.4 %branch.1 = (f32[640,1536]{1,0:T(8,128)}, bf16[640,1536]{1,0:T(8,128)(2,1)}, bf16[1536,768]{1,0:T(8,128)(2,1)}, bf16[1536,768]{1,0:T(8,128)(2,1)}, f32[1,1536]{1,0:T(1,128)}, /*index=5*/f32[128,1536]{1,0:T(8,128)}) custom-call(s32[2]{0:T(128)} %pad_add_fusion.place, f32[1,1536]{1,0:T(1,128)} %reshape.79.gain, bf16[1536,128]{1,0:T(8,128)(2,1)} %pad.14.router_weight, ...), custom_call_target="tpu_custom_call" | custom-call | flops 1000 | bytes 1000 | tf_op jit(solution)/shard_map/branch/pallas_call | solution.py:859
  361.5 22.5 %attend_back.1 = (bf16[640,2048]{1,0:T(8,128)(2,1)}, bf16[1536,1024]{1,0:T(8,128)(2,1)}, bf16[1536,1024]{1,0:T(8,128)(2,1)}) custom-call(s32[2]{0:T(128)} %pad_add_fusion.place, s32[1,640]{1,0:T(1,128)} %segment_row.3, s32[640,1]{1,0:T(8,128)} %copy.78.segment_col, s32[1,640]{1,0:T(1,128)} %pad_row.3, bf16[640,2048]{1,0:T(8,128)(2,1)} %get-tuple-element.193.qkv, ...), custom_call_target="tpu_custom_call" | custom-call | flops 1000 | bytes 1000 | tf_op jit(solution)/shard_map/attend_back/pallas_call | solution.py:655
  409.3 12.4 %collective-permute-done.32 = bf16[144,1536]{1,0:T(8,128)(2,1)} collective-permute-done((bf16[144,1536]{1,0:T(8,128)(2,1)}, bf16[144,1536]{1,0:T(8,128)(2,1)}, u32[]{:S(2)}, u32[]{:S(2)}) %collective-permute-start.32) | collective-permute-done | bytes 442400 | tf_op jit(solution)/shard_map/ppermute | solution.py:1071
  421.7 14.9 %input_grad.1 = (f32[640,1536]{1,0:T(8,128)}, f32[1,1536]{1,0:T(1,128)}) custom-call(s32[2]{0:T(128)} %pad_add_fusion.place, bf16[640,1536]{1,0:T(8,128)(2,1)} %tokens.5, f32[1,1536]{1,0:T(1,128)} %reshape.78.gain, bf16[640,2048]{1,0:T(8,128)(2,1)} %get-tuple-element.231.grad, f32[640,1536]{1,0:T(8,128)} %get-tuple-element.215.grad_hidden, ...), custom_call_target="tpu_custom_call" | custom-call | flops 1000 | bytes 1000 | tf_op jit(solution)/shard_map/input_grad/pallas_call | solution.py:921
  451.3 5.4 collective-permute-done.41
  465.0 11.4 %collective-permute-done.42 = bf16[192,1024]{1,0:T(8,128)(2,1)} collective-permute-done((bf16[192,1024]{1,0:T(8,128)(2,1)}, bf16[192,1024]{1,0:T(8,128)(2,1)}, u32[]{:S(2)}, u32[]{:S(2)}) %collective-permute-start.42) | collective-permute-done | bytes 393248 | tf_op jit(solution)/shard_map/ppermute | solution.py:1077
  479.7 11.4 %collective-permute-done.43 = bf16[96,1024]{1,0:T(8,128)(2,1)S(1)} collective-permute-done((bf16[96,1024]{1,0:T(8,128)(2,1)S(1)}, bf16[96,1024]{1,0:T(8,128)(2,1)S(1)}, u32[]{:S(2)}, u32[]{:S(2)}) %collective-permute-start.43) | collective-permute-done | bytes 196640 | tf_op jit(solution)/shard_map/ppermute | solution.py:1077
  499.3 6.9 %collective-permute-done.49 = bf16[96,1024]{1,0:T(8,128)(2,1)S(1)} collective-permute-done((bf16[96,1024]{1,0:T(8,128)(2,1)S(1)}, bf16[96,1024]{1,0:T(8,128)(2,1)S(1)}, u32[]{:S(2)}, u32[]{:S(2)}) %collective-permute-start.49) | collective-permute-done | bytes 196640 | tf_op jit(solution)/shard_map/ppermute | solution.py:1077
  549.0 11.9 %widened.1 = (f32[1536,768]{1,0:T(8,128)}, f32[1536,768]{1,0:T(8,128)}, f32[768,1536]{1,0:T(8,128)}) custom-call(bf16[2304,1536]{1,0:T(8,128)(2,1)} %all-gather.5.cloned.1.call-done.whole), custom_call_target="tpu_custom_call" | custom-call | flops 1000 | bytes 1000 | tf_op jit(solution)/shard_map/widened/pallas_call | solution.py:443
  (283 shorter events, 192.5 us)
Async XLA Ops:
  7.2 161.9 %all-gather.3.cloned.1.call-start = ((), (), s32[]{:S(2)}) async-start(), calls=%async_computation.2 | async-start | bytes 6144000 | tf_op jit(solution)/shard_map/all_gather | solution.py:1132
  11.2 36.1 %collective-permute-start = (bf16[384,1792]{1,0:T(8,128)(2,1)}, bf16[384,1792]{1,0:T(8,128)(2,1)S(1)}, u32[]{:S(2)}, u32[]{:S(2)}) collective-permute-start(bf16[384,1792]{1,0:T(8,128)(2,1)} %pad_maximum_fusion), channel_id=1, source_target_pairs={{0,8},{8,0},{16,24},{24,16},{1,9},{9,1},{17,25},{25,17},{2,10},{10... | collective-permute-start | bytes 4128776 | tf_op jit(solution)/shard_map/ppermute | solution.py:1080
  14.2 31.9 %collective-permute-start.1 = (bf16[384,1792]{1,0:T(8,128)(2,1)}, bf16[384,1792]{1,0:T(8,128)(2,1)S(1)}, u32[]{:S(2)}, u32[]{:S(2)}) collective-permute-start(bf16[384,1792]{1,0:T(8,128)(2,1)} %pad_maximum_fusion), channel_id=1, source_target_pairs={{0,16},{8,24},{16,0},{24,8},{1,17},{9,25},{17,1},{25,9},{2,18},{10... | collective-permute-start | bytes 4128776 | tf_op jit(solution)/shard_map/ppermute | solution.py:1080
  19.4 55.7 %collective-permute-start.4 = (bf16[400,1536]{1,0:T(8,128)(2,1)}, bf16[400,1536]{1,0:T(8,128)(2,1)}, u32[]{:S(2)}, u32[]{:S(2)}) collective-permute-start(bf16[400,1536]{1,0:T(8,128)(2,1)} %pad_maximum_fusion.1), channel_id=1, source_target_pairs={{0,4},{1,5},{2,6},{3,7},{4,0},{5,1},{6,2},{7,3},{8,12},{9,13},{10,... | collective-permute-start | bytes 3686408 | tf_op jit(solution)/shard_map/ppermute | solution.py:1074
  23.4 45.7 %collective-permute-start.5 = (bf16[320,1536]{1,0:T(8,128)(2,1)}, bf16[320,1536]{1,0:T(8,128)(2,1)}, u32[]{:S(2)}, u32[]{:S(2)}) collective-permute-start(bf16[320,1536]{1,0:T(8,128)(2,1)} %get-tuple-element.291), channel_id=1, source_target_pairs={{0,2},{1,3},{2,0},{3,1},{4,6},{5,7},{6,4},{7,5},{8,10},{9,11},{10,... | collective-permute-start | bytes 2949128 | tf_op jit(solution)/shard_map/ppermute | solution.py:1071
  47.0 28.2 %collective-permute-start.2 = (bf16[192,1792]{1,0:T(8,128)(2,1)}, bf16[192,1792]{1,0:T(8,128)(2,1)S(1)}, u32[]{:S(2)}, u32[]{:S(2)}) collective-permute-start(bf16[192,1792]{1,0:T(8,128)(2,1)} %slice.76), channel_id=1, source_target_pairs={{0,8},{8,0},{16,24},{24,16},{1,9},{9,1},{17,25},{25,17},{2,10},{10... | collective-permute-start | bytes 2064392 | tf_op jit(solution)/shard_map/ppermute | solution.py:1080
  84.5 247.4 %reduce-scatter.3.cloned.1.call-start = ((), (), s32[]{:S(2)}) async-start(), calls=%async_computation.3 | async-start | bytes 8847360 | tf_op jit(solution)/shard_map/reduce_scatter | solution.py:1179
  84.6 36.0 %collective-permute-start.12 = (bf16[640,1536]{1,0:T(8,128)(2,1)}, bf16[640,1536]{1,0:T(8,128)(2,1)}, u32[]{:S(2)}, u32[]{:S(2)}) collective-permute-start(bf16[640,1536]{1,0:T(8,128)(2,1)} %cotangent.1), channel_id=1, source_target_pairs={{0,1},{1,0},{2,3},{3,2},{4,5},{5,4},{6,7},{7,6},{8,9},{9,8},{10,11... | collective-permute-start | bytes 5898248 | tf_op jit(solution)/shard_map/ppermute | solution.py:1064
  84.8 35.8 %collective-permute-start.11 = (bf16[320,1536]{1,0:T(8,128)(2,1)}, bf16[320,1536]{1,0:T(8,128)(2,1)S(1)}, u32[]{:S(2)}, u32[]{:S(2)}) collective-permute-start(bf16[320,1536]{1,0:T(8,128)(2,1)} %get-tuple-element.159), channel_id=1, source_target_pairs={{0,2},{1,3},{2,0},{3,1},{4,6},{5,7},{6,4},{7,5},{8,10},{9,11},{10,... | collective-permute-start | bytes 2949128 | tf_op jit(solution)/shard_map/ppermute | solution.py:1071
  85.5 35.2 %collective-permute-start.13 = (bf16[320,1536]{1,0:T(8,128)(2,1)}, bf16[320,1536]{1,0:T(8,128)(2,1)S(1)}, u32[]{:S(2)}, u32[]{:S(2)}) collective-permute-start(bf16[320,1536]{1,0:T(8,128)(2,1)} %collective-permute-done.5.refs_3_), channel_id=1, source_target_pairs={{0,1},{1,0},{2,3},{3,2},{4,5},{5,4},{6,7},{7,6},{8,9},{9,8},{10,11... | collective-permute-start | bytes 2949128 | tf_op jit(solution)/shard_map/ppermute | solution.py:1064
  85.5 33.4 %collective-permute-start.10 = (bf16[176,1536]{1,0:T(8,128)(2,1)}, bf16[176,1536]{1,0:T(8,128)(2,1)S(1)}, u32[]{:S(2)}, u32[]{:S(2)}) collective-permute-start(bf16[176,1536]{1,0:T(8,128)(2,1)} %dynamic-slice_bitcast_fusion.3), channel_id=1, source_target_pairs={{0,4},{1,5},{2,6},{3,7},{4,0},{5,1},{6,2},{7,3},{8,12},{9,13},{10,... | collective-permute-start | bytes 1622024 | tf_op jit(solution)/shard_map/ppermute | solution.py:1074
  137.3 31.8 %collective-permute-start.15 = (bf16[176,1536]{1,0:T(8,128)(2,1)S(1)}, bf16[176,1536]{1,0:T(8,128)(2,1)S(1)}, u32[]{:S(2)}, u32[]{:S(2)}) collective-permute-start(bf16[176,1536]{1,0:T(8,128)(2,1)S(1)} %collective-permute-done.10.refs_6_.refs_8_), channel_id=1, source_target_pairs={{0,8},{8,0},{16,24},{24,16},{1,9},{9,1},{17,25},{25,17},{2,10},{10... | collective-permute-start | bytes 1622024 | tf_op jit(solution)/shard_map/ppermute | solution.py:1080
  137.8 31.3 %collective-permute-start.16 = (bf16[176,1536]{1,0:T(8,128)(2,1)S(1)}, bf16[176,1536]{1,0:T(8,128)(2,1)}, u32[]{:S(2)}, u32[]{:S(2)}) collective-permute-start(bf16[176,1536]{1,0:T(8,128)(2,1)S(1)} %collective-permute-done.10.refs_6_.refs_8_), channel_id=1, source_target_pairs={{0,16},{8,24},{16,0},{24,8},{1,17},{9,25},{17,1},{25,9},{2,18},{10... | collective-permute-start | bytes 1622024 | tf_op jit(solution)/shard_map/ppermute | solution.py:1080
  138.7 30.4 %collective-permute-start.17 = (bf16[176,1536]{1,0:T(8,128)(2,1)S(1)}, bf16[176,1536]{1,0:T(8,128)(2,1)}, u32[]{:S(2)}, u32[]{:S(2)}) collective-permute-start(bf16[176,1536]{1,0:T(8,128)(2,1)S(1)} %collective-permute-done.10.refs_6_.refs_8_), channel_id=1, source_target_pairs={{0,24},{8,16},{16,8},{24,0},{1,25},{9,17},{17,9},{25,1},{2,26},{10... | collective-permute-start | bytes 1622024 | tf_op jit(solution)/shard_map/ppermute | solution.py:1080
  140.8 56.0 %collective-permute-start.19 = (bf16[640,1664]{1,0:T(8,128)(2,1)}, bf16[640,1664]{1,0:T(8,128)(2,1)S(1)}, u32[]{:S(2)}, u32[]{:S(2)}) collective-permute-start(bf16[640,1664]{1,0:T(8,128)(2,1)} %get-tuple-element.164.refs_1_.payload), channel_id=1, source_target_pairs={{0,2},{1,3},{2,0},{3,1},{4,6},{5,7},{6,4},{7,5},{8,10},{9,11},{10,... | collective-permute-start | bytes 6389768 | tf_op jit(solution)/shard_map/ppermute | solution.py:1071
  248.4 209.1 %reduce-scatter.5.cloned.1.call-start = ((), (), s32[]{:S(2)}) async-start(), calls=%async_computation.4 | async-start | bytes 8847360 | tf_op jit(solution)/shard_map/reduce_scatter | solution.py:1179
  283.2 48.7 %collective-permute-start.23 = (bf16[640,1664]{1,0:T(8,128)(2,1)}, bf16[640,1664]{1,0:T(8,128)(2,1)}, u32[]{:S(2)}, u32[]{:S(2)}) collective-permute-start(bf16[640,1664]{1,0:T(8,128)(2,1)} %fusion), channel_id=1, source_target_pairs={{0,2},{1,3},{2,0},{3,1},{4,6},{5,7},{6,4},{7,5},{8,10},{9,11},{10,... | collective-permute-start | bytes 6389768 | tf_op jit(solution)/shard_map/ppermute | solution.py:1071
  331.9 215.8 %all-gather.5.cloned.1.call-start = ((), (), s32[]{:S(2)}) async-start(), calls=%async_computation.5 | async-start | bytes 8847360 | tf_op jit(solution)/shard_map/all_gather | solution.py:1251
  396.6 40.0 %collective-permute-start.34 = (bf16[2,384,512]{2,1,0:T(8,128)(2,1)}, bf16[2,384,512]{2,1,0:T(8,128)(2,1)S(1)}, u32[]{:S(2)}, u32[]{:S(2)}) collective-permute-start(bf16[2,384,512]{2,1,0:T(8,128)(2,1)} %get-tuple-element.220), channel_id=1, source_target_pairs={{0,16},{8,24},{16,0},{24,8},{1,17},{9,25},{17,1},{25,9},{2,18},{10... | collective-permute-start | bytes 2359304 | tf_op jit(solution)/shard_map/ppermute | solution.py:1080
  396.8 39.8 %collective-permute-start.35 = (bf16[2,384,512]{2,1,0:T(8,128)(2,1)}, bf16[2,384,512]{2,1,0:T(8,128)(2,1)S(1)}, u32[]{:S(2)}, u32[]{:S(2)}) collective-permute-start(bf16[2,384,512]{2,1,0:T(8,128)(2,1)} %get-tuple-element.222), channel_id=1, source_target_pairs={{0,8},{8,0},{16,24},{24,16},{1,9},{9,1},{17,25},{25,17},{2,10},{10... | collective-permute-start | bytes 2359304 | tf_op jit(solution)/shard_map/ppermute | solution.py:1080
  402.2 34.3 %collective-permute-start.36 = (bf16[2,384,384]{2,1,0:T(8,128)(2,1)}, bf16[2,384,384]{2,1,0:T(8,128)(2,1)}, u32[]{:S(2)}, u32[]{:S(2)}) collective-permute-start(bf16[2,384,384]{2,1,0:T(8,128)(2,1)} %get-tuple-element.226), channel_id=1, source_target_pairs={{0,16},{8,24},{16,0},{24,8},{1,17},{9,25},{17,1},{25,9},{2,18},{10... | collective-permute-start | bytes 1769480 | tf_op jit(solution)/shard_map/ppermute | solution.py:1080
  403.1 33.5 %collective-permute-start.37 = (bf16[2,384,384]{2,1,0:T(8,128)(2,1)}, bf16[2,384,384]{2,1,0:T(8,128)(2,1)}, u32[]{:S(2)}, u32[]{:S(2)}) collective-permute-start(bf16[2,384,384]{2,1,0:T(8,128)(2,1)} %get-tuple-element.228), channel_id=1, source_target_pairs={{0,8},{8,0},{16,24},{24,16},{1,9},{9,1},{17,25},{25,17},{2,10},{10... | collective-permute-start | bytes 1769480 | tf_op jit(solution)/shard_map/ppermute | solution.py:1080
  463.4 64.9 %collective-permute-start.52 = (bf16[640,1536]{1,0:T(8,128)(2,1)}, bf16[640,1536]{1,0:T(8,128)(2,1)}, u32[]{:S(2)}, u32[]{:S(2)}) collective-permute-start(bf16[640,1536]{1,0:T(8,128)(2,1)} %bitcast.78), channel_id=1, source_target_pairs={{0,1},{1,0},{2,3},{3,2},{4,5},{5,4},{6,7},{7,6},{8,9},{9,8},{10,11... | collective-permute-start | bytes 5898248 | tf_op jit(solution)/shard_map/ppermute | solution.py:1064
  464.4 28.8 %collective-permute-start.48 = (bf16[208,1536]{1,0:T(8,128)(2,1)S(1)}, bf16[208,1536]{1,0:T(8,128)(2,1)S(1)}, u32[]{:S(2)}, u32[]{:S(2)}) collective-permute-start(bf16[208,1536]{1,0:T(8,128)(2,1)S(1)} %slice.81), channel_id=1, source_target_pairs={{0,2},{1,3},{2,0},{3,1},{4,6},{5,7},{6,4},{7,5},{8,10},{9,11},{10,... | collective-permute-start | bytes 1916936 | tf_op jit(solution)/shard_map/ppermute | solution.py:1071
  (84 other events, 1038.0 us)
Sparse Core Ops, SparseCore 0:
  84.7 60.1 all-gather.2
  248.5 74.3 reduce-scatter.2
  332.0 78.4 reduce-scatter.4
  461.2 79.5 all-gather.4
